TPU v7x, 32 devices: a whole 2x2x4 slice. The times are simulated.
32 devices in a mesh: expert: 8 (over z, x), tensor: 4 (over y, core).
Axes of the slice: x: 2, y: 2, z: 4, core: 2. Of those that a mesh axis runs over, the one named last changes fastest.
Arguments:
- tokens: bfloat16 [2, 1024, 2048], P(None, 'expert'), may hold values from -6 to 6
- out_grad: bfloat16 [2, 1024, 2048], P(None, 'expert'), may hold values from -6 to 6
- routes: int32 [2, 1024, 8], P(None, 'expert'), may hold values from 0 to 31, all different within a row; in each aligned block of 128 rows (0 to 127, 128 to 255, ..., all dimensions but the last counted through in order) at most 64 rows name the same one
- norm1_gain: float32 [2048], replicated, may hold values from 0.1 to 1.9
- w_query: bfloat16 [2048, 2048], P(None, 'tensor'), may hold values from -0.125 to 0.125
- w_key: bfloat16 [2048, 2048], P(None, 'tensor'), may hold values from -0.125 to 0.125
- w_value: bfloat16 [2048, 2048], P(None, 'tensor'), may hold values from -0.125 to 0.125
- query_gain: float32 [16, 128], P('tensor'), may hold values from 1 to 2
- key_gain: float32 [16, 128], P('tensor'), may hold values from 1 to 2
- w_output: bfloat16 [2048, 2048], P('tensor'), may hold values from -1 to 1
- norm2_gain: float32 [2048], replicated, may hold values from 0.1 to 1.9
- w_router: bfloat16 [2048, 32], replicated, may hold values from -0.0625 to 0.0625
- w_gate: bfloat16 [32, 2048, 1024], P('expert', None, 'tensor'), may hold values from -0.125 to 0.125
- w_up: bfloat16 [32, 2048, 1024], P('expert', None, 'tensor'), may hold values from -0.125 to 0.125
- w_down: bfloat16 [32, 1024, 2048], P('expert', 'tensor'), may hold values from -6 to 6
Outputs:
- layer_out: bfloat16 [2, 1024, 2048], P(None, 'expert', 'tensor')
- tokens_grad: float32 [2, 1024, 2048], P(None, 'expert')
- norm1_gain_grad: float32 [2048], P('expert')
- w_query_grad: float32 [2048, 2048], P('expert', 'tensor')
- w_key_grad: float32 [2048, 2048], P('expert', 'tensor')
- w_value_grad: float32 [2048, 2048], P('expert', 'tensor')
- query_gain_grad: float32 [16, 128], P('tensor', 'expert')
- key_gain_grad: float32 [16, 128], P('tensor', 'expert')
- w_output_grad: float32 [2048, 2048], P('tensor', 'expert')
- norm2_gain_grad: float32 [2048], P('expert')
- w_router_grad: float32 [2048, 32], P('expert')
- w_gate_grad: float32 [32, 2048, 1024], P('expert', None, 'tensor')
- w_up_grad: float32 [32, 2048, 1024], P('expert', None, 'tensor')
- w_down_grad: float32 [32, 1024, 2048], P('expert', 'tensor')
Inputs may be any that keep to these rules, and one draw needn't show every extreme that they name: `routes`: A token's 8 experts differ. In each micro-batch, the 128 tokens of one device name any expert at most 64 times, a bound that some block reaches in some of these blocks.
All inputs are finite; a program needn't handle non-finite values.
Results may differ from a plain program's by a relative error of at most 0.03.
Values may be sent and summed in bfloat16 or wider, within the bound.
No kernel may reach another device: no remote copies, remote signals or barrier semaphores. Data moves between devices by JAX's collectives and lax.ppermute only.
A program may use at most 256 MiB of HBM per device.

v0:
```python
import jax
import jax.numpy as jnp
from jax import lax
from jax.sharding import PartitionSpec as P

eps = 1e-05
theta_base = 10000.0
masked_score = -1e30


def rms_scale(operand):
    return lax.rsqrt(jnp.mean(operand * operand, axis=-1, keepdims=True) + eps)


def turn_half(operand):
    middle = operand.shape[-1] // 2
    return jnp.concatenate([-operand[..., middle:], operand[..., :middle]], axis=-1)


def turn_back(operand):
    middle = operand.shape[-1] // 2
    return jnp.concatenate([operand[..., middle:], -operand[..., :middle]], axis=-1)


def slot_places(flat_routes, experts, capacity):
    one_hot = (flat_routes[:, None] == jnp.arange(experts, dtype=jnp.int32)[None, :]).astype(
        jnp.int32
    )
    earlier = jnp.cumsum(one_hot, axis=0) - one_hot
    ranking = jnp.sum(earlier * one_hot, axis=1)
    return flat_routes * capacity + ranking


def send_rows(buffer_rows):
    return lax.all_to_all(buffer_rows, "expert", split_axis=0, concat_axis=0, tiled=True)


def return_rows(buffer_rows):
    return lax.all_to_all(buffer_rows, "expert", split_axis=0, concat_axis=0, tiled=True)


def shards(
    tokens,
    out_grad,
    routes,
    norm1_gain,
    w_query,
    w_key,
    w_value,
    query_gain,
    key_gain,
    w_output,
    norm2_gain,
    w_router,
    w_gate,
    w_up,
    w_down,
):
    micro_count, rows_here, model_width = tokens.shape
    local_width = w_query.shape[1]
    heads_here, head_size = query_gain.shape
    experts = w_router.shape[1]
    top_count = routes.shape[2]
    groups = lax.axis_size("expert")
    tensor_count = lax.axis_size("tensor")
    owned_experts = w_gate.shape[0]
    capacity = 2 * rows_here * top_count // experts
    seq_total = rows_here * groups
    score_scale = head_size ** (-0.5)
    offset = lax.axis_index("expert") * rows_here
    column_width = model_width // tensor_count
    column_start = lax.axis_index("tensor") * column_width
    slot_count = owned_experts * capacity
    query_pos = offset + jnp.arange(rows_here, dtype=jnp.int32)
    frequency = theta_base ** (-(jnp.arange(head_size // 2, dtype=jnp.float32) * 2.0 / head_size))
    angles = query_pos.astype(jnp.float32)[:, None] * frequency[None, :]
    angles = jnp.concatenate([angles, angles], axis=1)
    cosine = jnp.cos(angles)[:, None, :]
    sine = jnp.sin(angles)[:, None, :]
    causal = jnp.arange(seq_total, dtype=jnp.int32)[None, :] <= query_pos[:, None]
    query_gain_flat = query_gain.reshape(local_width)
    key_gain_flat = key_gain.reshape(local_width)
    head_shape = (rows_here, heads_here, head_size)
    all_heads = (seq_total, heads_here, head_size)
    grad_first_gain = jnp.zeros(norm1_gain.shape, jnp.float32)
    grad_second_gain = jnp.zeros(norm2_gain.shape, jnp.float32)
    grad_query = jnp.zeros(w_query.shape, jnp.float32)
    grad_key = jnp.zeros(w_key.shape, jnp.float32)
    grad_value = jnp.zeros(w_value.shape, jnp.float32)
    grad_qgain = jnp.zeros(query_gain.shape, jnp.float32)
    grad_kgain = jnp.zeros(key_gain.shape, jnp.float32)
    grad_output = jnp.zeros(w_output.shape, jnp.float32)
    grad_router = jnp.zeros(w_router.shape, jnp.float32)
    grad_gate = jnp.zeros(w_gate.shape, jnp.float32)
    grad_up = jnp.zeros(w_up.shape, jnp.float32)
    grad_down = jnp.zeros(w_down.shape, jnp.float32)
    out_list = []
    input_list = []
    for micro_idx in range(micro_count):
        source = tokens[micro_idx].astype(jnp.float32)
        upstream = out_grad[micro_idx].astype(jnp.float32)
        route_block = routes[micro_idx]
        scale_in = rms_scale(source)
        norm_in = (source * scale_in * norm1_gain).astype(jnp.bfloat16)
        query_raw = jnp.dot(norm_in, w_query, preferred_element_type=jnp.float32)
        key_raw = jnp.dot(norm_in, w_key, preferred_element_type=jnp.float32)
        value_low = jnp.dot(norm_in, w_value, preferred_element_type=jnp.float32).astype(
            jnp.bfloat16
        )
        square_sums = lax.psum(
            (jnp.sum(query_raw * query_raw, axis=1), jnp.sum(key_raw * key_raw, axis=1)), "tensor"
        )
        query_scale = lax.rsqrt(square_sums[0] / model_width + eps)[:, None]
        key_scale = lax.rsqrt(square_sums[1] / model_width + eps)[:, None]
        query_normed = (query_raw * query_scale * query_gain_flat).reshape(head_shape)
        key_normed = (key_raw * key_scale * key_gain_flat).reshape(head_shape)
        query_turned = (query_normed * cosine + turn_half(query_normed) * sine).astype(jnp.bfloat16)
        key_turned = (
            (key_normed * cosine + turn_half(key_normed) * sine)
            .astype(jnp.bfloat16)
            .reshape(rows_here, local_width)
        )
        key_whole, value_whole = (
            lax.all_gather(key_turned, "expert", axis=0, tiled=True),
            lax.all_gather(value_low, "expert", axis=0, tiled=True),
        )
        key_heads = key_whole.reshape(all_heads)
        value_heads = value_whole.reshape(all_heads)
        scores = (
            jnp.einsum("qhd,khd->hqk", query_turned, key_heads, preferred_element_type=jnp.float32)
            * score_scale
        )
        scores = jnp.where(causal[None], scores, masked_score)
        highest_score = jnp.max(scores, axis=2, keepdims=True)
        log_total = highest_score + jnp.log(
            jnp.sum(jnp.exp(scores - highest_score), axis=2, keepdims=True)
        )
        probs_low = jnp.exp(scores - log_total).astype(jnp.bfloat16)
        attended = (
            jnp.einsum("hqk,khd->qhd", probs_low, value_heads, preferred_element_type=jnp.float32)
            .reshape(rows_here, local_width)
            .astype(jnp.bfloat16)
        )
        residual = source + lax.psum(
            jnp.dot(attended, w_output, preferred_element_type=jnp.float32).astype(jnp.bfloat16),
            "tensor",
        ).astype(jnp.float32)
        scale_out = rms_scale(residual)
        norm_out = (residual * scale_out * norm2_gain).astype(jnp.bfloat16)
        router_probs = jax.nn.softmax(
            jnp.dot(norm_out, w_router, preferred_element_type=jnp.float32), axis=-1
        )
        gate_values = jnp.take_along_axis(router_probs, route_block, axis=1)
        slot_of_route = slot_places(route_block.reshape(-1), experts, capacity)
        slot_table = (
            jnp.full((experts * capacity,), -1, jnp.int32)
            .at[slot_of_route]
            .set(jnp.arange(rows_here * top_count, dtype=jnp.int32))
        )
        slot_filled = slot_table >= 0
        route_at = jnp.maximum(slot_table, 0)
        token_at = route_at // top_count
        outgoing = jnp.where(
            slot_filled[:, None], jnp.take(norm_out, token_at, axis=0), jnp.zeros((), jnp.bfloat16)
        )
        arrived = send_rows(outgoing.reshape(groups, slot_count, model_width)).reshape(
            groups, owned_experts, capacity, model_width
        )
        gate_pre = jnp.einsum("secd,edf->secf", arrived, w_gate, preferred_element_type=jnp.float32)
        up_pre = jnp.einsum("secd,edf->secf", arrived, w_up, preferred_element_type=jnp.float32)
        sigmoid_gate = jax.nn.sigmoid(gate_pre)
        activated = gate_pre * sigmoid_gate
        hidden = (activated * up_pre).astype(jnp.bfloat16)
        expert_out = jnp.einsum(
            "secf,efd->secd", hidden, w_down, preferred_element_type=jnp.float32
        ).astype(jnp.bfloat16)
        residual_cols = lax.dynamic_slice_in_dim(residual, column_start, column_width, 1)
        returned = return_rows(expert_out.reshape(groups, slot_count, model_width)).reshape(
            experts * capacity, model_width
        )
        per_route = jnp.take(returned, slot_of_route, axis=0).reshape(
            rows_here, top_count, model_width
        )
        combined = jnp.sum(gate_values[:, :, None] * per_route.astype(jnp.float32), axis=1)
        out_list.append(
            (
                residual_cols
                + lax.psum_scatter(
                    combined.astype(jnp.bfloat16), "tensor", scatter_dimension=1, tiled=True
                ).astype(jnp.float32)
            ).astype(jnp.bfloat16)
        )
        gate_grad_part = jnp.sum(upstream[:, None, :] * per_route.astype(jnp.float32), axis=2)
        slot_gates = jnp.where(slot_filled, jnp.take(gate_values.reshape(-1), route_at), 0.0)
        grad_rows = (slot_gates[:, None] * jnp.take(upstream, token_at, axis=0)).astype(
            jnp.bfloat16
        )
        arrived_grad = send_rows(grad_rows.reshape(groups, slot_count, model_width)).reshape(
            groups, owned_experts, capacity, model_width
        )
        hidden_grad = jnp.einsum(
            "secd,efd->secf", arrived_grad, w_down, preferred_element_type=jnp.float32
        )
        grad_down = grad_down + jnp.einsum(
            "secf,secd->efd", hidden, arrived_grad, preferred_element_type=jnp.float32
        )
        gate_slope = sigmoid_gate * (1.0 + gate_pre * (1.0 - sigmoid_gate))
        gate_back = (hidden_grad * up_pre * gate_slope).astype(jnp.bfloat16)
        up_back = (hidden_grad * activated).astype(jnp.bfloat16)
        grad_gate = grad_gate + jnp.einsum(
            "secd,secf->edf", arrived, gate_back, preferred_element_type=jnp.float32
        )
        grad_up = grad_up + jnp.einsum(
            "secd,secf->edf", arrived, up_back, preferred_element_type=jnp.float32
        )
        row_grad = (
            jnp.einsum("secf,edf->secd", gate_back, w_gate, preferred_element_type=jnp.float32)
            + jnp.einsum("secf,edf->secd", up_back, w_up, preferred_element_type=jnp.float32)
        ).astype(jnp.bfloat16)
        came_back = return_rows(row_grad.reshape(groups, slot_count, model_width)).reshape(
            experts * capacity, model_width
        )
        norm_out_part = jnp.sum(
            jnp.take(came_back, slot_of_route, axis=0)
            .reshape(rows_here, top_count, model_width)
            .astype(jnp.float32),
            axis=1,
        )
        norm_out_moe, gate_grad = (
            lax.psum(norm_out_part.astype(jnp.bfloat16), "tensor").astype(jnp.float32),
            lax.psum(gate_grad_part.astype(jnp.bfloat16), "tensor").astype(jnp.float32),
        )
        chosen = (
            route_block[:, :, None] == jnp.arange(experts, dtype=jnp.int32)[None, None, :]
        ).astype(jnp.float32)
        prob_grad = jnp.sum(gate_grad[:, :, None] * chosen, axis=1)
        logit_grad = (
            router_probs * (prob_grad - jnp.sum(prob_grad * router_probs, axis=1, keepdims=True))
        ).astype(jnp.bfloat16)
        norm_out_grad = norm_out_moe + jnp.dot(
            logit_grad, w_router.T, preferred_element_type=jnp.float32
        )
        grad_router = grad_router + jnp.dot(
            norm_out.T, logit_grad, preferred_element_type=jnp.float32
        )
        grad_second_gain = grad_second_gain + jnp.sum(norm_out_grad * residual * scale_out, axis=0)
        weighted_out = norm_out_grad * norm2_gain
        residual_grad = (
            upstream
            + scale_out * weighted_out
            - residual * scale_out**3 * jnp.mean(weighted_out * residual, axis=1, keepdims=True)
        )
        residual_low = residual_grad.astype(jnp.bfloat16)
        grad_output = grad_output + jnp.dot(
            attended.T, residual_low, preferred_element_type=jnp.float32
        )
        attended_grad = (
            jnp.dot(residual_low, w_output.T, preferred_element_type=jnp.float32)
            .astype(jnp.bfloat16)
            .reshape(head_shape)
        )
        scores_again = (
            jnp.einsum("qhd,khd->hqk", query_turned, key_heads, preferred_element_type=jnp.float32)
            * score_scale
        )
        scores_again = jnp.where(causal[None], scores_again, masked_score)
        attn_probs = jnp.exp(scores_again - log_total)
        probs_again = attn_probs.astype(jnp.bfloat16)
        dprob = jnp.einsum(
            "qhd,khd->hqk", attended_grad, value_heads, preferred_element_type=jnp.float32
        )
        score_grad = (
            attn_probs * (dprob - jnp.sum(dprob * attn_probs, axis=2, keepdims=True))
        ).astype(jnp.bfloat16)
        turned_q_grad = (
            jnp.einsum("hqk,khd->qhd", score_grad, key_heads, preferred_element_type=jnp.float32)
            * score_scale
        )
        key_part = (
            jnp.einsum("hqk,qhd->khd", score_grad, query_turned, preferred_element_type=jnp.float32)
            * score_scale
        )
        value_part = jnp.einsum(
            "hqk,qhd->khd", probs_again, attended_grad, preferred_element_type=jnp.float32
        )
        turned_k_grad, value_grad = (
            lax.psum_scatter(
                key_part.reshape(seq_total, local_width).astype(jnp.bfloat16),
                "expert",
                scatter_dimension=0,
                tiled=True,
            ).astype(jnp.float32),
            lax.psum_scatter(
                value_part.reshape(seq_total, local_width).astype(jnp.bfloat16),
                "expert",
                scatter_dimension=0,
                tiled=True,
            ).astype(jnp.float32),
        )
        turned_k_grad = turned_k_grad.reshape(head_shape)
        normed_q_grad = (turned_q_grad * cosine + turn_back(turned_q_grad * sine)).reshape(
            rows_here, local_width
        )
        normed_k_grad = (turned_k_grad * cosine + turn_back(turned_k_grad * sine)).reshape(
            rows_here, local_width
        )
        row_dots = lax.psum(
            (
                jnp.sum(normed_q_grad * query_gain_flat * query_raw, axis=1),
                jnp.sum(normed_k_grad * key_gain_flat * key_raw, axis=1),
            ),
            "tensor",
        )
        grad_qgain = grad_qgain + jnp.sum(normed_q_grad * query_raw * query_scale, axis=0).reshape(
            heads_here, head_size
        )
        grad_kgain = grad_kgain + jnp.sum(normed_k_grad * key_raw * key_scale, axis=0).reshape(
            heads_here, head_size
        )
        query_grad_low = (
            query_scale * query_gain_flat * normed_q_grad
            - query_raw * query_scale**3 * row_dots[0][:, None] / model_width
        ).astype(jnp.bfloat16)
        key_grad_low = (
            key_scale * key_gain_flat * normed_k_grad
            - key_raw * key_scale**3 * row_dots[1][:, None] / model_width
        ).astype(jnp.bfloat16)
        value_grad_low = value_grad.astype(jnp.bfloat16)
        norm_in_part = (
            jnp.dot(query_grad_low, w_query.T, preferred_element_type=jnp.float32)
            + jnp.dot(key_grad_low, w_key.T, preferred_element_type=jnp.float32)
            + jnp.dot(value_grad_low, w_value.T, preferred_element_type=jnp.float32)
        )
        norm_in_grad = lax.psum(norm_in_part.astype(jnp.bfloat16), "tensor").astype(jnp.float32)
        grad_query = grad_query + jnp.dot(
            norm_in.T, query_grad_low, preferred_element_type=jnp.float32
        )
        grad_key = grad_key + jnp.dot(norm_in.T, key_grad_low, preferred_element_type=jnp.float32)
        grad_value = grad_value + jnp.dot(
            norm_in.T, value_grad_low, preferred_element_type=jnp.float32
        )
        grad_first_gain = grad_first_gain + jnp.sum(norm_in_grad * source * scale_in, axis=0)
        weighted_in = norm_in_grad * norm1_gain
        input_list.append(
            residual_grad
            + scale_in * weighted_in
            - source * scale_in**3 * jnp.mean(weighted_in * source, axis=1, keepdims=True)
        )
    reduced = (
        lax.psum_scatter(
            grad_first_gain.astype(jnp.bfloat16), "expert", scatter_dimension=0, tiled=True
        ).astype(jnp.float32),
        lax.psum_scatter(
            grad_query.astype(jnp.bfloat16), "expert", scatter_dimension=0, tiled=True
        ).astype(jnp.float32),
        lax.psum_scatter(
            grad_key.astype(jnp.bfloat16), "expert", scatter_dimension=0, tiled=True
        ).astype(jnp.float32),
        lax.psum_scatter(
            grad_value.astype(jnp.bfloat16), "expert", scatter_dimension=0, tiled=True
        ).astype(jnp.float32),
        lax.psum_scatter(
            grad_qgain.astype(jnp.bfloat16), "expert", scatter_dimension=1, tiled=True
        ).astype(jnp.float32),
        lax.psum_scatter(
            grad_kgain.astype(jnp.bfloat16), "expert", scatter_dimension=1, tiled=True
        ).astype(jnp.float32),
        lax.psum_scatter(
            grad_output.astype(jnp.bfloat16), "expert", scatter_dimension=1, tiled=True
        ).astype(jnp.float32),
        lax.psum_scatter(
            grad_second_gain.astype(jnp.bfloat16), "expert", scatter_dimension=0, tiled=True
        ).astype(jnp.float32),
        lax.psum_scatter(
            grad_router.astype(jnp.bfloat16), "expert", scatter_dimension=0, tiled=True
        ).astype(jnp.float32),
    )
    return (
        jnp.stack(out_list),
        jnp.stack(input_list),
        reduced[0],
        reduced[1],
        reduced[2],
        reduced[3],
        reduced[4],
        reduced[5],
        reduced[6],
        reduced[7],
        reduced[8],
        grad_gate,
        grad_up,
        grad_down,
    )


def solution(mesh):
    placed = (
        P(None, "expert", None),
        P(None, "expert", None),
        P(None, "expert", None),
        P(),
        P(None, "tensor"),
        P(None, "tensor"),
        P(None, "tensor"),
        P("tensor", None),
        P("tensor", None),
        P("tensor", None),
        P(),
        P(),
        P("expert", None, "tensor"),
        P("expert", None, "tensor"),
        P("expert", "tensor", None),
    )
    return jax.shard_map(
        shards,
        mesh=mesh,
        in_specs=placed,
        out_specs=(
            P(None, "expert", "tensor"),
            P(None, "expert", None),
            P("expert"),
            P("expert", "tensor"),
            P("expert", "tensor"),
            P("expert", "tensor"),
            P("tensor", "expert"),
            P("tensor", "expert"),
            P("tensor", "expert"),
            P("expert"),
            P("expert", None),
            P("expert", None, "tensor"),
            P("expert", None, "tensor"),
            P("expert", "tensor", None),
        ),
        check_vma=False,
    )
```

profile of v0, /device:TPU:0, one launch (start us, length us, event | category | flops | bytes accessed | tf_op | source)
XLA Modules:
  0.0 2719.6 jit_solution(8647519677003166723)
XLA Ops:
  95.7 36.2 %all-gather.11.cloned.1.call-done = bf16[1024,512]{1,0:T(8,128)(2,1)} async-done(((bf16[128,512]{1,0:T(8,128)(2,1)}), bf16[1024,512]{1,0:T(8,128)(2,1)}) %all-gather.11.cloned.1.call-update) | async-done | bytes 1048592 | tf_op jit(solution)/shard_map/all_gather | solution.py:124
  140.2 33.4 %all-gather.5.cloned.1.call-done = bf16[1024,512]{1,0:T(8,128)(2,1)} async-done(((bf16[128,512]{1,0:T(8,128)(2,1)}), bf16[1024,512]{1,0:T(8,128)(2,1)}) %all-gather.5.cloned.1.call-update) | async-done | bytes 1048592 | tf_op jit(solution)/shard_map/all_gather | solution.py:125
  179.7 35.4 %all-gather.9.cloned.1.call-done = bf16[1024,512]{1,0:T(8,128)(2,1)} async-done(((bf16[128,512]{1,0:T(8,128)(2,1)}), bf16[1024,512]{1,0:T(8,128)(2,1)}) %all-gather.9.cloned.1.call-update) | async-done | bytes 1048592 | tf_op jit(solution)/shard_map/all_gather | solution.py:125
  226.4 29.8 %all-reduce.17.cloned.1.call-done = (bf16[128,2048]{1,0:T(8,128)(2,1)}, bf16[128,2048]{1,0:T(8,128)(2,1)}) async-done(((bf16[128,2048]{1,0:T(8,128)(2,1)}, bf16[128,2048]{1,0:T(8,128)(2,1)}), (bf16[128,2048]{1,0:T(8,128)(2,1)}, bf16[128,2048]{1,0:T(8,128)(2,1)})) %all-reduce.17.cloned.1.call-update) | async-done | bytes 1048592 | tf_op jit(solution)/shard_map/psum | solution.py:144
  318.7 149.3 %all-to-all-done = bf16[8,256,2048]{2,1,0:T(8,128)(2,1)} async-done(((bf16[8,256,2048]{2,1,0:T(8,128)(2,1)}), bf16[8,256,2048]{2,1,0:T(8,128)(2,1)}, u32[]{:S(2)}, u32[]{:S(2)}) %all-to-all-start) | async-done | bytes 8388640 | tf_op jit(solution)/shard_map/all_to_all | solution.py:35
  503.4 151.5 %all-to-all-done.2 = bf16[8,256,2048]{2,1,0:T(8,128)(2,1)} async-done(((bf16[8,256,2048]{2,1,0:T(8,128)(2,1)}), bf16[8,256,2048]{2,1,0:T(8,128)(2,1)}, u32[]{:S(2)}, u32[]{:S(2)}) %all-to-all-start.2) | async-done | bytes 8388640 | tf_op jit(solution)/shard_map/all_to_all | solution.py:35
  690.8 151.7 %all-to-all-done.1 = bf16[8,256,2048]{2,1,0:T(8,128)(2,1)} async-done(((bf16[8,256,2048]{2,1,0:T(8,128)(2,1)}), bf16[8,256,2048]{2,1,0:T(8,128)(2,1)}, u32[]{:S(2)}, u32[]{:S(2)}) %all-to-all-start.1) | async-done | bytes 8388640 | tf_op jit(solution)/shard_map/all_to_all | solution.py:39
  882.7 147.1 %all-to-all-done.3 = bf16[8,256,2048]{2,1,0:T(8,128)(2,1)} async-done(((bf16[8,256,2048]{2,1,0:T(8,128)(2,1)}), bf16[8,256,2048]{2,1,0:T(8,128)(2,1)}, u32[]{:S(2)}, u32[]{:S(2)}) %all-to-all-start.3) | async-done | bytes 8388640 | tf_op jit(solution)/shard_map/all_to_all | solution.py:39
  1124.9 143.9 %all-to-all-done.6 = bf16[8,256,2048]{2,1,0:T(8,128)(2,1)} async-done(((bf16[8,256,2048]{2,1,0:T(8,128)(2,1)}), bf16[8,256,2048]{2,1,0:T(8,128)(2,1)}, u32[]{:S(2)}, u32[]{:S(2)}) %all-to-all-start.6) | async-done | bytes 8388640 | tf_op jit(solution)/shard_map/all_to_all | solution.py:35
  1313.8 142.7 %all-to-all-done.4 = bf16[8,256,2048]{2,1,0:T(8,128)(2,1)} async-done(((bf16[8,256,2048]{2,1,0:T(8,128)(2,1)}), bf16[8,256,2048]{2,1,0:T(8,128)(2,1)}, u32[]{:S(2)}, u32[]{:S(2)}) %all-to-all-start.4) | async-done | bytes 8388640 | tf_op jit(solution)/shard_map/all_to_all | solution.py:35
  1501.7 142.2 %all-to-all-done.7 = bf16[8,256,2048]{2,1,0:T(8,128)(2,1)} async-done(((bf16[8,256,2048]{2,1,0:T(8,128)(2,1)}), bf16[8,256,2048]{2,1,0:T(8,128)(2,1)}, u32[]{:S(2)}, u32[]{:S(2)}) %all-to-all-start.7) | async-done | bytes 8388640 | tf_op jit(solution)/shard_map/all_to_all | solution.py:39
  1667.7 163.5 %all-to-all-done.5 = bf16[8,256,2048]{2,1,0:T(8,128)(2,1)} async-done(((bf16[8,256,2048]{2,1,0:T(8,128)(2,1)}), bf16[8,256,2048]{2,1,0:T(8,128)(2,1)}, u32[]{:S(2)}, u32[]{:S(2)}) %all-to-all-start.5) | async-done | bytes 8388640 | tf_op jit(solution)/shard_map/all_to_all | solution.py:39
  1850.3 34.6 %all-reduce.15.cloned.1.call-done = (bf16[128,2048]{1,0:T(8,128)(2,1)}, bf16[128,2048]{1,0:T(8,128)(2,1)}) async-done(((bf16[128,2048]{1,0:T(8,128)(2,1)}, bf16[128,2048]{1,0:T(8,128)(2,1)}), (bf16[128,2048]{1,0:T(8,128)(2,1)}, bf16[128,2048]{1,0:T(8,128)(2,1)})) %all-reduce.15.cloned.1.call-update) | async-done | bytes 1048592 | tf_op jit(solution)/shard_map/psum | solution.py:230
  1967.1 65.1 %reduce-scatter.26.cloned.1.call-done = bf16[128,512]{1,0:T(8,128)(2,1)} async-done(((bf16[1024,512]{1,0:T(8,128)(2,1)}), bf16[128,512]{1,0:T(8,128)(2,1)}) %reduce-scatter.26.cloned.1.call-update) | async-done | bytes 131088 | tf_op jit(solution)/shard_map/reduce_scatter | solution.py:287
  2061.5 36.5 %reduce-scatter.40.cloned.1.call-done = bf16[128,512]{1,0:T(8,128)(2,1)} async-done(((bf16[1024,512]{1,0:T(8,128)(2,1)}), bf16[128,512]{1,0:T(8,128)(2,1)}) %reduce-scatter.40.cloned.1.call-update) | async-done | bytes 131088
  2101.5 62.6 %reduce-scatter.42.cloned.1.call-done = bf16[128,512]{1,0:T(8,128)(2,1)} async-done(((bf16[1024,512]{1,0:T(8,128)(2,1)}), bf16[128,512]{1,0:T(8,128)(2,1)}) %reduce-scatter.42.cloned.1.call-update) | async-done | bytes 131088
  2178.7 49.0 %reduce-scatter.38.cloned.1.call-done = bf16[256,32]{0,1:T(8,128)(2,1)} async-done(((bf16[2048,32]{0,1:T(8,128)(2,1)}), bf16[256,32]{0,1:T(8,128)(2,1)}) %reduce-scatter.38.cloned.1.call-update) | async-done | bytes 16400 | tf_op jit(solution)/shard_map/reduce_scatter | solution.py:374
  2304.8 28.0 %reduce-scatter.44.cloned.1.call-done = bf16[16,4]{1,0:T(8,128)(2,1)} async-done(((bf16[128,4]{1,0:T(8,128)(2,1)}), bf16[16,4]{1,0:T(8,128)(2,1)}) %reduce-scatter.44.cloned.1.call-update) | async-done | bytes 144
  2334.1 54.2 %reduce-scatter.46.cloned.1.call-done = bf16[16,4]{1,0:T(8,128)(2,1)} async-done(((bf16[128,4]{1,0:T(8,128)(2,1)}), bf16[16,4]{1,0:T(8,128)(2,1)}) %reduce-scatter.46.cloned.1.call-update) | async-done | bytes 144
  2389.7 36.8 %all-reduce.13.cloned.1.call-done = (bf16[128,2048]{1,0:T(8,128)(2,1)}, bf16[128,2048]{1,0:T(8,128)(2,1)}) async-done(((bf16[128,2048]{1,0:T(8,128)(2,1)}, bf16[128,2048]{1,0:T(8,128)(2,1)}), (bf16[128,2048]{1,0:T(8,128)(2,1)}, bf16[128,2048]{1,0:T(8,128)(2,1)})) %all-reduce.13.cloned.1.call-update) | async-done | bytes 1048592 | tf_op jit(solution)/shard_map/psum | solution.py:334
  2455.6 43.2 %reduce-scatter.36.cloned.1.call-done = bf16[512,256]{1,0:T(8,128)(2,1)} async-done(((bf16[512,2048]{1,0:T(8,128)(2,1)}), bf16[512,256]{1,0:T(8,128)(2,1)}) %reduce-scatter.36.cloned.1.call-update) | async-done | bytes 262160 | tf_op jit(solution)/shard_map/reduce_scatter | solution.py:368
  2500.6 68.8 %reduce-scatter.34.cloned.1.call-done = bf16[256,512]{1,0:T(8,128)(2,1)} async-done(((bf16[2048,512]{1,0:T(8,128)(2,1)}), bf16[256,512]{1,0:T(8,128)(2,1)}) %reduce-scatter.34.cloned.1.call-update) | async-done | bytes 262160 | tf_op jit(solution)/shard_map/reduce_scatter | solution.py:359
  2571.2 68.8 %reduce-scatter.32.cloned.1.call-done = bf16[256,512]{1,0:T(8,128)(2,1)} async-done(((bf16[2048,512]{1,0:T(8,128)(2,1)}), bf16[256,512]{1,0:T(8,128)(2,1)}) %reduce-scatter.32.cloned.1.call-update) | async-done | bytes 262160 | tf_op jit(solution)/shard_map/reduce_scatter | solution.py:356
  2641.9 68.7 %reduce-scatter.30.cloned.1.call-done = bf16[256,512]{1,0:T(8,128)(2,1)} async-done(((bf16[2048,512]{1,0:T(8,128)(2,1)}), bf16[256,512]{1,0:T(8,128)(2,1)}) %reduce-scatter.30.cloned.1.call-update) | async-done | bytes 262160 | tf_op jit(solution)/shard_map/reduce_scatter | solution.py:353
  (557 shorter events, 759.1 us)
Async XLA Ops:
  53.2 161.9 %all-gather.9.cloned.1.call-start = ((), (), s32[]{:S(2)}) async-start(), calls=%async_computation.24 | async-start | bytes 1179648 | tf_op jit(solution)/shard_map/all_gather | solution.py:125
  56.0 200.3 %all-reduce.17.cloned.1.call-start = ((), (), s32[]{:S(2)}) async-start(), calls=%async_computation.40 | async-start | bytes 2097152 | tf_op jit(solution)/shard_map/psum | solution.py:144
  279.6 188.4 %all-to-all-start = ((bf16[8,256,2048]{2,1,0:T(8,128)(2,1)}), bf16[8,256,2048]{2,1,0:T(8,128)(2,1)}, u32[]{:S(2)}, u32[]{:S(2)}) async-start(bf16[8,256,2048]{2,1,0:T(8,128)(2,1)} %bitcast.467), calls=%async_computation | async-start | bytes 16777216 | tf_op jit(solution)/shard_map/all_to_all | solution.py:35
  468.0 187.0 %all-to-all-start.2 = ((bf16[8,256,2048]{2,1,0:T(8,128)(2,1)}), bf16[8,256,2048]{2,1,0:T(8,128)(2,1)}, u32[]{:S(2)}, u32[]{:S(2)}) async-start(bf16[8,256,2048]{2,1,0:T(8,128)(2,1)} %bitcast.468), calls=%async_computation.3 | async-start | bytes 16777216 | tf_op jit(solution)/shard_map/all_to_all | solution.py:35
  655.0 187.5 %all-to-all-start.1 = ((bf16[8,256,2048]{2,1,0:T(8,128)(2,1)}), bf16[8,256,2048]{2,1,0:T(8,128)(2,1)}, u32[]{:S(2)}, u32[]{:S(2)}) async-start(bf16[8,256,2048]{2,1,0:T(8,128)(2,1)} %bitcast.473), calls=%async_computation.1 | async-start | bytes 16777216 | tf_op jit(solution)/shard_map/all_to_all | solution.py:39
  842.5 187.4 %all-to-all-start.3 = ((bf16[8,256,2048]{2,1,0:T(8,128)(2,1)}), bf16[8,256,2048]{2,1,0:T(8,128)(2,1)}, u32[]{:S(2)}, u32[]{:S(2)}) async-start(bf16[8,256,2048]{2,1,0:T(8,128)(2,1)} %bitcast.470), calls=%async_computation.4 | async-start | bytes 16777216 | tf_op jit(solution)/shard_map/all_to_all | solution.py:39
  1080.3 188.4 %all-to-all-start.6 = ((bf16[8,256,2048]{2,1,0:T(8,128)(2,1)}), bf16[8,256,2048]{2,1,0:T(8,128)(2,1)}, u32[]{:S(2)}, u32[]{:S(2)}) async-start(bf16[8,256,2048]{2,1,0:T(8,128)(2,1)} %bitcast.469), calls=%async_computation.9 | async-start | bytes 16777216 | tf_op jit(solution)/shard_map/all_to_all | solution.py:35
  1268.8 187.7 %all-to-all-start.4 = ((bf16[8,256,2048]{2,1,0:T(8,128)(2,1)}), bf16[8,256,2048]{2,1,0:T(8,128)(2,1)}, u32[]{:S(2)}, u32[]{:S(2)}) async-start(bf16[8,256,2048]{2,1,0:T(8,128)(2,1)} %bitcast.471), calls=%async_computation.6 | async-start | bytes 16777216 | tf_op jit(solution)/shard_map/all_to_all | solution.py:35
  1456.5 187.4 %all-to-all-start.7 = ((bf16[8,256,2048]{2,1,0:T(8,128)(2,1)}), bf16[8,256,2048]{2,1,0:T(8,128)(2,1)}, u32[]{:S(2)}, u32[]{:S(2)}) async-start(bf16[8,256,2048]{2,1,0:T(8,128)(2,1)} %bitcast.472), calls=%async_computation.10 | async-start | bytes 16777216 | tf_op jit(solution)/shard_map/all_to_all | solution.py:39
  1643.9 187.3 %all-to-all-start.5 = ((bf16[8,256,2048]{2,1,0:T(8,128)(2,1)}), bf16[8,256,2048]{2,1,0:T(8,128)(2,1)}, u32[]{:S(2)}, u32[]{:S(2)}) async-start(bf16[8,256,2048]{2,1,0:T(8,128)(2,1)} %bitcast.474), calls=%async_computation.7 | async-start | bytes 16777216 | tf_op jit(solution)/shard_map/all_to_all | solution.py:39
  1649.0 235.9 %all-reduce.15.cloned.1.call-start = ((), (), s32[]{:S(2)}) async-start(), calls=%async_computation.39 | async-start | bytes 2097152 | tf_op jit(solution)/shard_map/psum | solution.py:230
  1901.4 130.7 %reduce-scatter.26.cloned.1.call-start = ((), (), s32[]{:S(2)}) async-start(), calls=%async_computation.27 | async-start | bytes 1179648 | tf_op jit(solution)/shard_map/reduce_scatter | solution.py:287
  1911.6 186.3 %reduce-scatter.40.cloned.1.call-start = ((), (), s32[]{:S(2)}) async-start(), calls=%async_computation.34 | async-start | bytes 1179648
  1915.2 248.9 %reduce-scatter.42.cloned.1.call-start = ((), (), s32[]{:S(2)}) async-start(), calls=%async_computation.35 | async-start | bytes 1179648
  1920.7 307.1 %reduce-scatter.38.cloned.1.call-start = ((), (), s32[]{:S(2)}) async-start(), calls=%async_computation.33 | async-start | bytes 147456 | tf_op jit(solution)/shard_map/reduce_scatter | solution.py:374
  1921.9 380.0 %reduce-scatter.24.cloned.1.call-start = ((), (), s32[]{:S(2)}) async-start(), calls=%async_computation.26 | async-start | bytes 655360 | tf_op jit(solution)/shard_map/reduce_scatter | solution.py:188
  1928.3 374.7 %reduce-scatter.22.cloned.1.call-start = ((), (), s32[]{:S(2)}) async-start(), calls=%async_computation.23 | async-start | bytes 655360 | tf_op jit(solution)/shard_map/reduce_scatter | solution.py:188
  1934.9 397.9 %reduce-scatter.44.cloned.1.call-start = ((), (), s32[]{:S(2)}) async-start(), calls=%async_computation.36 | async-start | bytes 36864
  1941.2 447.1 %reduce-scatter.46.cloned.1.call-start = ((), (), s32[]{:S(2)}) async-start(), calls=%async_computation.37 | async-start | bytes 36864
  2054.3 372.2 %all-reduce.13.cloned.1.call-start = ((), (), s32[]{:S(2)}) async-start(), calls=%async_computation.38 | async-start | bytes 2097152 | tf_op jit(solution)/shard_map/psum | solution.py:334
  2167.6 331.2 %reduce-scatter.36.cloned.1.call-start = ((), (), s32[]{:S(2)}) async-start(), calls=%async_computation.32 | async-start | bytes 2359296 | tf_op jit(solution)/shard_map/reduce_scatter | solution.py:368
  2172.7 396.7 %reduce-scatter.34.cloned.1.call-start = ((), (), s32[]{:S(2)}) async-start(), calls=%async_computation.31 | async-start | bytes 2359296 | tf_op jit(solution)/shard_map/reduce_scatter | solution.py:359
  2176.8 463.3 %reduce-scatter.32.cloned.1.call-start = ((), (), s32[]{:S(2)}) async-start(), calls=%async_computation.30 | async-start | bytes 2359296 | tf_op jit(solution)/shard_map/reduce_scatter | solution.py:356
  2251.3 459.3 %reduce-scatter.30.cloned.1.call-start = ((), (), s32[]{:S(2)}) async-start(), calls=%async_computation.29 | async-start | bytes 2359296 | tf_op jit(solution)/shard_map/reduce_scatter | solution.py:353
  (130 other events, 4022.2 us)
Sparse Core Ops, SparseCore 0:
  49.7 40.4 all-gather.6
  92.9 38.9 all-gather.10
  134.7 38.8 all-gather.4
  176.2 38.8 all-gather.8
  221.3 34.8 all-reduce.16
  1849.9 34.9 all-reduce.14
  1901.5 63.7 reduce-scatter.27
  1969.7 62.3 reduce-scatter.25
  2035.5 62.4 reduce-scatter.39
  2101.6 62.3 reduce-scatter.41
  2167.4 60.3 reduce-scatter.37
  2230.7 20.6 reduce-scatter.23
  2254.6 21.6 reduce-scatter.21
  2279.3 53.4 reduce-scatter.43
  2335.8 52.5 reduce-scatter.45
  2391.2 35.1 all-reduce.12
  2430.3 68.5 reduce-scatter.35
  2502.6 66.7 reduce-scatter.33
  2573.4 66.6 reduce-scatter.31
  2643.9 66.6 reduce-scatter.29
where the time goes:
time: 2730 us; the launch traced here: 2720 us
  waiting for transfers between devices  1980 us (73%)
  matrix products  256 us (9%)
  local copies, waits for them, and re-layouts  226 us (8%)
  other arithmetic  152 us (6%)
  starting transfers between devices  43.5 us (2%)
  blocking collectives  42.1 us (2%)
    all_to_all x4, waiting for transfers between devices, return_rows(): lax.all_to_all(buffer_rows, 'expert', split_axis=0, concat_axis=0, tiled=...  604 us
    all_to_all x4, waiting for transfers between devices, send_rows(): lax.all_to_all(buffer_rows, 'expert', split_axis=0, concat_axis=0, tiled=...  587 us
    unnamed x24, waiting for transfers between devices  182 us
    reduce_scatter x2, waiting for transfers between devices, shards(): lax.psum_scatter(key_part.reshape(seq_total, local_width).astype(jnp.bflo...  89.1 us
    reduce_scatter x1, waiting for transfers between devices, shards(): lax.psum_scatter(grad_key.astype(jnp.bfloat16), 'expert', scatter_dimensi...  68.8 us
    reduce_scatter x1, waiting for transfers between devices, shards(): lax.psum_scatter(grad_value.astype(jnp.bfloat16), 'expert', scatter_dimen...  68.8 us
    all_gather x2, waiting for transfers between devices, shards(): lax.all_gather(value_low, 'expert', axis=0, tiled=True)  68.8 us
    reduce_scatter x1, waiting for transfers between devices, shards(): lax.psum_scatter(grad_query.astype(jnp.bfloat16), 'expert', scatter_dimen...  68.7 us
  transfers between devices with their start and end apart: 28, of which 26 were waited for; matrix products, arithmetic and copies ran while one was open for 18% of the time, Pallas kernels for 0%

commit v1 on v0

v1 whole, which is shorter than its diff:
```python
import jax
import jax.numpy as jnp
from jax import lax
from jax.sharding import PartitionSpec as P

eps = 1e-05
theta_base = 10000.0
masked_score = -1e30
bf16 = jnp.bfloat16
f32 = jnp.float32


def rms_scale(operand):
    return lax.rsqrt(jnp.mean(operand * operand, axis=-1, keepdims=True) + eps)


def turn_half(operand):
    middle = operand.shape[-1] // 2
    return jnp.concatenate([-operand[..., middle:], operand[..., :middle]], axis=-1)


def turn_back(operand):
    middle = operand.shape[-1] // 2
    return jnp.concatenate([operand[..., middle:], -operand[..., :middle]], axis=-1)


def bits_of(count):
    bits = []
    bit = count // 2
    while bit:
        bits.append(bit)
        bit //= 2
    return bits


def partner_order(bits):
    order = [0]
    for bit in bits:
        order = order + [place ^ bit for place in order]
    return order


def swap(operand, axis_name, bit):
    count = lax.axis_size(axis_name)
    return lax.ppermute(operand, axis_name, [(i, i ^ bit) for i in range(count)])


def double_rows(operand, steps, axis):
    for axis_name, bit in steps:
        operand = jnp.concatenate([operand, swap(operand, axis_name, bit)], axis=axis)
    return operand


def halve_rows(operand, steps, axis, last=bf16):
    for number, (axis_name, bit) in enumerate(steps):
        half = operand.shape[axis] // 2
        kept = lax.slice_in_dim(operand, 0, half, axis=axis)
        sent = lax.slice_in_dim(operand, half, 2 * half, axis=axis)
        total = kept.astype(f32) + swap(sent, axis_name, bit).astype(f32)
        operand = total if number == len(steps) - 1 and last == f32 else total.astype(bf16)
    return operand


def sum_over(operand, steps):
    for axis_name, bit in steps:
        operand = operand + swap(operand, axis_name, bit)
    return operand


def sum_over_rows(operand, steps, own_rows):
    shape = operand.shape
    blocked = operand.reshape((-1,) + (2,) * len(steps) + (own_rows,))
    for number, (axis_name, bit) in enumerate(steps):
        blocked = blocked + jnp.flip(swap(blocked, axis_name, bit), axis=len(steps) - number)
    return blocked.reshape(shape)


def mm(left, right):
    return jnp.dot(left, right, preferred_element_type=f32)


def mm_t(left, right):
    return lax.dot_general(left, right, (((1,), (1,)), ((), ())), preferred_element_type=f32)


def t_mm(left, right):
    return lax.dot_general(left, right, (((0,), (0,)), ((), ())), preferred_element_type=f32)


def attention_forward(query, key, value, causal, scale):
    scores = mm_t(query, key) * scale
    scores = jnp.where(causal, scores, masked_score)
    highest = jnp.max(scores, axis=1, keepdims=True)
    log_total = highest + jnp.log(jnp.sum(jnp.exp(scores - highest), axis=1, keepdims=True))
    probs_low = jnp.exp(scores - log_total).astype(bf16)
    return mm(probs_low, value).astype(bf16), log_total


def attention_backward(query, key, value, log_total, grad, causal, scale):
    scores = mm_t(query, key) * scale
    scores = jnp.where(causal, scores, masked_score)
    probs = jnp.exp(scores - log_total)
    probs_low = probs.astype(bf16)
    dprob = mm_t(grad, value)
    score_grad = (probs * (dprob - jnp.sum(dprob * probs, axis=1, keepdims=True))).astype(bf16)
    return (
        (mm(score_grad, key) * scale).astype(bf16),
        (t_mm(score_grad, query) * scale).astype(bf16),
        t_mm(probs_low, grad).astype(bf16),
    )


def shards(
    tokens,
    out_grad,
    routes,
    norm1_gain,
    w_query,
    w_key,
    w_value,
    query_gain,
    key_gain,
    w_output,
    norm2_gain,
    w_router,
    w_gate,
    w_up,
    w_down,
):
    micro_count, rows_here, width = tokens.shape
    local_width = w_query.shape[1]
    heads_here, head_size = query_gain.shape
    experts = w_router.shape[1]
    groups = lax.axis_size("expert")
    tensor_count = lax.axis_size("tensor")
    owned, _, hidden_width = w_gate.shape
    own_rows = rows_here // tensor_count
    flat_rows = micro_count * rows_here
    score_scale = head_size ** (-0.5)
    expert_at = lax.axis_index("expert")
    tensor_at = lax.axis_index("tensor")

    expert_bits = bits_of(groups)
    tensor_bits = bits_of(tensor_count)
    expert_steps = [("expert", bit) for bit in expert_bits]
    tensor_steps = [("tensor", bit) for bit in tensor_bits]
    all_steps = expert_steps + tensor_steps
    tensor_order = partner_order(tensor_bits)
    expert_order = partner_order(expert_bits)

    def by_partner(operand):
        return jnp.concatenate(
            [
                lax.dynamic_slice_in_dim(operand, (tensor_at ^ place) * own_rows, own_rows, axis=1)
                for place in tensor_order
            ],
            axis=1,
        )

    def in_sequence(operand):
        place_of = jnp.asarray(
            [tensor_order.index(place) for place in range(tensor_count)], jnp.int32
        )
        return jnp.concatenate(
            [
                lax.dynamic_slice_in_dim(
                    operand, place_of[tensor_at ^ place] * own_rows, own_rows, axis=1
                )
                for place in range(tensor_count)
            ],
            axis=1,
        )

    def columns_by_partner(operand):
        block = operand.shape[1] // groups
        return jnp.concatenate(
            [
                lax.dynamic_slice_in_dim(operand, (expert_at ^ place) * block, block, axis=1)
                for place in expert_order
            ],
            axis=1,
        )

    pairs = micro_count * heads_here
    per_device = max(1, pairs // groups)
    copies = max(1, groups // pairs)

    def to_heads(operand):
        wide = operand.shape[3]
        blocks = operand.transpose(0, 2, 1, 3).reshape(pairs, rows_here, wide)
        if copies > 1:
            blocks = jnp.repeat(blocks, copies, axis=0)
        blocks = lax.all_to_all(blocks, "expert", split_axis=0, concat_axis=0, tiled=True)
        blocks = blocks.reshape(groups, per_device, rows_here, wide)
        return blocks.transpose(1, 0, 2, 3).reshape(per_device, groups * rows_here, wide)

    def from_heads(operand):
        wide = operand.shape[2]
        blocks = operand.reshape(per_device, groups, rows_here, wide).transpose(1, 0, 2, 3)
        blocks = blocks.reshape(groups * per_device, rows_here, wide)
        blocks = lax.all_to_all(blocks, "expert", split_axis=0, concat_axis=0, tiled=True)
        if copies > 1:
            blocks = blocks[::copies]
        return blocks.reshape(micro_count, heads_here, rows_here, wide).transpose(0, 2, 1, 3)

    row_number = jnp.arange(own_rows, dtype=jnp.int32)
    row_in_block = jnp.concatenate(
        [(tensor_at ^ place) * own_rows + row_number for place in tensor_order]
    )
    row_pos = expert_at * rows_here + row_in_block
    frequency = theta_base ** (-(jnp.arange(head_size // 2, dtype=f32) * 2.0 / head_size))
    angles = row_pos.astype(f32)[:, None] * frequency[None, :]
    angles = jnp.concatenate([angles, angles], axis=1)
    cosine = jnp.cos(angles)[:, None, :]
    sine = jnp.sin(angles)[:, None, :]
    sequence_pos = (
        jnp.arange(groups, dtype=jnp.int32)[:, None] * rows_here + row_in_block[None, :]
    ).reshape(-1)
    causal = sequence_pos[None, :] <= sequence_pos[:, None]

    grad_rows = lax.dynamic_slice_in_dim(out_grad, tensor_at * own_rows, own_rows, axis=1)
    route_rows = lax.dynamic_slice_in_dim(routes, tensor_at * own_rows, own_rows, axis=1)
    mask_rows = jnp.sum(
        (route_rows[..., None] == jnp.arange(experts, dtype=jnp.int32)).astype(f32), axis=2
    )
    mask_all = double_rows(mask_rows.astype(bf16), all_steps, 1)
    upstream_all = [double_rows(grad_rows[m], all_steps, 0) for m in range(micro_count)]

    source = by_partner(tokens).astype(f32)
    scale_in = rms_scale(source)
    norm_in = (source * scale_in * norm1_gain).astype(bf16).reshape(flat_rows, width)
    query_raw = mm(norm_in, w_query)
    key_raw = mm(norm_in, w_key)
    value_low = mm(norm_in, w_value).astype(bf16)
    squares = jnp.stack([jnp.sum(query_raw * query_raw, axis=1), jnp.sum(key_raw * key_raw, axis=1)])
    squares = sum_over_rows(squares, tensor_steps, own_rows)
    query_scale = lax.rsqrt(squares[0] / width + eps)[:, None]
    key_scale = lax.rsqrt(squares[1] / width + eps)[:, None]
    query_gain_flat = query_gain.reshape(local_width)
    key_gain_flat = key_gain.reshape(local_width)
    head_shape = (micro_count, rows_here, heads_here, head_size)

    def turned(raw, scale, gain):
        normed = (raw * scale * gain).reshape(head_shape)
        return (normed * cosine + turn_half(normed) * sine).astype(bf16)

    packed = jnp.concatenate(
        [
            turned(query_raw, query_scale, query_gain_flat),
            turned(key_raw, key_scale, key_gain_flat),
            value_low.reshape(head_shape),
        ],
        axis=3,
    )
    packed = to_heads(packed)
    head_parts = []
    for number in range(per_device):
        parts = [
            packed[number, :, part * head_size : (part + 1) * head_size] for part in range(3)
        ]
        head_parts.append((parts, attention_forward(*parts, causal, score_scale)))
    attended = from_heads(jnp.stack([out for _, (out, _) in head_parts]))
    attended = attended.reshape(flat_rows, local_width)

    attn_part = mm(attended, w_output).astype(bf16).reshape(micro_count, rows_here, width)
    attn_rows = halve_rows(attn_part, tensor_steps[::-1], 1, f32)
    own_source = source[:, :own_rows]
    residual = own_source + attn_rows
    scale_out = rms_scale(residual)
    norm_out = (residual * scale_out * norm2_gain).astype(bf16)
    flat_out = norm_out.reshape(micro_count * own_rows, width)
    router_probs = jax.nn.softmax(mm(flat_out, w_router), axis=-1).reshape(
        micro_count, own_rows, experts
    )

    expert_base = expert_at * owned
    gathered = []
    out_rows = []
    row_grads = []
    prob_grads = []
    for m in range(micro_count):
        rows_all = double_rows(norm_out[m], all_steps, 0)
        probs_all = jax.nn.softmax(mm(rows_all, w_router), axis=-1) * mask_all[m].astype(f32)
        gates = lax.dynamic_slice_in_dim(probs_all, expert_base, owned, axis=1)[:, :, None]
        gate_pre = jnp.einsum("td,edf->tef", rows_all, w_gate, preferred_element_type=f32)
        up_pre = jnp.einsum("td,edf->tef", rows_all, w_up, preferred_element_type=f32)
        back = jnp.einsum("td,efd->tef", upstream_all[m], w_down, preferred_element_type=f32)
        sigmoid_gate = jax.nn.sigmoid(gate_pre)
        activated = gate_pre * sigmoid_gate
        hidden = activated * up_pre
        gated_hidden = (gates * hidden).astype(bf16)
        out_part = jnp.einsum(
            "tef,efd->td", gated_hidden, w_down, preferred_element_type=f32
        ).astype(bf16)
        gate_grad = jnp.sum(hidden * back, axis=2)
        hidden_grad = gates * back
        gate_back = (
            hidden_grad * up_pre * (sigmoid_gate * (1.0 + gate_pre * (1.0 - sigmoid_gate)))
        ).astype(bf16)
        up_back = (hidden_grad * activated).astype(bf16)
        row_part = (
            jnp.einsum("tef,edf->td", gate_back, w_gate, preferred_element_type=f32)
            + jnp.einsum("tef,edf->td", up_back, w_up, preferred_element_type=f32)
        ).astype(bf16)
        gathered.append((rows_all, upstream_all[m], gated_hidden, gate_back, up_back))
        row_grads.append(halve_rows(row_part, all_steps[::-1], 0, f32))
        spread = lax.dynamic_update_slice_in_dim(
            jnp.zeros((gate_grad.shape[0], experts), bf16), gate_grad.astype(bf16), expert_base, 1
        )
        prob_grads.append(halve_rows(spread, all_steps[::-1], 0, f32))
        out_rows.append(halve_rows(out_part, all_steps[::-1], 0, f32))
    grad_gate = sum(
        jnp.einsum("td,tef->edf", item[0], item[3], preferred_element_type=f32)
        for item in gathered
    )
    grad_up = sum(
        jnp.einsum("td,tef->edf", item[0], item[4], preferred_element_type=f32)
        for item in gathered
    )
    grad_down = sum(
        jnp.einsum("tef,td->efd", item[2], item[1], preferred_element_type=f32)
        for item in gathered
    )
    layer_out = (residual + jnp.stack(out_rows)).astype(bf16)
    layer_out = lax.all_to_all(layer_out, "tensor", split_axis=2, concat_axis=1, tiled=True)

    prob_grad = jnp.stack(prob_grads) * mask_rows
    logit_grad = (
        router_probs * (prob_grad - jnp.sum(prob_grad * router_probs, axis=2, keepdims=True))
    ).astype(bf16)
    flat_logit = logit_grad.reshape(micro_count * own_rows, experts)
    norm_out_grad = jnp.stack(row_grads) + mm_t(flat_logit, w_router).reshape(residual.shape)
    router_part = t_mm(flat_logit, flat_out)
    second_gain_part = jnp.sum(norm_out_grad * residual * scale_out, axis=(0, 1))
    weighted_out = norm_out_grad * norm2_gain
    residual_grad = (
        grad_rows.astype(f32)
        + scale_out * weighted_out
        - residual * scale_out**3 * jnp.mean(weighted_out * residual, axis=2, keepdims=True)
    )
    residual_low = double_rows(residual_grad.astype(bf16), tensor_steps, 1).reshape(
        flat_rows, width
    )

    first_step, later_steps = expert_steps[-1], expert_steps[:-1][::-1]

    def pair_left(operand):
        wide = columns_by_partner(operand)
        half = wide.shape[1] // 2
        return jnp.concatenate([wide[:, :half], swap(wide[:, half:], *first_step)], axis=0)

    def pair_right(operand):
        return jnp.concatenate([operand, swap(operand, *first_step)], axis=0)

    def weight_grad(left_pair, right_pair):
        return halve_rows(t_mm(left_pair, right_pair).astype(bf16), later_steps, 0, f32)

    norm_in_pair = pair_left(norm_in)
    attended_pair = pair_right(attended)
    grad_output = weight_grad(pair_left(residual_low), attended_pair).T

    attended_grad = mm_t(residual_low, w_output).astype(bf16).reshape(head_shape)
    attended_grad = to_heads(attended_grad)
    head_grads = []
    for number in range(per_device):
        parts, (_, log_total) = head_parts[number]
        grads = attention_backward(*parts, log_total, attended_grad[number], causal, score_scale)
        head_grads.append(jnp.concatenate(grads, axis=1))
    packed_grad = from_heads(jnp.stack(head_grads))
    value_grad_low = packed_grad[..., 2 * head_size :].reshape(flat_rows, local_width)

    def turned_back(grad):
        grad = grad.astype(f32)
        return (grad * cosine + turn_back(grad * sine)).reshape(flat_rows, local_width)

    normed_q_grad = turned_back(packed_grad[..., :head_size])
    normed_k_grad = turned_back(packed_grad[..., head_size : 2 * head_size])
    row_dots = jnp.stack(
        [
            jnp.sum(normed_q_grad * query_gain_flat * query_raw, axis=1),
            jnp.sum(normed_k_grad * key_gain_flat * key_raw, axis=1),
        ]
    )
    row_dots = sum_over_rows(row_dots, tensor_steps, own_rows)
    query_gain_part = jnp.sum(normed_q_grad * query_raw * query_scale, axis=0)
    key_gain_part = jnp.sum(normed_k_grad * key_raw * key_scale, axis=0)
    query_grad_low = (
        query_scale * query_gain_flat * normed_q_grad
        - query_raw * query_scale**3 * row_dots[0][:, None] / width
    ).astype(bf16)
    key_grad_low = (
        key_scale * key_gain_flat * normed_k_grad
        - key_raw * key_scale**3 * row_dots[1][:, None] / width
    ).astype(bf16)
    grad_value = weight_grad(norm_in_pair, pair_right(value_grad_low))
    grad_query = weight_grad(norm_in_pair, pair_right(query_grad_low))
    grad_key = weight_grad(norm_in_pair, pair_right(key_grad_low))
    norm_in_part = (
        mm_t(query_grad_low, w_query) + mm_t(key_grad_low, w_key) + mm_t(value_grad_low, w_value)
    )
    norm_in_grad = halve_rows(
        norm_in_part.astype(bf16).reshape(micro_count, rows_here, width),
        tensor_steps[::-1],
        1,
        f32,
    )
    own_scale = scale_in[:, :own_rows]
    first_gain_part = jnp.sum(norm_in_grad * own_source * own_scale, axis=(0, 1))
    weighted_in = norm_in_grad * norm1_gain
    tokens_grad = (
        residual_grad
        + own_scale * weighted_in
        - own_source * own_scale**3 * jnp.mean(weighted_in * own_source, axis=2, keepdims=True)
    )
    tokens_grad = in_sequence(double_rows(tokens_grad.astype(bf16), tensor_steps, 1)).astype(f32)

    head_block = head_size // groups
    head_gains = jnp.stack([query_gain_part, key_gain_part]).reshape(
        2 * heads_here, groups, head_block
    )
    head_gains = head_gains.transpose(1, 0, 2).reshape(groups, 2 * heads_here * head_block)
    column_block = width // groups
    head_gains = jnp.pad(head_gains, ((0, 0), (0, column_block - head_gains.shape[1])))
    head_rows = jnp.where(
        jnp.arange(tensor_count, dtype=jnp.int32)[:, None] == tensor_at,
        head_gains.reshape(1, width),
        0.0,
    )
    small = jnp.concatenate(
        [router_part, first_gain_part[None], second_gain_part[None], head_rows], axis=0
    )
    padding = -small.shape[0] % 16
    small = jnp.pad(small, ((0, padding), (0, 0))).astype(bf16)
    small = columns_by_partner(small)
    small = halve_rows(small, expert_steps[::-1], 1)
    small = sum_over(small, tensor_steps).astype(f32)
    grad_router = small[:experts].T
    own_heads = lax.dynamic_slice_in_dim(small, experts + 2 + tensor_at, 1, axis=0)
    own_heads = own_heads[0, : 2 * heads_here * head_block].reshape(2, heads_here, head_block)
    return (
        layer_out,
        tokens_grad,
        small[experts],
        grad_query,
        grad_key,
        grad_value,
        own_heads[0],
        own_heads[1],
        grad_output,
        small[experts + 1],
        grad_router,
        grad_gate,
        grad_up,
        grad_down,
    )


def solution(mesh):
    placed = (
        P(None, "expert", None),
        P(None, "expert", None),
        P(None, "expert", None),
        P(),
        P(None, "tensor"),
        P(None, "tensor"),
        P(None, "tensor"),
        P("tensor", None),
        P("tensor", None),
        P("tensor", None),
        P(),
        P(),
        P("expert", None, "tensor"),
        P("expert", None, "tensor"),
        P("expert", "tensor", None),
    )
    return jax.shard_map(
        shards,
        mesh=mesh,
        in_specs=placed,
        out_specs=(
            P(None, "expert", "tensor"),
            P(None, "expert", None),
            P("expert"),
            P("expert", "tensor"),
            P("expert", "tensor"),
            P("expert", "tensor"),
            P("tensor", "expert"),
            P("tensor", "expert"),
            P("tensor", "expert"),
            P("expert"),
            P("expert", None),
            P("expert", None, "tensor"),
            P("expert", None, "tensor"),
            P("expert", "tensor", None),
        ),
        check_vma=False,
    )
```

time: 2730 us -> 773 us (0.28)
  waiting for transfers between devices: 1980 us -> 295 us
  local copies, waits for them, and re-layouts: 226 us -> 102 us
  other arithmetic: 152 us -> 70.8 us
  matrix products: 256 us -> 176 us
  starting transfers between devices: 43.5 us -> 112 us
  blocking collectives: 42.1 us -> 0 us
    all_to_all x8 -> x5, waiting for transfers between devices: 1190 us -> 9.94 us  [the longest x2 6.3 us: from_heads(): lax.all_to_all(blocks, 'expert', split_axis=0, concat_axis=0, tiled=True)]
    reduce_scatter x9 -> x0, waiting for transfers between devices: 388 us -> none  [the longest x2 89.1 us: shards(): lax.psum_scatter(key_part.reshape(seq_total, local_width).astype(jnp.bflo...]
    ppermute x0 -> x86, waiting for transfers between devices: none -> 285 us  [swap(): lax.ppermute(operand, axis_name, [(i, i ^ bit) for i in range(count)])]
    unnamed x24 -> x0, waiting for transfers between devices: 182 us -> none
    gather x16 -> x0, local copies, waits for them, and re-layouts: 137 us -> none  [the longest x2 30.3 us: shards(): jnp.take(upstream, token_at, axis=0)]
    all_gather x4 -> x0, waiting for transfers between devices: 119 us -> none  [the longest x2 68.8 us: shards(): lax.all_gather(value_low, 'expert', axis=0, tiled=True)]
    psum x3 -> x0, waiting for transfers between devices: 101 us -> none  [the longest x1 36.8 us: shards(): lax.psum(norm_in_part.astype(jnp.bfloat16), 'tensor').astype(jnp.float32)]
    ppermute x0 -> x86, starting transfers between devices: none -> 90.2 us  [swap(): lax.ppermute(operand, axis_name, [(i, i ^ bit) for i in range(count)])]
  transfers between devices with their start and end apart: 28 -> 91, of which waited for: 26 -> 42; matrix products, arithmetic and copies ran while one was open for 18% -> 42% of each run, Pallas kernels for 0% -> 0%
where the time goes in v1:
time: 773 us; the launch traced here: 764 us
  waiting for transfers between devices  295 us (38%)
  matrix products  176 us (23%)
  starting transfers between devices  112 us (14%)
  local copies, waits for them, and re-layouts  102 us (13%)
  other arithmetic  70.8 us (9%)
    ppermute x86, waiting for transfers between devices, swap(): lax.ppermute(operand, axis_name, [(i, i ^ bit) for i in range(count)])  285 us
    ppermute x86, starting transfers between devices, swap(): lax.ppermute(operand, axis_name, [(i, i ^ bit) for i in range(count)])  90.2 us
    unnamed x263, local copies, waits for them, and re-layouts  51.5 us
    dot_general x2, matrix products, shards(): jnp.einsum('td,efd->tef', upstream_all[m], w_down, preferred_element_type...  25.1 us
    dot_general x2, matrix products, shards(): jnp.einsum('td,tef->edf', item[0], item[4], preferred_element_type=f32)  21.2 us
    convert_element_type x33, other arithmetic, halve_rows(): total.astype(bf16)  18.4 us
    dot_general x2, matrix products, shards(): jnp.einsum('td,edf->tef', rows_all, w_up, preferred_element_type=f32)  15.9 us
  transfers between devices with their start and end apart: 91, of which 42 were waited for; matrix products, arithmetic and copies ran while one was open for 42% of the time, Pallas kernels for 0%

profile of v1, /device:TPU:0, one launch (start us, length us, event | category | flops | bytes accessed | tf_op | source)
XLA Modules:
  0.0 763.7 jit_solution(4126619719615787522)
XLA Ops:
  107.1 10.1 %collective-permute-done.41 = bf16[128,2048]{1,0:T(8,128)(2,1)S(1)} collective-permute-done((bf16[128,2048]{1,0:T(8,128)(2,1)S(1)}, bf16[128,2048]{1,0:T(8,128)(2,1)S(1)}, u32[]{:S(2)}, u32[]{:S(2)}) %collective-permute-start.41) | collective-permute-done | bytes 524320 | tf_op jit(solution)/shard_map/ppermute | solution.py:45
  145.8 19.1 %collective-permute-done.32 = bf16[256,2048]{1,0:T(8,128)(2,1)S(1)} collective-permute-done((bf16[256,2048]{1,0:T(8,128)(2,1)S(1)}, bf16[256,2048]{1,0:T(8,128)(2,1)S(1)}, u32[]{:S(2)}, u32[]{:S(2)}) %collective-permute-start.32) | collective-permute-done | bytes 1048608 | tf_op jit(solution)/shard_map/ppermute | solution.py:45
  167.1 6.9 collective-permute-done.5
  175.6 16.1 %collective-permute-done.22 = bf16[256,2048]{1,0:T(8,128)(2,1)S(1)} collective-permute-done((bf16[256,2048]{1,0:T(8,128)(2,1)S(1)}, bf16[256,2048]{1,0:T(8,128)(2,1)S(1)}, u32[]{:S(2)}, u32[]{:S(2)}) %collective-permute-start.22) | collective-permute-done | bytes 1048608 | tf_op jit(solution)/shard_map/ppermute | solution.py:45
  194.2 24.4 %collective-permute-done.7 = bf16[256,2048]{1,0:T(8,128)(2,1)S(1)} collective-permute-done((bf16[256,2048]{1,0:T(8,128)(2,1)S(1)}, bf16[256,2048]{1,0:T(8,128)(2,1)S(1)}, u32[]{:S(2)}, u32[]{:S(2)}) %collective-permute-start.7) | collective-permute-done | bytes 1048608 | tf_op jit(solution)/shard_map/ppermute | solution.py:45
  235.8 9.7 %fusion.22 = f32[1024,4,256]{0,2,1:T(8,128)} fusion(bf16[4,2048,256]{2,1,0:T(8,128)(2,1)} %param.29, bf16[1024,2048]{1,0:T(8,128)(2,1)S(1)} %constant_dynamic-update-slice_fusion.5), kind=kOutput, calls=%fused_computation.28 | convolution fusion | flops 4294967296 | bytes 12582912 | tf_op jit(solution)/shard_map/td,edf->tef/dot_general | solution.py:286
  253.8 11.8 %multiply_reduce_fusion.1 = (bf16[1024,4]{0,1:T(4,128)(2,1)S(1)}, bf16[1024,4,256]{0,2,1:T(8,128)(2,1)S(1)}, bf16[1024,4,256]{0,2,1:T(8,128)(2,1)}, bf16[1024,4,256]{0,2,1:T(8,128)(2,1)}) fusion(f32[1024,4,256]{0,2,1:T(8,128)} %fusion.14, f32[1024,4,256]{0,2,1:T(8,128)} %fusion.16, f32[1024,4]{0,1:T(4,128)S(1)} %divide_multiply_fusion, ...), kind=kOutput, calls=%fused_computation.34 | convolution fusion | flops 4314886144 | bytes 23093248 | tf_op jit(solution)/shard_map/td,efd->tef/dot_general | solution.py:287
  272.4 6.9 fusion.12
  281.9 13.3 %multiply_reduce_fusion.2 = (bf16[1024,4]{0,1:T(4,128)(2,1)S(1)}, bf16[1024,4,256]{0,2,1:T(8,128)(2,1)}, bf16[1024,4,256]{0,2,1:T(8,128)(2,1)}, bf16[1024,4,256]{0,2,1:T(8,128)(2,1)}) fusion(f32[1024,4,256]{0,2,1:T(8,128)} %fusion.22, f32[1024,4,256]{0,2,1:T(8,128)} %fusion.24, f32[1024,4]{0,1:T(4,128)S(1)} %divide_multiply_fusion.1, ...), kind=kOutput, calls=%fused_computation.35 | convolution fusion | flops 4314886144 | bytes 23093248 | tf_op jit(solution)/shard_map/td,efd->tef/dot_general | solution.py:287
  296.6 10.9 %fusion.10 = f32[4,256,2048]{2,1,0:T(8,128)} fusion(bf16[1024,4,256]{0,2,1:T(8,128)(2,1)} %get-tuple-element.127, bf16[1024,2048]{1,0:T(8,128)(2,1)} %copy-done.9), kind=kOutput, calls=%fused_computation.16 | convolution fusion | flops 4294967296 | bytes 14680064 | tf_op jit(solution)/shard_map/td,tef->edf/dot_general | solution.py:317
  307.5 7.4 fusion
  319.3 6.8 fusion.127
  326.1 7.9 %fusion.1 = bf16[1024,2048]{1,0:T(8,128)(2,1)S(1)} fusion(f32[1024,2048,1]{1,0,2:T(8,128)} %fusion.127, bf16[1024,4,256]{0,2,1:T(8,128)(2,1)} %get-tuple-element.129, bf16[4,2048,256]{2,1,0:T(8,128)(2,1)S(1)} %copy-done.111), kind=kOutput, calls=%fused_computation.3 | convolution fusion | flops 4299161600 | bytes 18874368 | tf_op jit(solution)/shard_map/tef,edf->td/dot_general | solution.py:303
  351.8 10.3 %add_bitcast_fusion = f32[4,2048,256]{1,2,0:T(8,128)} fusion(f32[4,256,2048]{2,1,0:T(8,128)} %fusion.10, bf16[1024,4,256]{0,2,1:T(8,128)(2,1)} %get-tuple-element.129, bf16[1024,2048]{1,0:T(8,128)(2,1)S(1)} %copy-done.8), kind=kOutput, calls=%fused_computation.6 | convolution fusion | flops 4297064448 | bytes 23068672 | tf_op jit(solution)/shard_map/td,tef->edf/dot_general | solution.py:317
  366.7 8.4 %fusion.32 = f32[4,256,2048]{2,1,0:T(8,128)} fusion(f32[4,256,2048]{2,1,0:T(8,128)S(1)} %fusion.2, bf16[1024,4,256]{0,2,1:T(8,128)(2,1)} %get-tuple-element.128, bf16[1024,2048]{1,0:T(8,128)(2,1)S(1)} %copy-done.99), kind=kOutput, calls=%fused_computation.53 | convolution fusion | flops 4297064448 | bytes 23068672 | tf_op jit(solution)/shard_map/tef,td->efd/dot_general | solution.py:321
  384.0 8.7 %copy.210 = f32[4,2048,256]{2,1,0:T(8,128)} copy(f32[4,2048,256]{1,2,0:T(8,128)} %add_bitcast_fusion.1) | data formatting | bytes 16777216
  392.7 8.8 %copy.211 = f32[4,2048,256]{2,1,0:T(8,128)} copy(f32[4,2048,256]{1,2,0:T(8,128)} %add_bitcast_fusion) | data formatting | bytes 16777216
  452.7 15.5 %collective-permute-done.45 = bf16[256,2048]{1,0:T(8,128)(2,1)S(1)} collective-permute-done((bf16[256,2048]{1,0:T(8,128)(2,1)S(1)}, bf16[256,2048]{1,0:T(8,128)(2,1)S(1)}, u32[]{:S(2)}, u32[]{:S(2)}) %collective-permute-start.45) | collective-permute-done | bytes 1048608 | tf_op jit(solution)/shard_map/ppermute | solution.py:45
  469.2 21.5 %collective-permute-done.35 = bf16[256,2048]{1,0:T(8,128)(2,1)S(1)} collective-permute-done((bf16[256,2048]{1,0:T(8,128)(2,1)S(1)}, bf16[256,2048]{1,0:T(8,128)(2,1)S(1)}, u32[]{:S(2)}, u32[]{:S(2)}) %collective-permute-start.35) | collective-permute-done | bytes 1048608 | tf_op jit(solution)/shard_map/ppermute | solution.py:45
  491.4 21.7 %collective-permute-done.25 = bf16[256,2048]{1,0:T(8,128)(2,1)S(1)} collective-permute-done((bf16[256,2048]{1,0:T(8,128)(2,1)S(1)}, bf16[256,2048]{1,0:T(8,128)(2,1)S(1)}, u32[]{:S(2)}, u32[]{:S(2)}) %collective-permute-start.25) | collective-permute-done | bytes 1048608 | tf_op jit(solution)/shard_map/ppermute | solution.py:45
  513.9 21.0 %collective-permute-done.15 = bf16[256,2048]{1,0:T(8,128)(2,1)S(1)} collective-permute-done((bf16[256,2048]{1,0:T(8,128)(2,1)S(1)}, bf16[256,2048]{1,0:T(8,128)(2,1)S(1)}, u32[]{:S(2)}, u32[]{:S(2)}) %collective-permute-start.15) | collective-permute-done | bytes 1048608 | tf_op jit(solution)/shard_map/ppermute | solution.py:45
  620.1 15.5 %collective-permute-done.84 = bf16[512,512]{1,0:T(8,128)(2,1)} collective-permute-done((bf16[512,512]{1,0:T(8,128)(2,1)}, bf16[512,512]{1,0:T(8,128)(2,1)}, u32[]{:S(2)}, u32[]{:S(2)}) %collective-permute-start.84) | collective-permute-done | bytes 524320 | tf_op jit(solution)/shard_map/ppermute | solution.py:45
  638.7 9.8 %collective-permute-done.85 = bf16[256,512]{1,0:T(8,128)(2,1)S(1)} collective-permute-done((bf16[256,512]{1,0:T(8,128)(2,1)S(1)}, bf16[256,512]{1,0:T(8,128)(2,1)S(1)}, u32[]{:S(2)}, u32[]{:S(2)}) %collective-permute-start.85) | collective-permute-done | bytes 262176 | tf_op jit(solution)/shard_map/ppermute | solution.py:45
  694.0 22.8 %collective-permute-done.68 = bf16[48,512]{1,0:T(8,128)(2,1)S(1)} collective-permute-done((bf16[48,512]{1,0:T(8,128)(2,1)S(1)}, bf16[48,512]{1,0:T(8,128)(2,1)S(1)}, u32[]{:S(2)}, u32[]{:S(2)}) %collective-permute-start.68) | collective-permute-done | bytes 49184 | tf_op jit(solution)/shard_map/ppermute | solution.py:45
  (700 shorter events, 442.0 us)
Async XLA Ops:
  10.7 37.8 %collective-permute-start.9 = (bf16[2,32,32]{1,2,0:T(8,128)(2,1)S(1)}, bf16[2,32,32]{1,2,0:T(8,128)(2,1)}, u32[]{:S(2)}, u32[]{:S(2)}) collective-permute-start(bf16[2,32,32]{1,2,0:T(8,128)(2,1)S(1)} %copy.184), channel_id=1, source_target_pairs={{0,16},{4,20},{8,24},{12,28},{16,0},{20,4},{24,8},{28,12},{1,17},{... | collective-permute-start | bytes 12296 | tf_op jit(solution)/shard_map/ppermute | solution.py:45
  15.0 57.6 %collective-permute-start.39 = (bf16[32,2048]{1,0:T(8,128)(2,1)S(1)}, bf16[32,2048]{1,0:T(8,128)(2,1)}, u32[]{:S(2)}, u32[]{:S(2)}) collective-permute-start(bf16[32,2048]{1,0:T(8,128)(2,1)S(1)} %get-tuple-element.153), channel_id=1, source_target_pairs={{0,16},{4,20},{8,24},{12,28},{16,0},{20,4},{24,8},{28,12},{1,17},{... | collective-permute-start | bytes 393224 | tf_op jit(solution)/shard_map/ppermute | solution.py:45
  15.5 61.4 %collective-permute-start.29 = (bf16[32,2048]{1,0:T(8,128)(2,1)S(1)}, bf16[32,2048]{1,0:T(8,128)(2,1)S(1)}, u32[]{:S(2)}, u32[]{:S(2)}) collective-permute-start(bf16[32,2048]{1,0:T(8,128)(2,1)S(1)} %get-tuple-element.111), channel_id=1, source_target_pairs={{0,16},{4,20},{8,24},{12,28},{16,0},{20,4},{24,8},{28,12},{1,17},{... | collective-permute-start | bytes 393224 | tf_op jit(solution)/shard_map/ppermute | solution.py:45
  20.9 651.1 %collective-permute-start.72 = (bf16[256,1024]{1,0:T(8,128)(2,1)}, bf16[256,1024]{1,0:T(8,128)(2,1)}, u32[]{:S(2)}, u32[]{:S(2)}) collective-permute-start(bf16[256,1024]{1,0:T(8,128)(2,1)} %pad_maximum_fusion.15), channel_id=1, source_target_pairs={{0,4},{4,0},{8,12},{12,8},{16,20},{20,16},{24,28},{28,24},{1,5},{5... | collective-permute-start | bytes 1572872 | tf_op jit(solution)/shard_map/ppermute | solution.py:45
  127.9 36.9 %collective-permute-start.32 = (bf16[256,2048]{1,0:T(8,128)(2,1)S(1)}, bf16[256,2048]{1,0:T(8,128)(2,1)S(1)}, u32[]{:S(2)}, u32[]{:S(2)}) collective-permute-start(bf16[256,2048]{1,0:T(8,128)(2,1)S(1)} %pad_maximum_fusion.2), channel_id=1, source_target_pairs={{0,2},{1,3},{2,0},{3,1},{4,6},{5,7},{6,4},{7,5},{8,10},{9,11},{10,... | collective-permute-start | bytes 3145736 | tf_op jit(solution)/shard_map/ppermute | solution.py:45
  144.6 49.2 %collective-permute-start.43 = (bf16[512,2048]{1,0:T(8,128)(2,1)S(1)}, bf16[512,2048]{1,0:T(8,128)(2,1)S(1)}, u32[]{:S(2)}, u32[]{:S(2)}) collective-permute-start(bf16[512,2048]{1,0:T(8,128)(2,1)S(1)} %get-tuple-element.154), channel_id=1, source_target_pairs={{0,1},{1,0},{2,3},{3,2},{4,5},{5,4},{6,7},{7,6},{8,9},{9,8},{10,11... | collective-permute-start | bytes 6291464 | tf_op jit(solution)/shard_map/ppermute | solution.py:45
  280.6 121.0 %collective-permute-start.54 = (bf16[512,32]{1,0:T(8,128)(2,1)S(1)}, bf16[512,32]{1,0:T(8,128)(2,1)S(1)}, u32[]{:S(2)}, u32[]{:S(2)}) collective-permute-start(bf16[512,32]{1,0:T(8,128)(2,1)S(1)} %slice.566), channel_id=1, source_target_pairs={{0,1},{1,0},{2,3},{3,2},{4,5},{5,4},{6,7},{7,6},{8,9},{9,8},{10,11... | collective-permute-start | bytes 98312 | tf_op jit(solution)/shard_map/ppermute | solution.py:45
  296.5 105.7 %collective-permute-start.49 = (bf16[512,32]{1,0:T(8,128)(2,1)S(1)}, bf16[512,32]{1,0:T(8,128)(2,1)S(1)}, u32[]{:S(2)}, u32[]{:S(2)}) collective-permute-start(bf16[512,32]{1,0:T(8,128)(2,1)S(1)} %slice.556), channel_id=1, source_target_pairs={{0,1},{1,0},{2,3},{3,2},{4,5},{5,4},{6,7},{7,6},{8,9},{9,8},{10,11... | collective-permute-start | bytes 98312 | tf_op jit(solution)/shard_map/ppermute | solution.py:45
  318.0 119.1 %collective-permute-start.44 = (bf16[512,2048]{1,0:T(8,128)(2,1)}, bf16[512,2048]{1,0:T(8,128)(2,1)}, u32[]{:S(2)}, u32[]{:S(2)}) collective-permute-start(bf16[512,2048]{1,0:T(8,128)(2,1)} %slice.546), channel_id=1, source_target_pairs={{0,1},{1,0},{2,3},{3,2},{4,5},{5,4},{6,7},{7,6},{8,9},{9,8},{10,11... | collective-permute-start | bytes 6291464 | tf_op jit(solution)/shard_map/ppermute | solution.py:45
  337.1 105.0 %collective-permute-start.34 = (bf16[512,2048]{1,0:T(8,128)(2,1)}, bf16[512,2048]{1,0:T(8,128)(2,1)}, u32[]{:S(2)}, u32[]{:S(2)}) collective-permute-start(bf16[512,2048]{1,0:T(8,128)(2,1)} %slice.536), channel_id=1, source_target_pairs={{0,1},{1,0},{2,3},{3,2},{4,5},{5,4},{6,7},{7,6},{8,9},{9,8},{10,11... | collective-permute-start | bytes 6291464 | tf_op jit(solution)/shard_map/ppermute | solution.py:45
  401.6 43.8 %collective-permute-start.24 = (bf16[512,2048]{1,0:T(8,128)(2,1)}, bf16[512,2048]{1,0:T(8,128)(2,1)}, u32[]{:S(2)}, u32[]{:S(2)}) collective-permute-start(bf16[512,2048]{1,0:T(8,128)(2,1)} %slice.526), channel_id=1, source_target_pairs={{0,1},{1,0},{2,3},{3,2},{4,5},{5,4},{6,7},{7,6},{8,9},{9,8},{10,11... | collective-permute-start | bytes 6291464 | tf_op jit(solution)/shard_map/ppermute | solution.py:45
  437.1 170.3 %collective-permute-start.83 = (bf16[256,512]{1,0:T(8,128)(2,1)}, bf16[256,512]{1,0:T(8,128)(2,1)}, u32[]{:S(2)}, u32[]{:S(2)}) collective-permute-start(bf16[256,512]{1,0:T(8,128)(2,1)} %bitcast.287), channel_id=1, source_target_pairs={{0,4},{4,0},{8,12},{12,8},{16,20},{20,16},{24,28},{28,24},{1,5},{5... | collective-permute-start | bytes 786440 | tf_op jit(solution)/shard_map/ppermute | solution.py:45
  445.4 45.3 %collective-permute-start.35 = (bf16[256,2048]{1,0:T(8,128)(2,1)S(1)}, bf16[256,2048]{1,0:T(8,128)(2,1)S(1)}, u32[]{:S(2)}, u32[]{:S(2)}) collective-permute-start(bf16[256,2048]{1,0:T(8,128)(2,1)S(1)} %slice.538), channel_id=1, source_target_pairs={{0,2},{1,3},{2,0},{3,1},{4,6},{5,7},{6,4},{7,5},{8,10},{9,11},{10,... | collective-permute-start | bytes 3145736 | tf_op jit(solution)/shard_map/ppermute | solution.py:45
  449.6 63.5 %collective-permute-start.25 = (bf16[256,2048]{1,0:T(8,128)(2,1)S(1)}, bf16[256,2048]{1,0:T(8,128)(2,1)S(1)}, u32[]{:S(2)}, u32[]{:S(2)}) collective-permute-start(bf16[256,2048]{1,0:T(8,128)(2,1)S(1)} %slice.528), channel_id=1, source_target_pairs={{0,2},{1,3},{2,0},{3,1},{4,6},{5,7},{6,4},{7,5},{8,10},{9,11},{10,... | collective-permute-start | bytes 3145736 | tf_op jit(solution)/shard_map/ppermute | solution.py:45
  468.2 66.7 %collective-permute-start.15 = (bf16[256,2048]{1,0:T(8,128)(2,1)S(1)}, bf16[256,2048]{1,0:T(8,128)(2,1)S(1)}, u32[]{:S(2)}, u32[]{:S(2)}) collective-permute-start(bf16[256,2048]{1,0:T(8,128)(2,1)S(1)} %slice.516), channel_id=1, source_target_pairs={{0,2},{1,3},{2,0},{3,1},{4,6},{5,7},{6,4},{7,5},{8,10},{9,11},{10,... | collective-permute-start | bytes 3145736 | tf_op jit(solution)/shard_map/ppermute | solution.py:45
  490.7 45.0 %collective-permute-start.46 = (bf16[128,2048]{1,0:T(8,128)(2,1)S(1)}, bf16[128,2048]{1,0:T(8,128)(2,1)S(1)}, u32[]{:S(2)}, u32[]{:S(2)}) collective-permute-start(bf16[128,2048]{1,0:T(8,128)(2,1)S(1)} %slice.550), channel_id=1, source_target_pairs={{0,4},{4,0},{8,12},{12,8},{16,20},{20,16},{24,28},{28,24},{1,5},{5... | collective-permute-start | bytes 1572872 | tf_op jit(solution)/shard_map/ppermute | solution.py:45
  534.9 30.4 %collective-permute-start.26 = (bf16[128,2048]{1,0:T(8,128)(2,1)S(1)}, bf16[128,2048]{1,0:T(8,128)(2,1)S(1)}, u32[]{:S(2)}, u32[]{:S(2)}) collective-permute-start(bf16[128,2048]{1,0:T(8,128)(2,1)S(1)} %slice.530), channel_id=1, source_target_pairs={{0,4},{4,0},{8,12},{12,8},{16,20},{20,16},{24,28},{28,24},{1,5},{5... | collective-permute-start | bytes 1572872 | tf_op jit(solution)/shard_map/ppermute | solution.py:45
  535.7 35.7 %collective-permute-start.16 = (bf16[128,2048]{1,0:T(8,128)(2,1)S(1)}, bf16[128,2048]{1,0:T(8,128)(2,1)S(1)}, u32[]{:S(2)}, u32[]{:S(2)}) collective-permute-start(bf16[128,2048]{1,0:T(8,128)(2,1)S(1)} %slice.518), channel_id=1, source_target_pairs={{0,4},{4,0},{8,12},{12,8},{16,20},{20,16},{24,28},{28,24},{1,5},{5... | collective-permute-start | bytes 1572872 | tf_op jit(solution)/shard_map/ppermute | solution.py:45
  575.9 42.4 %collective-permute-start.28 = (bf16[32,2048]{1,0:T(8,128)(2,1)}, bf16[32,2048]{1,0:T(8,128)(2,1)}, u32[]{:S(2)}, u32[]{:S(2)}) collective-permute-start(bf16[32,2048]{1,0:T(8,128)(2,1)} %slice.534), channel_id=1, source_target_pairs={{0,16},{4,20},{8,24},{12,28},{16,0},{20,4},{24,8},{28,12},{1,17},{... | collective-permute-start | bytes 393224 | tf_op jit(solution)/shard_map/ppermute | solution.py:45
  589.2 47.9 %collective-permute-start.18 = (bf16[32,2048]{1,0:T(8,128)(2,1)}, bf16[32,2048]{1,0:T(8,128)(2,1)}, u32[]{:S(2)}, u32[]{:S(2)}) collective-permute-start(bf16[32,2048]{1,0:T(8,128)(2,1)} %slice.522), channel_id=1, source_target_pairs={{0,16},{4,20},{8,24},{12,28},{16,0},{20,4},{24,8},{28,12},{1,17},{... | collective-permute-start | bytes 393224 | tf_op jit(solution)/shard_map/ppermute | solution.py:45
  614.5 36.9 %all-to-all-start.4 = ((bf16[8,128,384]{2,1,0:T(8,128)(2,1)}), bf16[8,128,384]{2,1,0:T(8,128)(2,1)S(1)}, u32[]{:S(2)}, u32[]{:S(2)}) async-start(bf16[8,128,384]{2,1,0:T(8,128)(2,1)} %bitcast.304), calls=%async_computation.4 | async-start | bytes 1572864 | tf_op jit(solution)/shard_map/all_to_all | solution.py:201
  682.8 47.0 %collective-permute-start.74 = (bf16[512,512]{1,0:T(8,128)(2,1)}, bf16[512,512]{1,0:T(8,128)(2,1)}, u32[]{:S(2)}, u32[]{:S(2)}) collective-permute-start(bf16[512,512]{1,0:T(8,128)(2,1)} %slice.594), channel_id=1, source_target_pairs={{0,8},{4,12},{8,0},{12,4},{16,24},{20,28},{24,16},{28,20},{1,9},{5... | collective-permute-start | bytes 1572872 | tf_op jit(solution)/shard_map/ppermute | solution.py:45
  686.8 52.9 %collective-permute-start.77 = (bf16[512,512]{1,0:T(8,128)(2,1)}, bf16[512,512]{1,0:T(8,128)(2,1)}, u32[]{:S(2)}, u32[]{:S(2)}) collective-permute-start(bf16[512,512]{1,0:T(8,128)(2,1)} %slice.598), channel_id=1, source_target_pairs={{0,8},{4,12},{8,0},{12,4},{16,24},{20,28},{24,16},{28,20},{1,9},{5... | collective-permute-start | bytes 1572872 | tf_op jit(solution)/shard_map/ppermute | solution.py:45
  689.9 63.9 %collective-permute-start.81 = (bf16[256,512]{1,0:T(8,128)(2,1)}, bf16[256,512]{1,0:T(8,128)(2,1)}, u32[]{:S(2)}, u32[]{:S(2)}) collective-permute-start(bf16[256,512]{1,0:T(8,128)(2,1)} %slice.604), channel_id=1, source_target_pairs={{0,16},{4,20},{8,24},{12,28},{16,0},{20,4},{24,8},{28,12},{1,17},{... | collective-permute-start | bytes 786440 | tf_op jit(solution)/shard_map/ppermute | solution.py:45
  (186 other events, 2170.0 us)

commit v2 on v1

v2 whole, which is shorter than its diff:
```python
import functools

import jax
import jax.numpy as jnp
from jax import lax
from jax.experimental import pallas as pl
from jax.experimental.pallas import tpu as pltpu
from jax.sharding import PartitionSpec as P

eps = 1e-05
theta_base = 10000.0
masked_score = -1e30
bf16 = jnp.bfloat16
f32 = jnp.float32
vmem_limit = 56 * 1024 * 1024
expert_rows_most = 1024


def rms_scale(operand):
    return lax.rsqrt(jnp.mean(operand * operand, axis=-1, keepdims=True) + eps)


def turn_half(operand):
    middle = operand.shape[-1] // 2
    return jnp.concatenate([-operand[..., middle:], operand[..., :middle]], axis=-1)


def turn_back(operand):
    middle = operand.shape[-1] // 2
    return jnp.concatenate([operand[..., middle:], -operand[..., :middle]], axis=-1)


def bits_of(count):
    bits = []
    bit = count // 2
    while bit:
        bits.append(bit)
        bit //= 2
    return bits


def partner_order(bits):
    order = [0]
    for bit in bits:
        order = order + [place ^ bit for place in order]
    return order


def swap(operand, axis_name, bit):
    count = lax.axis_size(axis_name)
    return lax.ppermute(operand, axis_name, [(i, i ^ bit) for i in range(count)])


def double_rows(operand, steps, axis):
    for axis_name, bit in steps:
        operand = jnp.concatenate([operand, swap(operand, axis_name, bit)], axis=axis)
    return operand


def halve_rows(operand, steps, axis, last=bf16):
    for number, (axis_name, bit) in enumerate(steps):
        half = operand.shape[axis] // 2
        kept = lax.slice_in_dim(operand, 0, half, axis=axis)
        sent = lax.slice_in_dim(operand, half, 2 * half, axis=axis)
        total = kept.astype(f32) + swap(sent, axis_name, bit).astype(f32)
        operand = total if number == len(steps) - 1 and last == f32 else total.astype(bf16)
    return operand


def sum_over(operand, steps):
    for axis_name, bit in steps:
        operand = operand + swap(operand, axis_name, bit)
    return operand


def sum_over_rows(operand, steps, own_rows):
    shape = operand.shape
    blocked = operand.reshape((-1,) + (2,) * len(steps) + (own_rows,))
    for number, (axis_name, bit) in enumerate(steps):
        blocked = blocked + jnp.flip(swap(blocked, axis_name, bit), axis=len(steps) - number)
    return blocked.reshape(shape)


def mm(left, right):
    return jnp.dot(left, right, preferred_element_type=f32)


def mm_t(left, right):
    return lax.dot_general(left, right, (((1,), (1,)), ((), ())), preferred_element_type=f32)


def t_mm(left, right):
    return lax.dot_general(left, right, (((0,), (0,)), ((), ())), preferred_element_type=f32)


def after(operand, *others):
    def nothing(*refs):
        pass

    anywhere = pl.BlockSpec(memory_space=pl.ANY)
    return pl.pallas_call(
        nothing,
        out_shape=jax.ShapeDtypeStruct(operand.shape, operand.dtype),
        in_specs=[anywhere] * (1 + len(others)),
        out_specs=anywhere,
        input_output_aliases={0: 0},
    )(operand, *others)


def after_all(operands, *others):
    return [after(operand, *others) for operand in operands] if others else list(operands)


def upstream_kernel(place, blocks, width, table_ref, down_ref, gathered_ref, *refs):
    back_ref, mask_ref, rows_ref, sems = refs[-4:]
    own_rows = rows_ref.shape[0] // blocks

    @pl.when(pl.program_id(0) == 0)
    def _():
        copies = []
        for number in range(blocks):
            start = pl.multiple_of(table_ref[place * blocks + number] * own_rows, own_rows)
            source = gathered_ref.at[pl.ds(start, own_rows)]
            there = pl.ds(number * own_rows, own_rows)
            copies.append(
                pltpu.make_async_copy(
                    source.at[:, pl.ds(0, width)], rows_ref.at[there], sems.at[0, number]
                )
            )
            copies.append(
                pltpu.make_async_copy(
                    source.at[:, pl.ds(width, 128)], mask_ref.at[there], sems.at[1, number]
                )
            )
        for copy in copies:
            copy.start()
        for copy in copies:
            copy.wait()

    back_ref[...] = mm_t(rows_ref[...], down_ref[0])


def upstream_products(place, calls, table, gathered, w_down, kept, tokens):
    owned, hidden_width, width = w_down.shape
    blocks = table.shape[0] // calls
    rows = gathered.shape[0] // calls
    anywhere = pl.BlockSpec(memory_space=pl.ANY)
    others = [gathered] + kept + tokens
    return pl.pallas_call(
        functools.partial(upstream_kernel, place, blocks, width),
        out_shape=[
            jax.ShapeDtypeStruct((rows, owned * hidden_width), f32),
            jax.ShapeDtypeStruct((rows, 128), bf16),
            jax.ShapeDtypeStruct((calls * rows, width), bf16),
        ],
        grid_spec=pltpu.PrefetchScalarGridSpec(
            num_scalar_prefetch=1,
            grid=(owned,),
            in_specs=[pl.BlockSpec((1, hidden_width, width), lambda step, table: (step, 0, 0))]
            + [anywhere] * len(others),
            out_specs=[
                pl.BlockSpec((rows, hidden_width), lambda step, table: (0, step)),
                pl.BlockSpec((rows, 128), lambda step, table: (0, 0)),
                pl.BlockSpec((rows, width), lambda step, table: (place, 0)),
            ],
            scratch_shapes=[pltpu.SemaphoreType.DMA((2, blocks))],
        ),
        input_output_aliases={3: 2} if kept else {},
        compiler_params=pltpu.CompilerParams(vmem_limit_bytes=vmem_limit),
        cost_estimate=pl.CostEstimate(
            flops=2 * rows * width * owned * hidden_width,
            bytes_accessed=8 * rows * width,
            transcendentals=0,
        ),
    )(table, w_down, *others)


def expert_kernel(
    plan, copy_count, width, base_ref, mask_ref, router_ref, gate_ref, up_ref, back_ref, *refs
):
    piece_count = sum(len(block) for block in plan)
    piece_refs = refs[:piece_count]
    part_refs = refs[-11 - copy_count : -11]
    copy_ref, gated_ref, gate_back_ref, up_back_ref = refs[-11:-7]
    rows, gates, ups, probs, row_sems, gate_sems, up_sems = refs[-7:]
    step = pl.program_id(0)
    experts = router_ref.shape[1]
    owned, _, hidden_width = gate_ref.shape

    def row_copies(block):
        copies, start = [], 0
        first = sum(len(item) for item in plan[:block])
        for number in range(len(plan[block])):
            piece_ref = piece_refs[first + number]
            count = piece_ref.shape[0]
            copies.append(
                pltpu.make_async_copy(
                    piece_ref,
                    rows.at[block % 2, pl.ds(start, count)],
                    row_sems.at[block % 2, number],
                )
            )
            start += count
        return copies

    def weight_copies(number):
        here = pl.ds(number * hidden_width, hidden_width)
        return [
            pltpu.make_async_copy(gate_ref.at[number], gates.at[:, here], gate_sems.at[number]),
            pltpu.make_async_copy(up_ref.at[number], ups.at[:, here], up_sems.at[number]),
        ]

    @pl.when(step == 0)
    def _():
        for copy in row_copies(0):
            copy.start()
        for number in range(owned):
            for copy in weight_copies(number):
                copy.start()

    for block in range(len(plan)):

        @pl.when(step == block)
        def _(block=block):
            for copy in row_copies(block):
                copy.wait()
            if block + 1 < len(plan):
                for copy in row_copies(block + 1):
                    copy.start()

    own_rows = rows[step % 2]
    copy_ref[...] = own_rows
    logits = mm(own_rows, router_ref[...])
    weights = jnp.exp(logits - jnp.max(logits, axis=1, keepdims=True))
    weights = weights / jnp.sum(weights, axis=1, keepdims=True)
    probs[...] = weights * mask_ref[:, :experts].astype(f32)
    lane = lax.broadcasted_iota(jnp.int32, probs.shape, 1)
    slope_lane = lax.broadcasted_iota(jnp.int32, (own_rows.shape[0], 128), 1)

    slopes = jnp.zeros(slope_lane.shape, f32)
    for number in range(owned):
        here = slice(number * hidden_width, (number + 1) * hidden_width)
        owner = base_ref[0] + number

        @pl.when(step == 0)
        def _(number=number):
            for copy in weight_copies(number):
                copy.wait()

        gate = jnp.sum(jnp.where(lane == owner, probs[...], 0.0), axis=1, keepdims=True)
        gate_pre = mm(rows[step % 2], gates[:, here])
        up_pre = mm(rows[step % 2], ups[:, here])
        back = back_ref[:, here]
        sigmoid_gate = 1.0 / (1.0 + jnp.exp(-gate_pre))
        activated = gate_pre * sigmoid_gate
        hidden = activated * up_pre
        gated_ref[:, here] = (gate * hidden).astype(bf16)
        slope = jnp.sum(hidden * back, axis=1, keepdims=True)
        slopes = slopes + jnp.where(slope_lane == owner, slope, 0.0)
        hidden_grad = gate * back
        gate_back_ref[:, here] = (
            hidden_grad * up_pre * (sigmoid_gate * (1.0 + gate_pre * (1.0 - sigmoid_gate)))
        ).astype(bf16)
        up_back_ref[:, here] = (hidden_grad * activated).astype(bf16)
    part = mm_t(gate_back_ref[...], gates[...]) + mm_t(up_back_ref[...], ups[...])
    part = part.astype(bf16)
    per_copy = len(plan) // copy_count
    for copy, part_ref in enumerate(part_refs):

        @pl.when(step // per_copy == copy)
        def _(part_ref=part_ref):
            part_ref[:, :width] = part
            part_ref[:, width:] = slopes.astype(bf16)


def expert_call(
    place, total_rows, part, base, copies, block_rows, mask, router, w_gate, w_up, back, kept
):
    plan, pieces = [], []
    for copy in copies:
        for piece in copy:
            if not plan or sum(item.shape[0] for item in plan[-1]) == block_rows:
                plan.append([])
            plan[-1].append(piece)
            pieces.append(piece)
    copy_count = len(copies)
    per_copy = len(plan) // copy_count
    owned, width, hidden_width = w_gate.shape
    hidden = owned * hidden_width
    experts = router.shape[1]
    blocks = len(plan)
    anywhere = pl.BlockSpec(memory_space=pl.ANY)
    here = lambda step, base_ref: (place * blocks + step, 0)
    in_specs = [
        pl.BlockSpec((block_rows, 128), lambda step, base_ref: (part * blocks + step, 0)),
        pl.BlockSpec((width, experts), lambda step, base_ref: (0, 0)),
        anywhere,
        anywhere,
        pl.BlockSpec((block_rows, hidden), lambda step, base_ref: (part * blocks + step, 0)),
    ] + [anywhere] * len(pieces)

    def part_block(copy):
        return pl.BlockSpec(
            (block_rows, width + 128),
            lambda step, base_ref: (jnp.clip(step - copy * per_copy, 0, per_copy - 1), 0),
        )

    out_specs = [part_block(copy) for copy in range(copy_count)] + [
        pl.BlockSpec((block_rows, width), here),
        pl.BlockSpec((block_rows, hidden), here),
        pl.BlockSpec((block_rows, hidden), here),
        pl.BlockSpec((block_rows, hidden), here),
    ]
    hidden_shape = jax.ShapeDtypeStruct((total_rows, hidden), bf16)
    out_shape = [
        jax.ShapeDtypeStruct((per_copy * block_rows, width + 128), bf16)
    ] * copy_count + [
        jax.ShapeDtypeStruct((total_rows, width), bf16),
        hidden_shape,
        hidden_shape,
        hidden_shape,
    ]
    aliases = {}
    if kept:
        aliases = {
            1 + len(in_specs) + number: copy_count + number for number in range(len(kept))
        }
    in_specs += [anywhere] * len(kept)
    most_pieces = max(len(block) for block in plan)
    count = blocks * block_rows
    outs = pl.pallas_call(
        functools.partial(expert_kernel, plan, copy_count, width),
        out_shape=out_shape,
        grid_spec=pltpu.PrefetchScalarGridSpec(
            num_scalar_prefetch=1,
            grid=(blocks,),
            in_specs=in_specs,
            out_specs=out_specs,
            scratch_shapes=[
                pltpu.VMEM((2, block_rows, width), bf16),
                pltpu.VMEM((width, hidden), bf16),
                pltpu.VMEM((width, hidden), bf16),
                pltpu.VMEM((block_rows, experts), f32),
                pltpu.SemaphoreType.DMA((2, most_pieces)),
                pltpu.SemaphoreType.DMA((owned,)),
                pltpu.SemaphoreType.DMA((owned,)),
            ],
        ),
        input_output_aliases=aliases,
        compiler_params=pltpu.CompilerParams(vmem_limit_bytes=vmem_limit),
        cost_estimate=pl.CostEstimate(
            flops=8 * count * width * hidden,
            bytes_accessed=4 * width * hidden + 8 * count * width,
            transcendentals=count * hidden,
        ),
    )(base, mask, router, w_gate, w_up, back, *pieces, *kept)
    return list(outs[:copy_count]), list(outs[copy_count:])


def down_kernel(copy_count, gated_ref, down_ref, *refs):
    total = None
    for number in range(down_ref.shape[0]):
        hidden_width = down_ref.shape[1]
        here = slice(number * hidden_width, (number + 1) * hidden_width)
        part = mm(gated_ref[:, here], down_ref[number])
        total = part if total is None else total + part
    for copy, out_ref in enumerate(refs[-copy_count:]):

        @pl.when(pl.program_id(0) == copy)
        def _(out_ref=out_ref):
            out_ref[...] = total.astype(bf16)


def down_products(place, calls, copy_count, gated, w_down, tokens):
    owned, hidden_width, width = w_down.shape
    block = gated.shape[0] // (calls * copy_count)
    return pl.pallas_call(
        functools.partial(down_kernel, copy_count),
        out_shape=[jax.ShapeDtypeStruct((block, width), bf16)] * copy_count,
        grid=(copy_count,),
        in_specs=[
            pl.BlockSpec(
                (block, owned * hidden_width), lambda step: (place * copy_count + step, 0)
            ),
            pl.BlockSpec((owned, hidden_width, width), lambda step: (0, 0, 0)),
        ]
        + [pl.BlockSpec(memory_space=pl.ANY)] * len(tokens),
        out_specs=[pl.BlockSpec((block, width), lambda step: (0, 0))] * copy_count,
        compiler_params=pltpu.CompilerParams(vmem_limit_bytes=vmem_limit),
        cost_estimate=pl.CostEstimate(
            flops=2 * block * copy_count * width * owned * hidden_width,
            bytes_accessed=4 * block * copy_count * width,
            transcendentals=0,
        ),
    )(gated, w_down, *tokens)


def product_kernel(left_ref, right_ref, *refs):
    refs[-1][0] = t_mm(left_ref[...], right_ref[...])


def expert_grads(left, right, owned, tokens):
    total_rows = left.shape[0]
    whole = lambda count: pl.BlockSpec(
        (total_rows, count), lambda step: (0, 0), pipeline_mode=pl.Buffered(1)
    )
    cut = lambda count: pl.BlockSpec((total_rows, count), lambda step: (0, step))
    if left.shape[1] > right.shape[1]:
        out = (left.shape[1], right.shape[1] // owned)
        specs = [whole(out[0]), cut(out[1])]
    else:
        out = (left.shape[1] // owned, right.shape[1])
        specs = [cut(out[0]), whole(out[1])]
    return pl.pallas_call(
        product_kernel,
        grid=(owned,),
        out_shape=jax.ShapeDtypeStruct((owned,) + out, f32),
        in_specs=specs + [pl.BlockSpec(memory_space=pl.ANY)] * len(tokens),
        out_specs=pl.BlockSpec((1,) + out, lambda step: (step, 0, 0)),
        compiler_params=pltpu.CompilerParams(vmem_limit_bytes=vmem_limit),
        cost_estimate=pl.CostEstimate(
            flops=2 * total_rows * owned * out[0] * out[1],
            bytes_accessed=4 * owned * out[0] * out[1] + 4 * total_rows * max(out),
            transcendentals=0,
        ),
    )(left, right, *tokens)


def kernel_params():
    return pltpu.CompilerParams(vmem_limit_bytes=vmem_limit)


def in_vmem(count):
    return [pl.BlockSpec(memory_space=pltpu.VMEM)] * count


def as_row(columns):
    return columns.T[:8]


def as_columns(rows):
    count = rows.shape[1]
    return jnp.concatenate([rows, jnp.zeros((120, count), rows.dtype)], axis=0).T


def in_lanes(*columns):
    lane = lax.broadcasted_iota(jnp.int32, (columns[0].shape[0], 128), 1)
    total = jnp.zeros(lane.shape, f32)
    for number, column in enumerate(columns):
        total = jnp.where(lane == number, column, total)
    return total


def summed_rows(own_ref, arrived_refs, own_rows):
    total = as_columns(own_ref[...])
    count = total.shape[0] // own_rows
    places = len(arrived_refs) + 1
    for place, arrived_ref in enumerate(arrived_refs, 1):
        arrived = as_columns(arrived_ref[...])
        blocks = [
            arrived[other * own_rows : (other + 1) * own_rows]
            for other in ((block // places) * places + ((block % places) ^ place) for block in range(count))
        ]
        total = total + jnp.concatenate(blocks, axis=0)
    return total


def project_kernel(
    rows_ref, gain_ref, query_ref, key_ref, value_ref, normed_ref, q_ref, k_ref, v_ref, squares_ref, sums
):
    step = pl.program_id(0)

    @pl.when(step == 0)
    def _():
        rows = rows_ref[...].astype(f32)
        normed_ref[...] = (rows * rms_scale(rows) * gain_ref[...]).astype(bf16)

    normed = normed_ref[...]
    query, key = mm(normed, query_ref[...]), mm(normed, key_ref[...])
    q_ref[...] = query
    k_ref[...] = key
    v_ref[...] = mm(normed, value_ref[...]).astype(bf16)
    here = in_lanes(
        jnp.sum(query * query, axis=1, keepdims=True), jnp.sum(key * key, axis=1, keepdims=True)
    )
    sums[...] = jnp.where(step == 0, 0.0, sums[...]) + here
    squares_ref[...] = as_row(sums[...])


def project(rows, gain, w_query, w_key, w_value):
    count, width = rows.shape
    local_width = w_query.shape[1]
    block = min(256, local_width)
    weight = pl.BlockSpec((width, block), lambda step: (0, step))
    whole = lambda *shape: pl.BlockSpec(shape, lambda step: (0, 0))
    out = pl.BlockSpec((count, block), lambda step: (0, step))
    raw = jax.ShapeDtypeStruct((count, local_width), f32)
    return pl.pallas_call(
        project_kernel,
        grid=(local_width // block,),
        out_shape=[
            jax.ShapeDtypeStruct((count, width), bf16),
            raw,
            raw,
            jax.ShapeDtypeStruct((count, local_width), bf16),
            jax.ShapeDtypeStruct((8, count), f32),
        ],
        in_specs=[whole(count, width), whole(1, width), weight, weight, weight],
        out_specs=[whole(count, width), out, out, out, whole(8, count)],
        scratch_shapes=[pltpu.VMEM((count, 128), f32)],
        compiler_params=kernel_params(),
    )(rows, gain[None], w_query, w_key, w_value)


def turn_kernel(
    own_rows, width, partners, q_ref, k_ref, v_ref, q_gain_ref, k_gain_ref, cos_ref, sin_ref, own_ref, *refs
):
    packed_ref, scales_ref = refs[partners:]
    squares = summed_rows(own_ref, refs[:partners], own_rows)
    scales = lax.rsqrt(squares / width + eps)
    scales_ref[...] = scales
    pairs, rows, wide = packed_ref.shape
    size = wide // 3
    heads = q_ref.shape[1] // size
    for pair in range(pairs):
        micro, head = pair // heads, pair % heads
        here = slice(micro * rows, (micro + 1) * rows)
        lanes = slice(head * size, (head + 1) * size)
        for part, (raw_ref, gain_ref) in enumerate(((q_ref, q_gain_ref), (k_ref, k_gain_ref))):
            normed = raw_ref[here, lanes] * scales[here, part : part + 1] * gain_ref[:, lanes]
            turned = normed * cos_ref[...] + turn_half(normed) * sin_ref[...]
            packed_ref[pair, :, part * size : (part + 1) * size] = turned.astype(bf16)
        packed_ref[pair, :, 2 * size :] = v_ref[here, lanes]


def turn_and_pack(query, key, value, gains, cosine, sine, squares, arrived, own_rows, width, pairs):
    rows, size = cosine.shape
    count = query.shape[0]
    return pl.pallas_call(
        functools.partial(turn_kernel, own_rows, width, len(arrived)),
        out_shape=[
            jax.ShapeDtypeStruct((pairs, rows, 3 * size), bf16),
            jax.ShapeDtypeStruct((count, 128), f32),
        ],
        in_specs=in_vmem(8 + len(arrived)),
        out_specs=in_vmem(2),
        compiler_params=kernel_params(),
    )(query, key, value, *gains, cosine, sine, squares, *arrived)


def unturn_kernel(
    packed_ref, q_ref, k_ref, q_gain_ref, k_gain_ref, cos_ref, sin_ref, scales_ref,
    q_grad_ref, k_grad_ref, v_grad_ref, dots_ref, gains_ref,
):
    pairs, rows, wide = packed_ref.shape
    size = wide // 3
    heads = q_ref.shape[1] // size
    gains_ref[...] = jnp.zeros_like(gains_ref)
    dots = []
    for micro in range(pairs // heads):
        here = slice(micro * rows, (micro + 1) * rows)
        sums = [jnp.zeros((rows, 1), f32)] * 2
        for head in range(heads):
            lanes = slice(head * size, (head + 1) * size)
            refs = ((q_ref, q_gain_ref, q_grad_ref), (k_ref, k_gain_ref, k_grad_ref))
            for part, (raw_ref, gain_ref, out_ref) in enumerate(refs):
                grad = packed_ref[micro * heads + head, :, part * size : (part + 1) * size]
                grad = grad.astype(f32)
                grad = grad * cos_ref[...] + turn_back(grad * sin_ref[...])
                out_ref[here, lanes] = grad
                product = grad * raw_ref[here, lanes]
                sums[part] = sums[part] + jnp.sum(
                    product * gain_ref[:, lanes], axis=1, keepdims=True
                )
                gains_ref[part : part + 1, lanes] += jnp.sum(
                    product * scales_ref[here, part : part + 1], axis=0, keepdims=True
                )
            v_grad_ref[here, lanes] = packed_ref[micro * heads + head, :, 2 * size :]
        dots.append(in_lanes(*sums))
    dots_ref[...] = as_row(jnp.concatenate(dots, axis=0))


def unturn(packed, query, key, gains, cosine, sine, scales):
    count, local_width = query.shape
    raw = jax.ShapeDtypeStruct((count, local_width), f32)
    return pl.pallas_call(
        unturn_kernel,
        out_shape=[
            raw,
            raw,
            jax.ShapeDtypeStruct((count, local_width), bf16),
            jax.ShapeDtypeStruct((8, count), f32),
            jax.ShapeDtypeStruct((8, local_width), f32),
        ],
        in_specs=in_vmem(8),
        out_specs=in_vmem(5),
        compiler_params=kernel_params(),
    )(packed, query, key, *gains, cosine, sine, scales)


def norm_back_kernel(
    own_rows, width, partners, q_grad_ref, k_grad_ref, q_ref, k_ref, q_gain_ref, k_gain_ref, scales_ref, own_ref, *refs
):
    outs = refs[partners:]
    dots = summed_rows(own_ref, refs[:partners], own_rows)
    refs = ((q_grad_ref, q_ref, q_gain_ref), (k_grad_ref, k_ref, k_gain_ref))
    for part, (grad_ref, raw_ref, gain_ref) in enumerate(refs):
        scale = scales_ref[:, part : part + 1]
        dot = dots[:, part : part + 1]
        grad = scale * gain_ref[...] * grad_ref[...] - raw_ref[...] * (scale**3 * dot / width)
        outs[part][...] = grad.astype(bf16)


def norm_back(q_grad, k_grad, query, key, gains, scales, dots, arrived, own_rows, width):
    count, local_width = query.shape
    return pl.pallas_call(
        functools.partial(norm_back_kernel, own_rows, width, len(arrived)),
        out_shape=[jax.ShapeDtypeStruct((count, local_width), bf16)] * 2,
        in_specs=in_vmem(8 + len(arrived)),
        out_specs=in_vmem(2),
        compiler_params=kernel_params(),
    )(q_grad, k_grad, query, key, *gains, scales, dots, *arrived)


def project_back_kernel(
    q_ref, k_ref, v_ref, rows_ref, scale_ref, query_ref, key_ref, value_ref, out_ref, gain_ref
):
    part = (
        mm_t(q_ref[...], query_ref[...])
        + mm_t(k_ref[...], key_ref[...])
        + mm_t(v_ref[...], value_ref[...])
    )
    out_ref[...] = part.astype(bf16)
    rows = rows_ref[...].astype(f32) * scale_ref[...]
    gain_ref[...] = jnp.sum(part * rows, axis=0, keepdims=True)


def project_back(query_grad, key_grad, value_grad, rows, scale, w_query, w_key, w_value):
    count, width = rows.shape
    local_width = w_query.shape[1]
    block = min(512, width)
    whole = lambda *shape: pl.BlockSpec(shape, lambda step: (0, 0))
    weight = pl.BlockSpec((block, local_width), lambda step: (step, 0))
    cut = pl.BlockSpec((count, block), lambda step: (0, step))
    return pl.pallas_call(
        project_back_kernel,
        grid=(width // block,),
        out_shape=[
            jax.ShapeDtypeStruct((count, width), bf16),
            jax.ShapeDtypeStruct((1, width), f32),
        ],
        in_specs=[
            whole(count, local_width),
            whole(count, local_width),
            whole(count, local_width),
            cut,
            whole(count, 1),
            weight,
            weight,
            weight,
        ],
        out_specs=[cut, pl.BlockSpec((1, block), lambda step: (0, step))],
        compiler_params=kernel_params(),
    )(query_grad, key_grad, value_grad, rows, scale, w_query, w_key, w_value)


def rows_back_kernel(
    parts_ref, residual_ref, normed_ref, mask_ref, router_ref, gain_ref, upstream_ref,
    grad_ref, low_ref, router_grad_ref, gain_grad_ref,
):
    width = residual_ref.shape[1]
    experts = router_ref.shape[1]
    total = parts_ref[0].astype(f32)
    for number in range(1, parts_ref.shape[0]):
        total = total + parts_ref[number].astype(f32)
    normed = normed_ref[...]
    logits = mm(normed, router_ref[...])
    probs = jnp.exp(logits - jnp.max(logits, axis=1, keepdims=True))
    probs = probs / jnp.sum(probs, axis=1, keepdims=True)
    prob_grad = total[:, width : width + experts] * mask_ref[:, :experts].astype(f32)
    logit_grad = probs * (prob_grad - jnp.sum(prob_grad * probs, axis=1, keepdims=True))
    logit_grad = logit_grad.astype(bf16)
    grad = total[:, :width] + mm_t(logit_grad, router_ref[...])
    router_grad_ref[...] = t_mm(logit_grad, normed)
    residual = residual_ref[...]
    scale = rms_scale(residual)
    scaled = residual * scale
    gain_grad_ref[...] = jnp.sum(grad * scaled, axis=0, keepdims=True)
    weighted = grad * gain_ref[...]
    back = (
        upstream_ref[...].astype(f32)
        + scale * weighted
        - scaled * (scale**2 * jnp.mean(weighted * residual, axis=1, keepdims=True))
    )
    grad_ref[...] = back
    low_ref[...] = back.astype(bf16)


def rows_back(parts, residual, normed, mask, router, gain, upstream):
    rows, width = residual.shape
    return pl.pallas_call(
        rows_back_kernel,
        out_shape=[
            jax.ShapeDtypeStruct((rows, width), f32),
            jax.ShapeDtypeStruct((rows, width), bf16),
            jax.ShapeDtypeStruct((router.shape[1], width), f32),
            jax.ShapeDtypeStruct((1, width), f32),
        ],
        in_specs=in_vmem(7),
        out_specs=in_vmem(4),
        compiler_params=kernel_params(),
    )(parts, residual, normed, mask, router, gain[None], upstream)


def attention_forward(query, key, value, causal, scale):
    scores = mm_t(query, key) * scale
    scores = jnp.where(causal, scores, masked_score)
    highest = jnp.max(scores, axis=1, keepdims=True)
    log_total = highest + jnp.log(jnp.sum(jnp.exp(scores - highest), axis=1, keepdims=True))
    probs_low = jnp.exp(scores - log_total).astype(bf16)
    return mm(probs_low, value).astype(bf16), log_total


def attention_backward(query, key, value, log_total, grad, causal, scale):
    scores = mm_t(query, key) * scale
    scores = jnp.where(causal, scores, masked_score)
    probs = jnp.exp(scores - log_total)
    probs_low = probs.astype(bf16)
    dprob = mm_t(grad, value)
    score_grad = (probs * (dprob - jnp.sum(dprob * probs, axis=1, keepdims=True))).astype(bf16)
    return (
        (mm(score_grad, key) * scale).astype(bf16),
        (t_mm(score_grad, query) * scale).astype(bf16),
        t_mm(probs_low, grad).astype(bf16),
    )


def shards(
    tokens,
    out_grad,
    routes,
    norm1_gain,
    w_query,
    w_key,
    w_value,
    query_gain,
    key_gain,
    w_output,
    norm2_gain,
    w_router,
    w_gate,
    w_up,
    w_down,
):
    micro_count, rows_here, width = tokens.shape
    local_width = w_query.shape[1]
    heads_here, head_size = query_gain.shape
    experts = w_router.shape[1]
    groups = lax.axis_size("expert")
    tensor_count = lax.axis_size("tensor")
    owned, _, hidden_width = w_gate.shape
    own_rows = rows_here // tensor_count
    flat_rows = micro_count * rows_here
    score_scale = head_size ** (-0.5)
    expert_at = lax.axis_index("expert")
    tensor_at = lax.axis_index("tensor")

    expert_bits = bits_of(groups)
    tensor_bits = bits_of(tensor_count)
    tensor_steps = [("tensor", bit) for bit in tensor_bits]
    tensor_order = partner_order(tensor_bits)

    def by_partner(operand):
        return jnp.concatenate(
            [
                lax.dynamic_slice_in_dim(operand, (tensor_at ^ place) * own_rows, own_rows, axis=1)
                for place in tensor_order
            ],
            axis=1,
        )

    def in_sequence(operand):
        place_of = jnp.asarray(
            [tensor_order.index(place) for place in range(tensor_count)], jnp.int32
        )
        return jnp.concatenate(
            [
                lax.dynamic_slice_in_dim(
                    operand, place_of[tensor_at ^ place] * own_rows, own_rows, axis=1
                )
                for place in range(tensor_count)
            ],
            axis=1,
        )

    pairs = micro_count * heads_here
    per_device = max(1, pairs // groups)
    copies = max(1, groups // pairs)

    def to_heads(operand, work=None):
        wide = operand.shape[3]
        return pairs_to_heads(
            operand.transpose(0, 2, 1, 3).reshape(pairs, rows_here, wide), work
        )

    def pairs_to_heads(blocks, work=None):
        wide = blocks.shape[2]
        if copies > 1:
            blocks = jnp.repeat(blocks, copies, axis=0)
        arrived = lax.all_to_all(blocks, "expert", split_axis=0, concat_axis=0, tiled=True)
        if work is not None:
            arrived = after(arrived, *work(blocks))
        blocks = arrived.reshape(groups, per_device, rows_here, wide)
        return blocks.transpose(1, 0, 2, 3).reshape(per_device, groups * rows_here, wide)

    def pairs_from_heads(operand, others=()):
        wide = operand.shape[2]
        blocks = operand.reshape(per_device, groups, rows_here, wide).transpose(1, 0, 2, 3)
        blocks = blocks.reshape(groups * per_device, rows_here, wide)
        blocks = lax.all_to_all(blocks, "expert", split_axis=0, concat_axis=0, tiled=True)
        if others:
            blocks = after(blocks, *others)
        if copies > 1:
            blocks = blocks[::copies]
        return blocks

    def from_heads(operand, others=()):
        blocks = pairs_from_heads(operand, others)
        wide = blocks.shape[2]
        return blocks.reshape(micro_count, heads_here, rows_here, wide).transpose(0, 2, 1, 3)

    row_number = jnp.arange(own_rows, dtype=jnp.int32)
    row_in_block = jnp.concatenate(
        [(tensor_at ^ place) * own_rows + row_number for place in tensor_order]
    )
    row_pos = expert_at * rows_here + row_in_block
    frequency = theta_base ** (-(jnp.arange(head_size // 2, dtype=f32) * 2.0 / head_size))
    angles = row_pos.astype(f32)[:, None] * frequency[None, :]
    angles = jnp.concatenate([angles, angles], axis=1)
    cosine = jnp.cos(angles)
    sine = jnp.sin(angles)
    sequence_pos = (
        jnp.arange(groups, dtype=jnp.int32)[:, None] * rows_here + row_in_block[None, :]
    ).reshape(-1)
    causal = sequence_pos[None, :] <= sequence_pos[:, None]

    near, side = 1, tensor_bits[0]
    far = groups // 2
    far_groups = [[2 * place + last for place in range(far)] for last in range(2)]
    copy_count = tensor_count // 2

    def far_exchange(blocks):
        return lax.all_to_all(
            blocks, "expert", split_axis=0, concat_axis=0, axis_index_groups=far_groups, tiled=True
        )

    def gather_far(rows, work=None):
        block = far_exchange(jnp.broadcast_to(rows[None], (far,) + rows.shape))
        if work is not None:
            block = after(block, *work())
        return block.reshape((far * rows.shape[0],) + rows.shape[1:])

    def gather_sides(block, work=None):
        arrived = [swap(block, "expert", near), swap(block, "tensor", side)]
        return after_all(arrived, *work()) if work is not None else arrived

    def gather_diagonal(by_near, by_side):
        half = by_near.shape[0] // 2
        low, high = swap(by_side[:half], "expert", near), swap(by_near[half:], "tensor", side)
        return jnp.concatenate([low, high], axis=0)

    def gather_rest(block, by_near, by_side):
        half = block.shape[0] // 2
        by_both_low = swap(by_side[:half], "expert", near)
        by_both_high = swap(by_near[half:], "tensor", side)
        copies = [[[block, by_near], [by_side, by_both_low, by_both_high]]]
        for bit in tensor_bits[1:]:
            copies = copies + [
                [[swap(piece, "tensor", bit) for piece in call] for call in copy]
                for copy in copies
            ]
        return [[copy[call] for copy in copies] for call in range(2)]

    def add(*terms):
        total = terms[0].astype(f32)
        for term in terms[1:]:
            total = total + term.astype(f32)
        return total

    def reduce_copies(parts, work=None):
        for bit in tensor_bits[1:][::-1]:
            half = len(parts) // 2
            arrived = [swap(part, "tensor", bit) for part in parts[half:]]
            if work is not None and half == 1:
                arrived = after_all(arrived, *work(parts[1]))
            parts = [add(part, other).astype(bf16) for part, other in zip(parts[:half], arrived)]
        return parts[0]

    def reduce_diagonal(second, work=None):
        half, quarter = second.shape[0] // 2, second.shape[0] // 4
        low, high = second[half : half + quarter], second[half + quarter :]
        arrived = [swap(low, "expert", near), swap(high, "tensor", side)]
        return after_all(arrived, *work(low)) if work is not None else arrived

    def side_parts(first, second, from_near, from_side):
        half, quarter = second.shape[0] // 2, second.shape[0] // 4
        near_part = [first[half : half + quarter], add(first[half + quarter :], from_side)]
        side_part = [add(second[:quarter], from_near), second[quarter:half]]
        return [
            jnp.concatenate([part.astype(bf16) for part in parts], axis=0)
            for parts in (near_part, side_part)
        ]

    def reduce_sides(near_part, side_part, work=None):
        arrived = [swap(near_part, "expert", near), swap(side_part, "tensor", side)]
        return after_all(arrived, *work(near_part)) if work is not None else arrived

    def far_block(first, by_near, by_side):
        return add(first[: first.shape[0] // 2], by_near, by_side).astype(bf16)

    def reduce_far(block, work=None):
        parts = far_exchange(block.reshape((far, block.shape[0] // far) + block.shape[1:]))
        if work is not None:
            parts = after(parts, *work(block))
        return parts

    def far_sum(parts):
        return jnp.sum(parts.astype(f32), axis=0)

    high_bits = [bit for bit in expert_bits if bit >= 4]
    low_places = [place for place in range(1, min(4, groups))]

    def columns_of(operand, low_place):
        block = operand.shape[1] // groups
        return jnp.concatenate(
            [
                lax.dynamic_slice_in_dim(
                    operand, (expert_at ^ low_place ^ place) * block, block, axis=1
                )
                for place in partner_order(high_bits)
            ],
            axis=1,
        )

    near_count = min(4, groups)
    near_groups = [
        [first + place for place in range(near_count)] for first in range(0, groups, near_count)
    ]

    def near_exchange(operand):
        block = operand.shape[1] // groups
        high = expert_at - expert_at % near_count
        parts = [
            jnp.concatenate(
                [
                    lax.dynamic_slice_in_dim(
                        operand, ((high ^ above) + place) * block, block, axis=1
                    )
                    for above in partner_order(high_bits)
                ],
                axis=1,
            )
            for place in range(near_count)
        ]
        arrived = lax.all_to_all(
            jnp.stack(parts),
            "expert",
            split_axis=0,
            concat_axis=0,
            axis_index_groups=near_groups,
            tiled=True,
        )
        return arrived.reshape(near_count * flat_rows, -1)

    def near_gather(operand):
        return lax.all_gather(
            operand, "expert", axis_index_groups=near_groups, axis=0, tiled=True
        )

    def near_rows(gathered, place):
        return lax.dynamic_slice_in_dim(
            gathered, ((expert_at % 4) ^ place) * flat_rows, flat_rows, axis=0
        )

    def near_swaps(operand):
        return [swap(operand, "expert", place) for place in low_places]

    def halve_product(product):
        return halve_rows(product, [("expert", bit) for bit in high_bits[::-1]], 0, f32)

    grad_rows = lax.dynamic_slice_in_dim(out_grad, tensor_at * own_rows, own_rows, axis=1)
    route_rows = lax.dynamic_slice_in_dim(routes, tensor_at * own_rows, own_rows, axis=1)
    mask_rows = jnp.sum(
        (route_rows[..., None] == jnp.arange(experts, dtype=jnp.int32)).astype(f32), axis=2
    )
    upstream = jnp.concatenate(
        [grad_rows, jnp.pad(mask_rows, ((0, 0), (0, 0), (0, 128 - experts))).astype(bf16)], axis=2
    )
    upstream = upstream.reshape(micro_count * own_rows, width + 128)
    upstream_gathered = lax.all_gather(upstream, ("expert", "tensor"), axis=0, tiled=True)

    tokens_here = by_partner(tokens)
    flat_tokens = tokens_here.reshape(flat_rows, width)
    norm_in, query_raw, key_raw, value_low, squares = project(
        flat_tokens, norm1_gain, w_query, w_key, w_value
    )
    gains = [query_gain.reshape(1, local_width), key_gain.reshape(1, local_width)]
    head_shape = (micro_count, rows_here, heads_here, head_size)

    def from_partners(operand):
        return [swap(operand, "tensor", place) for place in tensor_order[1:]]

    packed, scales = turn_and_pack(
        query_raw,
        key_raw,
        value_low,
        gains,
        cosine,
        sine,
        squares,
        from_partners(squares),
        own_rows,
        width,
        pairs,
    )
    packed = pairs_to_heads(packed)
    head_parts = []
    for number in range(per_device):
        parts = [
            packed[number, :, part * head_size : (part + 1) * head_size] for part in range(3)
        ]
        head_parts.append((parts, attention_forward(*parts, causal, score_scale)))
    attended = from_heads(jnp.stack([out for _, (out, _) in head_parts]))
    attended = attended.reshape(flat_rows, local_width)

    attn_part = mm(attended, w_output).astype(bf16).reshape(micro_count, rows_here, width)
    halves = jnp.split(attn_part, 2, axis=1)
    attn_half = add(halves[0], swap(halves[1], *tensor_steps[-1]))
    attn_rows = halve_rows(attn_half.astype(bf16), tensor_steps[:-1][::-1], 1, f32)
    own_source = tokens_here[:, :own_rows].astype(f32)
    residual = (own_source + attn_rows).reshape(micro_count * own_rows, width)
    norm_out = (residual * rms_scale(residual) * norm2_gain).astype(bf16)

    expert_base = jnp.reshape(expert_at * owned, (1,)).astype(jnp.int32)
    table = []
    for call in range(2):
        for copy_place in partner_order(tensor_bits[1:]):
            for last in range(2):
                for place in range(far):
                    owner = 2 * place + (expert_at % 2 ^ last)
                    table.append(
                        owner * tensor_count + (tensor_at ^ (copy_place ^ (call * side)))
                    )
    table = jnp.stack(table).astype(jnp.int32)
    upstream_made = []

    def upstream_work(call, token):
        def work():
            upstream_made.append(
                upstream_products(
                    call,
                    2,
                    table,
                    upstream_gathered,
                    w_down,
                    [upstream_made[-1][2]] if upstream_made else [],
                    [token],
                )
            )
            return upstream_made[-1][:1]

        return work

    block = gather_far(norm_out, upstream_work(0, norm_out))
    by_near, by_side = gather_sides(block, upstream_work(1, block))
    gathered = gather_rest(block, by_near, by_side)
    upstream_all = upstream_made[-1][2]
    total_rows = micro_count * groups * rows_here
    kept = []

    def expert_rows(call):
        nonlocal kept
        copies = gathered[call]
        rows = sum(piece.shape[0] for piece in copies[0])
        count = min(copy_count, max(1, expert_rows_most // rows))
        all_parts = []
        for part in range(copy_count // count):
            parts, kept = expert_call(
                call * (copy_count // count) + part,
                total_rows,
                part,
                expert_base,
                copies[part * count : (part + 1) * count],
                rows // 2,
                upstream_made[call][1],
                w_router,
                w_gate,
                w_up,
                upstream_made[call][0],
                kept,
            )
            all_parts += parts
        return all_parts

    made = {}

    def down_work(call):
        def work(token):
            made[call] = down_products(call, 2, copy_count, kept[1], w_down, [token])
            return list(made[call][:1])

        return work

    def grad_work(name, left, right, *others):
        def work(token):
            tokens = token if isinstance(token, list) else [token]
            made[name] = expert_grads(left, right, owned, tokens)
            return [made[name], *others]

        return work

    attended_gathered = near_gather(after(attended, gathered[1][0][-1]))
    first = expert_rows(0)
    norm_in_gathered = near_exchange(after(norm_in, first[0]))
    first = reduce_copies(first)
    second = expert_rows(1)
    second = reduce_copies([after(second[0], norm_in_gathered)] + second[1:])
    near_part, side_part = side_parts(first, second, *reduce_diagonal(second, down_work(0)))
    arrived = reduce_sides(
        near_part,
        side_part,
        lambda token: down_work(1)(token) + grad_work("down", kept[1], upstream_all)(token),
    )
    out_first, out_second = (reduce_copies(made[call]) for call in range(2))
    out_diagonal = reduce_diagonal(out_second)
    row_parts = reduce_far(
        far_block(first, *arrived),
        lambda token: grad_work("gate", kept[0], kept[2])([token, out_first, out_second]),
    )
    residual_grad, residual_low, router_part, second_gain_part = rows_back(
        row_parts,
        residual,
        norm_out,
        upstream[:, width:],
        w_router,
        norm2_gain,
        grad_rows.reshape(micro_count * own_rows, width),
    )
    out_sides = reduce_sides(
        *side_parts(out_first, out_second, *after_all(out_diagonal, residual_low))
    )
    residual_grad, residual_low = (
        item.reshape(micro_count, own_rows, width) for item in (residual_grad, residual_low)
    )
    residual_low = jnp.concatenate(
        [residual_low, swap(residual_low, *tensor_steps[0])], axis=1
    )
    residual_low = double_rows(residual_low, tensor_steps[1:], 1).reshape(flat_rows, width)

    attended_grad = mm_t(residual_low, w_output).astype(bf16).reshape(head_shape)
    attended_grad = to_heads(attended_grad, grad_work("up", kept[0], kept[3], *out_sides))
    head_grads = []
    for number in range(per_device):
        parts, (_, log_total) = head_parts[number]
        grads = attention_backward(*parts, log_total, attended_grad[number], causal, score_scale)
        head_grads.append(jnp.concatenate(grads, axis=1))
    residual_gathered = near_exchange(after(residual_low, attended_grad))
    head_grads = after(jnp.stack(head_grads), residual_gathered)
    out_block = far_block(out_first, *after_all(out_sides, attended_grad))
    packed_grad = pairs_from_heads(head_grads)
    out_parts = reduce_far(after(out_block, packed_grad))
    normed_q_grad, normed_k_grad, value_grad_low, row_dots, gain_parts = unturn(
        packed_grad, query_raw, key_raw, gains, cosine, sine, scales
    )
    value_arrived = near_swaps(value_grad_low)
    query_grad_low, key_grad_low = norm_back(
        normed_q_grad,
        normed_k_grad,
        query_raw,
        key_raw,
        gains,
        scales,
        row_dots,
        [after(dots, out_parts) for dots in from_partners(row_dots)],
        own_rows,
        width,
    )
    query_arrived = near_swaps(query_grad_low)
    norm_in_there = after(norm_in_gathered, query_grad_low)
    norm_in_near = jnp.concatenate(
        [near_rows(norm_in_there, place) for place in range(near_count)], axis=0
    )

    def near_product(own, arrived, *others):
        right = jnp.concatenate([own] + after_all(arrived, *others), axis=0)
        return t_mm(norm_in_near, right).astype(bf16)

    value_product = near_product(value_grad_low, value_arrived, query_grad_low)
    query_arrived = after_all(query_arrived, value_product)
    key_arrived = near_swaps(after(key_grad_low, *query_arrived))
    query_product = near_product(query_grad_low, query_arrived)
    key_arrived = after_all(key_arrived, query_product)
    key_product = near_product(key_grad_low, key_arrived)
    grad_value, grad_query = (halve_product(item) for item in (value_product, query_product))
    grad_key = halve_product(key_product)
    output_product = t_mm(residual_gathered, after(attended_gathered, query_grad_low))
    grad_output = halve_product(output_product.astype(bf16)).T
    out_rows = far_sum(after(out_parts, query_product))
    layer_out = (residual + out_rows).astype(bf16)
    layer_out = layer_out.reshape(micro_count, own_rows, tensor_count, -1).transpose(2, 0, 1, 3)
    layer_out = lax.all_to_all(layer_out, "tensor", split_axis=0, concat_axis=0, tiled=True)
    layer_out = layer_out.transpose(1, 0, 2, 3).reshape(micro_count, rows_here, -1)

    column_block = width // groups

    def reduce_small(rows):
        rows = jnp.pad(rows, ((0, -rows.shape[0] % 16), (0, 0))).astype(bf16)
        rows = rows.reshape(-1, groups, column_block).transpose(1, 0, 2)
        rows = lax.all_to_all(rows, "expert", split_axis=0, concat_axis=0, tiled=True)
        rows = jnp.sum(rows.astype(f32), axis=0).astype(bf16)
        return sum_over(rows, tensor_steps).astype(f32)

    head_block = head_size // groups
    head_gains = gain_parts[:2].reshape(2 * heads_here, groups, head_block)
    head_gains = head_gains.transpose(1, 0, 2).reshape(groups, 2 * heads_here * head_block)
    head_gains = jnp.pad(head_gains, ((0, 0), (0, column_block - head_gains.shape[1])))
    head_rows = jnp.where(
        jnp.arange(tensor_count, dtype=jnp.int32)[:, None] == tensor_at,
        head_gains.reshape(1, width),
        0.0,
    )
    small = reduce_small(
        after(jnp.concatenate([router_part, second_gain_part, head_rows], axis=0), query_product)
    )
    grad_router = small[:experts].T
    own_heads = lax.dynamic_slice_in_dim(small, experts + 1 + tensor_at, 1, axis=0)
    own_heads = own_heads[0, : 2 * heads_here * head_block].reshape(2, heads_here, head_block)

    scale_in = rms_scale(tokens_here.astype(f32))
    norm_in_part, first_gain_part = project_back(
        after(query_grad_low, query_product),
        key_grad_low,
        value_grad_low,
        flat_tokens,
        scale_in.reshape(flat_rows, 1),
        w_query,
        w_key,
        w_value,
    )
    norm_in_grad = halve_rows(
        norm_in_part.reshape(micro_count, rows_here, width),
        tensor_steps[::-1],
        1,
        f32,
    )
    own_scale = scale_in[:, :own_rows]
    weighted_in = norm_in_grad * norm1_gain
    tokens_grad = (
        residual_grad
        + own_scale * weighted_in
        - own_source * own_scale**3 * jnp.mean(weighted_in * own_source, axis=2, keepdims=True)
    )
    tokens_grad = in_sequence(double_rows(tokens_grad.astype(bf16), tensor_steps, 1)).astype(f32)

    first_gain = reduce_small(first_gain_part)
    return (
        layer_out,
        tokens_grad,
        first_gain[0],
        grad_query,
        grad_key,
        grad_value,
        own_heads[0],
        own_heads[1],
        grad_output,
        small[experts],
        grad_router,
        made["gate"],
        made["up"],
        made["down"],
    )


def solution(mesh):
    placed = (
        P(None, "expert", None),
        P(None, "expert", None),
        P(None, "expert", None),
        P(),
        P(None, "tensor"),
        P(None, "tensor"),
        P(None, "tensor"),
        P("tensor", None),
        P("tensor", None),
        P("tensor", None),
        P(),
        P(),
        P("expert", None, "tensor"),
        P("expert", None, "tensor"),
        P("expert", "tensor", None),
    )
    return jax.shard_map(
        shards,
        mesh=mesh,
        in_specs=placed,
        out_specs=(
            P(None, "expert", "tensor"),
            P(None, "expert", None),
            P("expert"),
            P("expert", "tensor"),
            P("expert", "tensor"),
            P("expert", "tensor"),
            P("tensor", "expert"),
            P("tensor", "expert"),
            P("tensor", "expert"),
            P("expert"),
            P("expert", None),
            P("expert", None, "tensor"),
            P("expert", None, "tensor"),
            P("expert", "tensor", None),
        ),
        check_vma=False,
    )
```

time: 773 us -> 617 us (0.80)
  Pallas kernels: 0 us -> 182 us
  matrix products: 176 us -> 23.4 us
  waiting for transfers between devices: 295 us -> 149 us
  local copies, waits for them, and re-layouts: 102 us -> 58.5 us
  blocking collectives: 0 us -> 20.4 us
  starting transfers between devices: 112 us -> 96.4 us
  between operations: 6.35 us -> 18.1 us
  other arithmetic: 70.8 us -> 60.1 us
    ppermute x86 -> x52, waiting for transfers between devices: 285 us -> 52.5 us  [swap(): lax.ppermute(operand, axis_name, [(i, i ^ bit) for i in range(count)])]
    pallas_call x0 -> x52, Pallas kernels: none -> 182 us  [the longest x2 66.9 us: expert_call(): pl.pallas_call(functools.partial(expert_kernel, plan, copy_count, width),...]
    dot_general x18 -> x0, matrix products: 141 us -> none  [the longest x2 25.1 us: shards(): jnp.einsum('td,efd->tef', upstream_all[m], w_down, preferred_element_type...]
    all_to_all x5 -> x11, waiting for transfers between devices: 9.94 us -> 90 us  [the longest x2 32.8 us: pairs_to_heads(): lax.all_to_all(blocks, 'expert', split_axis=0, concat_axis=0, tiled=True)]
    ppermute x86 -> x52, starting transfers between devices: 90.2 us -> 52.4 us  [swap(): lax.ppermute(operand, axis_name, [(i, i ^ bit) for i in range(count)])]
    unnamed x263 -> x128, local copies, waits for them, and re-layouts: 51.5 us -> 23.6 us
    all_to_all x5 -> x11, starting transfers between devices: 22.3 us -> 44 us  [the longest x3 11.6 us: far_exchange(): lax.all_to_all(blocks, 'expert', split_axis=0, concat_axis=0, axis_index_...]
    all_to_all x0 -> x1, blocking collectives: none -> 20.4 us  [pairs_from_heads(): lax.all_to_all(blocks, 'expert', split_axis=0, concat_axis=0, tiled=True)]
  transfers between devices with their start and end apart: 91 -> 65, of which waited for: 42 -> 25; matrix products, arithmetic and copies ran while one was open for 42% -> 19% of each run, Pallas kernels for 0% -> 24%
where the time goes in v2:
time: 617 us; the launch traced here: 608 us
  Pallas kernels  182 us (29%)
  waiting for transfers between devices  149 us (24%)
  starting transfers between devices  96.4 us (16%)
  other arithmetic  60.1 us (10%)
  local copies, waits for them, and re-layouts  58.5 us (9%)
  matrix products  23.4 us (4%)
  blocking collectives  20.4 us (3%)
  between operations  18.1 us (3%)
    pallas_call x2, Pallas kernels, expert_call(): pl.pallas_call(functools.partial(expert_kernel, plan, copy_count, width),...  66.9 us
    ppermute x52, waiting for transfers between devices, swap(): lax.ppermute(operand, axis_name, [(i, i ^ bit) for i in range(count)])  52.5 us
    ppermute x52, starting transfers between devices, swap(): lax.ppermute(operand, axis_name, [(i, i ^ bit) for i in range(count)])  52.4 us
    pallas_call x3, Pallas kernels, expert_grads(): pl.pallas_call(product_kernel, grid=(owned,), out_shape=jax.ShapeDtypeStr...  45.3 us
    all_to_all x2, waiting for transfers between devices, pairs_to_heads(): lax.all_to_all(blocks, 'expert', split_axis=0, concat_axis=0, tiled=True)  32.8 us
    pallas_call x2, Pallas kernels, upstream_products(): pl.pallas_call(functools.partial(upstream_kernel, place, blocks, width),...  24.1 us
    unnamed x128, local copies, waits for them, and re-layouts  23.6 us
    all_to_all x1, blocking collectives, pairs_from_heads(): lax.all_to_all(blocks, 'expert', split_axis=0, concat_axis=0, tiled=True)  20.4 us
  transfers between devices with their start and end apart: 65, of which 25 were waited for; matrix products, arithmetic and copies ran while one was open for 19% of the time, Pallas kernels for 24%

profile of v2, /device:TPU:0, one launch (start us, length us, event | category | flops | bytes accessed | tf_op | source)
XLA Modules:
  0.0 608.1 jit_solution(14485218759571836776)
XLA Ops:
  13.3 5.8 shard_map.263
  29.5 5.7 all-to-all-start
  35.3 32.8 %all-to-all-done = bf16[8,128,384]{2,1,0:T(8,128)(2,1)} async-done(((bf16[8,128,384]{2,1,0:T(8,128)(2,1)}), bf16[8,128,384]{2,1,0:T(8,128)(2,1)}, u32[]{:S(2)}, u32[]{:S(2)}) %all-to-all-start) | async-done | bytes 786464 | tf_op jit(solution)/shard_map/all_to_all | solution.py:810
  73.7 20.4 %all_to_all.60 = bf16[8,128,128]{2,1,0:T(8,128)(2,1)S(1)} all-to-all(bf16[8,128,128]{2,1,0:T(8,128)(2,1)S(1)} %bitcast.196), channel_id=1, replica_groups=mesh['expert'=8,'tensor'=4] {'expert'}, dimensions={0} | all-to-all | bytes 524288 | tf_op jit(solution)/shard_map/all_to_all | solution.py:820
  98.2 7.6 %collective-permute-done.4 = bf16[2,32,2048]{2,1,0:T(8,128)(2,1)S(1)} collective-permute-done((bf16[2,32,2048]{2,1,0:T(8,128)(2,1)S(1)}, bf16[2,32,2048]{2,1,0:T(8,128)(2,1)S(1)}, u32[]{:S(2)}, u32[]{:S(2)}) %collective-permute-start.4) | collective-permute-done | bytes 262176 | tf_op jit(solution)/shard_map/ppermute | solution.py:51
  112.0 12.0 %shard_map.265 = (f32[1024,1024]{1,0:T(8,128)}, bf16[1024,128]{1,0:T(8,128)(2,1)}, bf16[2048,2048]{1,0:T(8,128)(2,1)}) custom-call(s32[32]{0:T(128)} %stack.164.table_ref, bf16[4,256,2048]{2,1,0:T(8,128)(2,1)} %down_ref.7, bf16[2048,2176]{1,0:T(8,128)(2,1)} %all-gather.3.cloned.1.call-done.gathered_ref, bf16[64,2048]{1,0:T(8,128)(2,1)} %copy-done.34), custom_call_target="tpu_custom_call" | custom-call | flops 4294967296 | bytes 16777216 | tf_op jit(solution)/shard_map/pallas_call | solution.py:149
  124.1 12.7 %all-to-all-done.2.refs_0_ = bf16[4,64,2048]{2,1,0:T(8,128)(2,1)S(1)} async-done(((bf16[4,64,2048]{2,1,0:T(8,128)(2,1)}), bf16[4,64,2048]{2,1,0:T(8,128)(2,1)S(1)}, u32[]{:S(2)}, u32[]{:S(2)}) %all-to-all-start.2) | async-done | bytes 1048608 | tf_op jit(solution)/shard_map/all_to_all | solution.py:853
  140.1 12.0 %shard_map.267 = (f32[1024,1024]{1,0:T(8,128)}, bf16[1024,128]{1,0:T(8,128)(2,1)}, bf16[2048,2048]{1,0:T(8,128)(2,1)}) custom-call(s32[32]{0:T(128)} %stack.164.table_ref, bf16[4,256,2048]{2,1,0:T(8,128)(2,1)} %down_ref.7, bf16[2048,2176]{1,0:T(8,128)(2,1)} %all-gather.3.cloned.1.call-done.gathered_ref, ...), custom_call_target="tpu_custom_call", output_to_operand_aliasing={{2}: (3, {})} | custom-call | flops 4294967296 | bytes 16777216 | tf_op jit(solution)/shard_map/pallas_call | solution.py:149
  152.1 10.1 %collective-permute-done.7.refs_0_ = bf16[256,2048]{1,0:T(8,128)(2,1)} collective-permute-done((bf16[256,2048]{1,0:T(8,128)(2,1)}, bf16[256,2048]{1,0:T(8,128)(2,1)}, u32[]{:S(2)}, u32[]{:S(2)}) %collective-permute-start.7) | collective-permute-done | bytes 1048608 | tf_op jit(solution)/shard_map/ppermute | solution.py:51
  169.5 9.3 %collective-permute-done.8.refs_2_.refs_1_ = bf16[128,2048]{1,0:T(8,128)(2,1)} collective-permute-done((bf16[128,2048]{1,0:T(8,128)(2,1)}, bf16[128,2048]{1,0:T(8,128)(2,1)}, u32[]{:S(2)}, u32[]{:S(2)}) %collective-permute-start.8) | collective-permute-done | bytes 524320 | tf_op jit(solution)/shard_map/ppermute | solution.py:51
  181.2 33.6 %shard_map.270 = (bf16[512,2176]{1,0:T(8,128)(2,1)}, bf16[512,2176]{1,0:T(8,128)(2,1)}, bf16[2048,2048]{1,0:T(8,128)(2,1)}, bf16[2048,1024]{1,0:T(8,128)(2,1)}, ...) custom-call(s32[1]{0:T(128)} %bitcast.13.base_ref, bf16[1024,128]{1,0:T(8,128)(2,1)} %get-tuple-element.65.mask_ref, ...), custom_call_target="tpu_custom_call" | custom-call | flops 17179869184 | bytes 25165824 | tf_op jit(solution)/shard_map/pallas_call | solution.py:331
  216.1 33.3 %shard_map.271 = (bf16[512,2176]{1,0:T(8,128)(2,1)}, bf16[512,2176]{1,0:T(8,128)(2,1)}, bf16[2048,2048]{1,0:T(8,128)(2,1)}, bf16[2048,1024]{1,0:T(8,128)(2,1)}, ...) custom-call(s32[1]{0:T(128)} %bitcast.13.base_ref, ...), custom_call_target="tpu_custom_call", output_to_operand_aliasing={{2}: (12, {}), {3}: (13, {}), {4}: (14, {}), {5}: (15, {})} | custom-call | flops 17179869184 | bytes 25165824 | tf_op jit(solution)/shard_map/pallas_call | solution.py:331
  257.7 12.6 %all-to-all-done.3 = bf16[4,256,512]{2,1,0:T(8,128)(2,1)S(1)} async-done(((bf16[4,256,512]{2,1,0:T(8,128)(2,1)}), bf16[4,256,512]{2,1,0:T(8,128)(2,1)S(1)}, u32[]{:S(2)}, u32[]{:S(2)}) %all-to-all-start.3) | async-done | bytes 1048608 | tf_op jit(solution)/shard_map/all_to_all | solution.py:965
  276.9 9.8 %shard_map.274 = (bf16[512,2048]{1,0:T(8,128)(2,1)}, bf16[512,2048]{1,0:T(8,128)(2,1)}) custom-call(bf16[2048,1024]{1,0:T(8,128)(2,1)} %get-tuple-element.70.gated_ref.left_ref, bf16[4,256,2048]{2,1,0:T(8,128)(2,1)} %down_ref.7, bf16[128,2176]{1,0:T(8,128)(2,1)} %get-tuple-element.178.refs_0_), custom_call_target="tpu_custom_call" | custom-call | flops 4294967296 | bytes 8388608 | tf_op jit(solution)/shard_map/pallas_call | solution.py:377
  291.4 10.4 %collective-permute-done.17.refs_0_ = bf16[128,2176]{1,0:T(8,128)(2,1)S(1)} collective-permute-done((bf16[128,2176]{1,0:T(8,128)(2,1)S(1)}, bf16[128,2176]{1,0:T(8,128)(2,1)S(1)}, u32[]{:S(2)}, u32[]{:S(2)}) %collective-permute-start.17) | collective-permute-done | bytes 557088 | tf_op jit(solution)/shard_map/ppermute | solution.py:51
  310.4 9.6 %shard_map.276 = (bf16[512,2048]{1,0:T(8,128)(2,1)}, bf16[512,2048]{1,0:T(8,128)(2,1)}) custom-call(bf16[2048,1024]{1,0:T(8,128)(2,1)} %get-tuple-element.70.gated_ref.left_ref, bf16[4,256,2048]{2,1,0:T(8,128)(2,1)} %down_ref.7, bf16[256,2176]{1,0:T(8,128)(2,1)} %pad_maximum_fusion.refs_0_), custom_call_target="tpu_custom_call" | custom-call | flops 4294967296 | bytes 8388608 | tf_op jit(solution)/shard_map/pallas_call | solution.py:377
  320.0 14.6 %shard_map.277.refs_2_ = f32[4,256,2048]{2,1,0:T(8,128)} custom-call(bf16[2048,1024]{1,0:T(8,128)(2,1)} %get-tuple-element.70.gated_ref.left_ref, bf16[2048,2048]{1,0:T(8,128)(2,1)} %get-tuple-element.80.right_ref, bf16[256,2176]{1,0:T(8,128)(2,1)} %pad_maximum_fusion.refs_0_), custom_call_target="tpu_custom_call" | custom-call | flops 8589934592 | bytes 25165824 | tf_op jit(solution)/shard_map/pallas_call | solution.py:414
  353.9 15.3 %shard_map.281.refs_1_ = f32[4,2048,256]{2,1,0:T(8,128)} custom-call(bf16[2048,2048]{1,0:T(8,128)(2,1)} %get-tuple-element.81.left_ref, bf16[2048,1024]{1,0:T(8,128)(2,1)} %get-tuple-element.82.right_ref, bf16[256,2176]{1,0:T(8,128)(2,1)} %add_convert_fusion.4.refs_0_, bf16[512,2048]{1,0:T(8,128)(2,1)} %copy-done.17, bf16[512,2048]{1,0:T(8,128)(2,1)} %copy-done.16), custom_call_target="tpu_custom_call" | custom-call | flops 8589934592 | bytes 25165824 | tf_op jit(solution)/shard_map/pallas_call | solution.py:414
  395.9 15.4 %shard_map.285.refs_1_ = f32[4,2048,256]{2,1,0:T(8,128)} custom-call(bf16[2048,2048]{1,0:T(8,128)(2,1)} %get-tuple-element.81.left_ref, bf16[2048,1024]{1,0:T(8,128)(2,1)} %get-tuple-element.84.right_ref, bf16[8,128,128]{2,1,0:T(8,128)(2,1)} %bitcast.194), custom_call_target="tpu_custom_call" | custom-call | flops 8589934592 | bytes 25165824 | tf_op jit(solution)/shard_map/pallas_call | solution.py:414
  441.6 16.7 %all-to-all-done.7.refs_1_.packed_ref = bf16[8,128,384]{2,1,0:T(8,128)(2,1)S(1)} async-done(((bf16[8,128,384]{2,1,0:T(8,128)(2,1)}), bf16[8,128,384]{2,1,0:T(8,128)(2,1)S(1)}, u32[]{:S(2)}, u32[]{:S(2)}) %all-to-all-start.7) | async-done | bytes 786464 | tf_op jit(solution)/shard_map/all_to_all | solution.py:820
  482.0 4.7 all-to-all-done.8.refs_1_.refs_0_
  494.3 5.0 collective-permute-start.35
  499.3 6.4 %all-gather.5.cloned.1.call-done.refs_0_ = bf16[1024,512]{1,0:T(8,128)(2,1)} async-done(((bf16[256,512]{1,0:T(8,128)(2,1)}), bf16[1024,512]{1,0:T(8,128)(2,1)}) %all-gather.5.cloned.1.call-update) | async-done | bytes 1048592 | tf_op jit(solution)/shard_map/all_gather | solution.py:976
  526.1 6.2 %shard_map.307 = (bf16[256,2048]{1,0:T(8,128)(2,1)}, f32[1,2048]{1,0:T(1,128)}) custom-call(bf16[256,512]{1,0:T(8,128)(2,1)} %shard_map.306.q_ref, bf16[256,512]{1,0:T(8,128)(2,1)} %get-tuple-element.92.k_ref, bf16[256,512]{1,0:T(8,128)(2,1)} %get-tuple-element.90.v_ref, bf16[256,2048]{1,0:T(8,128)(2,1)} %bitcast.174, f32[256,1]{1,0:T(8,128)} %copy.136.scale_ref, ...), custom_call_target="tpu_custom_call" | custom-call | tf_op jit(solution)/shard_map/pallas_call | solution.py:645
  (422 shorter events, 267.9 us)
Async XLA Ops:
  7.2 104.8 %all-gather.3.cloned.1.call-start = ((), (), s32[]{:S(2)}) async-start(), calls=%async_computation.12 | async-start | bytes 9191424 | tf_op jit(solution)/shard_map/all_gather | solution.py:1000
  29.5 38.6 %all-to-all-start = ((bf16[8,128,384]{2,1,0:T(8,128)(2,1)}), bf16[8,128,384]{2,1,0:T(8,128)(2,1)}, u32[]{:S(2)}, u32[]{:S(2)}) async-start(bf16[8,128,384]{2,1,0:T(8,128)(2,1)} %get-tuple-element.60), calls=%async_computation | async-start | bytes 1572864 | tf_op jit(solution)/shard_map/all_to_all | solution.py:810
  107.3 29.5 %all-to-all-start.2 = ((bf16[4,64,2048]{2,1,0:T(8,128)(2,1)}), bf16[4,64,2048]{2,1,0:T(8,128)(2,1)S(1)}, u32[]{:S(2)}, u32[]{:S(2)}) async-start(bf16[4,64,2048]{2,1,0:T(8,128)(2,1)} %broadcast_in_dim.35), calls=%async_computation.2 | async-start | bytes 2097152 | tf_op jit(solution)/shard_map/all_to_all | solution.py:853
  140.1 41.1 %collective-permute-start.12 = (bf16[256,2048]{1,0:T(8,128)(2,1)}, bf16[256,2048]{1,0:T(8,128)(2,1)}, u32[]{:S(2)}, u32[]{:S(2)}) collective-permute-start(bf16[256,2048]{1,0:T(8,128)(2,1)} %bitcast.167), channel_id=1, source_target_pairs={{0,1},{1,0},{2,3},{3,2},{4,5},{5,4},{6,7},{7,6},{8,9},{9,8},{10,11... | collective-permute-start | bytes 3145736 | tf_op jit(solution)/shard_map/ppermute | solution.py:51
  169.5 45.3 %collective-permute-start.9 = (bf16[256,2048]{1,0:T(8,128)(2,1)}, bf16[256,2048]{1,0:T(8,128)(2,1)S(1)}, u32[]{:S(2)}, u32[]{:S(2)}) collective-permute-start(bf16[256,2048]{1,0:T(8,128)(2,1)} %shard_map.268.refs_0_), channel_id=1, source_target_pairs={{0,1},{1,0},{2,3},{3,2},{4,5},{5,4},{6,7},{7,6},{8,9},{9,8},{10,11... | collective-permute-start | bytes 3145736 | tf_op jit(solution)/shard_map/ppermute | solution.py:51
  178.8 36.0 %collective-permute-start.11 = (bf16[128,2048]{1,0:T(8,128)(2,1)}, bf16[128,2048]{1,0:T(8,128)(2,1)S(1)}, u32[]{:S(2)}, u32[]{:S(2)}) collective-permute-start(bf16[128,2048]{1,0:T(8,128)(2,1)} %collective-permute-done.8.refs_2_.refs_1_), channel_id=1, source_target_pairs={{0,1},{1,0},{2,3},{3,2},{4,5},{5,4},{6,7},{7,6},{8,9},{9,8},{10,11... | collective-permute-start | bytes 1572872 | tf_op jit(solution)/shard_map/ppermute | solution.py:51
  181.1 33.7 %collective-permute-start.10 = (bf16[128,2048]{1,0:T(8,128)(2,1)S(1)}, bf16[128,2048]{1,0:T(8,128)(2,1)S(1)}, u32[]{:S(2)}, u32[]{:S(2)}) collective-permute-start(bf16[128,2048]{1,0:T(8,128)(2,1)S(1)} %collective-permute-done.6.refs_1_), channel_id=1, source_target_pairs={{0,1},{1,0},{2,3},{3,2},{4,5},{5,4},{6,7},{7,6},{8,9},{9,8},{10,11... | collective-permute-start | bytes 1572872 | tf_op jit(solution)/shard_map/ppermute | solution.py:51
  256.1 31.8 %collective-permute-start.16 = (bf16[512,2176]{1,0:T(8,128)(2,1)}, bf16[512,2176]{1,0:T(8,128)(2,1)}, u32[]{:S(2)}, u32[]{:S(2)}) collective-permute-start(bf16[512,2176]{1,0:T(8,128)(2,1)} %get-tuple-element.77), channel_id=1, source_target_pairs={{0,1},{1,0},{2,3},{3,2},{4,5},{5,4},{6,7},{7,6},{8,9},{9,8},{10,11... | collective-permute-start | bytes 6684680 | tf_op jit(solution)/shard_map/ppermute | solution.py:51
  275.5 30.3 %collective-permute-start.21 = (bf16[128,2176]{1,0:T(8,128)(2,1)}, bf16[128,2176]{1,0:T(8,128)(2,1)}, u32[]{:S(2)}, u32[]{:S(2)}) collective-permute-start(bf16[128,2176]{1,0:T(8,128)(2,1)} %get-tuple-element.178.refs_0_), channel_id=1, source_target_pairs={{0,4},{4,0},{8,12},{12,8},{16,20},{20,16},{24,28},{28,24},{1,5},{5... | collective-permute-start | bytes 1671176 | tf_op jit(solution)/shard_map/ppermute | solution.py:51
  286.7 57.0 %collective-permute-start.15 = (bf16[512,2048]{1,0:T(8,128)(2,1)}, bf16[512,2048]{1,0:T(8,128)(2,1)}, u32[]{:S(2)}, u32[]{:S(2)}) collective-permute-start(bf16[512,2048]{1,0:T(8,128)(2,1)} %get-tuple-element.76), channel_id=1, source_target_pairs={{0,1},{1,0},{2,3},{3,2},{4,5},{5,4},{6,7},{7,6},{8,9},{9,8},{10,11... | collective-permute-start | bytes 6291464 | tf_op jit(solution)/shard_map/ppermute | solution.py:51
  305.2 29.4 %collective-permute-start.20 = (bf16[256,2176]{1,0:T(8,128)(2,1)}, bf16[256,2176]{1,0:T(8,128)(2,1)S(1)}, u32[]{:S(2)}, u32[]{:S(2)}) collective-permute-start(bf16[256,2176]{1,0:T(8,128)(2,1)} %pad_maximum_fusion.refs_0_), channel_id=1, source_target_pairs={{0,4},{4,0},{8,12},{12,8},{16,20},{20,16},{24,28},{28,24},{1,5},{5... | collective-permute-start | bytes 3342344 | tf_op jit(solution)/shard_map/ppermute | solution.py:51
  320.0 27.0 %collective-permute-start.18 = (bf16[512,2048]{1,0:T(8,128)(2,1)}, bf16[512,2048]{1,0:T(8,128)(2,1)}, u32[]{:S(2)}, u32[]{:S(2)}) collective-permute-start(bf16[512,2048]{1,0:T(8,128)(2,1)} %get-tuple-element.79), channel_id=1, source_target_pairs={{0,1},{1,0},{2,3},{3,2},{4,5},{5,4},{6,7},{7,6},{8,9},{9,8},{10,11... | collective-permute-start | bytes 6291464 | tf_op jit(solution)/shard_map/ppermute | solution.py:51
  339.8 32.0 %all-to-all-start.4 = ((bf16[4,64,2176]{2,1,0:T(8,128)(2,1)}), bf16[4,64,2176]{2,1,0:T(8,128)(2,1)S(1)}, u32[]{:S(2)}, u32[]{:S(2)}) async-start(bf16[4,64,2176]{2,1,0:T(8,128)(2,1)} %bitcast.177), calls=%async_computation.4 | async-start | bytes 2228224 | tf_op jit(solution)/shard_map/all_to_all | solution.py:853
  352.4 28.8 %collective-permute-start.26 = (bf16[128,2048]{1,0:T(8,128)(2,1)}, bf16[128,2048]{1,0:T(8,128)(2,1)}, u32[]{:S(2)}, u32[]{:S(2)}) collective-permute-start(bf16[128,2048]{1,0:T(8,128)(2,1)} %get-tuple-element.181), channel_id=1, source_target_pairs={{0,4},{4,0},{8,12},{12,8},{16,20},{20,16},{24,28},{28,24},{1,5},{5... | collective-permute-start | bytes 1572872 | tf_op jit(solution)/shard_map/ppermute | solution.py:51
  379.8 31.5 %collective-permute-start.23 = (bf16[256,2048]{1,0:T(8,128)(2,1)}, bf16[256,2048]{1,0:T(8,128)(2,1)}, u32[]{:S(2)}, u32[]{:S(2)}) collective-permute-start(bf16[256,2048]{1,0:T(8,128)(2,1)} %pad_maximum_fusion.4), channel_id=1, source_target_pairs={{0,4},{4,0},{8,12},{12,8},{16,20},{20,16},{24,28},{28,24},{1,5},{5... | collective-permute-start | bytes 3145736 | tf_op jit(solution)/shard_map/ppermute | solution.py:51
  459.2 27.5 %all-to-all-start.8 = ((bf16[4,64,2048]{2,1,0:T(8,128)(2,1)}), bf16[4,64,2048]{2,1,0:T(8,128)(2,1)S(1)}, u32[]{:S(2)}, u32[]{:S(2)}) async-start(bf16[4,64,2048]{2,1,0:T(8,128)(2,1)} %bitcast.172), calls=%async_computation.8 | async-start | bytes 2097152 | tf_op jit(solution)/shard_map/all_to_all | solution.py:853
  462.9 42.9 %all-gather.5.cloned.1.call-start = ((), (), s32[]{:S(2)}) async-start(), calls=%async_computation.13 | async-start | bytes 1310720 | tf_op jit(solution)/shard_map/all_gather | solution.py:976
  476.7 31.8 %collective-permute-start.32 = (bf16[256,512]{1,0:T(8,128)(2,1)}, bf16[256,512]{1,0:T(8,128)(2,1)}, u32[]{:S(2)}, u32[]{:S(2)}) collective-permute-start(bf16[256,512]{1,0:T(8,128)(2,1)} %get-tuple-element.90.v_ref), channel_id=1, source_target_pairs={{0,4},{4,0},{8,12},{12,8},{16,20},{20,16},{24,28},{28,24},{1,5},{5... | collective-permute-start | bytes 786440 | tf_op jit(solution)/shard_map/ppermute | solution.py:51
  478.1 33.7 %collective-permute-start.33 = (bf16[256,512]{1,0:T(8,128)(2,1)}, bf16[256,512]{1,0:T(8,128)(2,1)}, u32[]{:S(2)}, u32[]{:S(2)}) collective-permute-start(bf16[256,512]{1,0:T(8,128)(2,1)} %get-tuple-element.90.v_ref), channel_id=1, source_target_pairs={{0,8},{4,12},{8,0},{12,4},{16,24},{20,28},{24,16},{28,20},{1,9},{5... | collective-permute-start | bytes 786440 | tf_op jit(solution)/shard_map/ppermute | solution.py:51
  481.8 32.8 %collective-permute-start.34 = (bf16[256,512]{1,0:T(8,128)(2,1)}, bf16[256,512]{1,0:T(8,128)(2,1)}, u32[]{:S(2)}, u32[]{:S(2)}) collective-permute-start(bf16[256,512]{1,0:T(8,128)(2,1)} %get-tuple-element.90.v_ref), channel_id=1, source_target_pairs={{0,12},{4,8},{8,4},{12,0},{16,28},{20,24},{24,20},{28,16},{1,13},{... | collective-permute-start | bytes 786440 | tf_op jit(solution)/shard_map/ppermute | solution.py:51
  511.8 33.4 %collective-permute-start.51 = (bf16[256,512]{1,0:T(8,128)(2,1)}, bf16[256,512]{1,0:T(8,128)(2,1)}, u32[]{:S(2)}, u32[]{:S(2)}) collective-permute-start(bf16[256,512]{1,0:T(8,128)(2,1)} %slice.205), channel_id=1, source_target_pairs={{0,16},{4,20},{8,24},{12,28},{16,0},{20,4},{24,8},{28,12},{1,17},{... | collective-permute-start | bytes 786440 | tf_op jit(solution)/shard_map/ppermute | solution.py:51
  517.6 35.2 %collective-permute-start.48 = (bf16[256,512]{1,0:T(8,128)(2,1)}, bf16[256,512]{1,0:T(8,128)(2,1)}, u32[]{:S(2)}, u32[]{:S(2)}) collective-permute-start(bf16[256,512]{1,0:T(8,128)(2,1)} %slice.203), channel_id=1, source_target_pairs={{0,16},{4,20},{8,24},{12,28},{16,0},{20,4},{24,8},{28,12},{1,17},{... | collective-permute-start | bytes 786440 | tf_op jit(solution)/shard_map/ppermute | solution.py:51
  523.0 52.8 %collective-permute-start.44 = (bf16[256,512]{1,0:T(8,128)(2,1)}, bf16[256,512]{1,0:T(8,128)(2,1)}, u32[]{:S(2)}, u32[]{:S(2)}) collective-permute-start(bf16[256,512]{1,0:T(8,128)(2,1)} %shard_map.308), channel_id=1, source_target_pairs={{0,4},{4,0},{8,12},{12,8},{16,20},{20,16},{24,28},{28,24},{1,5},{5... | collective-permute-start | bytes 786440 | tf_op jit(solution)/shard_map/ppermute | solution.py:51
  525.1 50.7 %collective-permute-start.45 = (bf16[256,512]{1,0:T(8,128)(2,1)}, bf16[256,512]{1,0:T(8,128)(2,1)}, u32[]{:S(2)}, u32[]{:S(2)}) collective-permute-start(bf16[256,512]{1,0:T(8,128)(2,1)} %shard_map.308), channel_id=1, source_target_pairs={{0,8},{4,12},{8,0},{12,4},{16,24},{20,28},{24,16},{28,20},{1,9},{5... | collective-permute-start | bytes 786440 | tf_op jit(solution)/shard_map/ppermute | solution.py:51
  (104 other events, 1073.6 us)
Sparse Core Ops, SparseCore 0:
  10.9 95.5 all-gather.2
  465.3 40.4 all-gather.4

commit v3 on v2

--- a/solution.py
+++ b/solution.py
@@ -1106,7 +1106,8 @@
 
     def down_work(call):
         def work(token):
-            made[call] = down_products(call, 2, copy_count, kept[1], w_down, [token])
+            tokens = token if isinstance(token, list) else [token]
+            made[call] = down_products(call, 2, copy_count, kept[1], w_down, tokens)
             return list(made[call][:1])
 
         return work
@@ -1119,13 +1120,13 @@
 
         return work
 
-    attended_gathered = near_gather(after(attended, gathered[1][0][-1]))
+    attended_gathered = near_gather(attended)
     first = expert_rows(0)
     norm_in_gathered = near_exchange(after(norm_in, first[0]))
     first = reduce_copies(first)
     second = expert_rows(1)
-    second = reduce_copies([after(second[0], norm_in_gathered)] + second[1:])
-    near_part, side_part = side_parts(first, second, *reduce_diagonal(second, down_work(0)))
+    second = reduce_copies(after_all(second, norm_in_gathered))
+    near_part, side_part = side_parts(first, second, *reduce_diagonal(second, lambda token: down_work(0)([token, first])))
     arrived = reduce_sides(
         near_part,
         side_part,
@@ -1135,10 +1136,10 @@
     out_diagonal = reduce_diagonal(out_second)
     row_parts = reduce_far(
         far_block(first, *arrived),
-        lambda token: grad_work("gate", kept[0], kept[2])([token, out_first, out_second]),
+        lambda token: [out_first, out_second],
     )
     residual_grad, residual_low, router_part, second_gain_part = rows_back(
-        row_parts,
+        after(row_parts, attended_gathered),
         residual,
         norm_out,
         upstream[:, width:],
@@ -1167,7 +1168,9 @@
     residual_gathered = near_exchange(after(residual_low, attended_grad))
     head_grads = after(jnp.stack(head_grads), residual_gathered)
     out_block = far_block(out_first, *after_all(out_sides, attended_grad))
-    packed_grad = pairs_from_heads(head_grads)
+    packed_grad = pairs_from_heads(
+        head_grads, grad_work("gate", kept[0], kept[2])(head_grads)
+    )
     out_parts = reduce_far(after(out_block, packed_grad))
     normed_q_grad, normed_k_grad, value_grad_low, row_dots, gain_parts = unturn(
         packed_grad, query_raw, key_raw, gains, cosine, sine, scales
@@ -1205,7 +1208,35 @@
     grad_key = halve_product(key_product)
     output_product = t_mm(residual_gathered, after(attended_gathered, query_grad_low))
     grad_output = halve_product(output_product.astype(bf16)).T
-    out_rows = far_sum(after(out_parts, query_product))
+
+    scale_in = rms_scale(tokens_here.astype(f32))
+    norm_in_part, first_gain_part = project_back(
+        after(query_grad_low, value_product),
+        key_grad_low,
+        value_grad_low,
+        flat_tokens,
+        scale_in.reshape(flat_rows, 1),
+        w_query,
+        w_key,
+        w_value,
+    )
+    norm_in_grad = halve_rows(
+        norm_in_part.reshape(micro_count, rows_here, width),
+        tensor_steps[::-1],
+        1,
+        f32,
+    )
+    own_scale = scale_in[:, :own_rows]
+    weighted_in = norm_in_grad * norm1_gain
+    tokens_grad = (
+        residual_grad
+        + own_scale * weighted_in
+        - own_source * own_scale**3 * jnp.mean(weighted_in * own_source, axis=2, keepdims=True)
+    )
+    tokens_low = tokens_grad.astype(bf16)
+    tokens_grad = in_sequence(double_rows(tokens_low, tensor_steps, 1)).astype(f32)
+
+    out_rows = far_sum(after(out_parts, tokens_low))
     layer_out = (residual + out_rows).astype(bf16)
     layer_out = layer_out.reshape(micro_count, own_rows, tensor_count, -1).transpose(2, 0, 1, 3)
     layer_out = lax.all_to_all(layer_out, "tensor", split_axis=0, concat_axis=0, tiled=True)
@@ -1230,43 +1261,22 @@
         0.0,
     )
     small = reduce_small(
-        after(jnp.concatenate([router_part, second_gain_part, head_rows], axis=0), query_product)
+        after(
+            jnp.concatenate(
+                [router_part, second_gain_part, first_gain_part, head_rows], axis=0
+            ),
+            tokens_low,
+        )
     )
     grad_router = small[:experts].T
-    own_heads = lax.dynamic_slice_in_dim(small, experts + 1 + tensor_at, 1, axis=0)
+    own_heads = lax.dynamic_slice_in_dim(small, experts + 2 + tensor_at, 1, axis=0)
     own_heads = own_heads[0, : 2 * heads_here * head_block].reshape(2, heads_here, head_block)
 
-    scale_in = rms_scale(tokens_here.astype(f32))
-    norm_in_part, first_gain_part = project_back(
-        after(query_grad_low, query_product),
-        key_grad_low,
-        value_grad_low,
-        flat_tokens,
-        scale_in.reshape(flat_rows, 1),
-        w_query,
-        w_key,
-        w_value,
-    )
-    norm_in_grad = halve_rows(
-        norm_in_part.reshape(micro_count, rows_here, width),
-        tensor_steps[::-1],
-        1,
-        f32,
-    )
-    own_scale = scale_in[:, :own_rows]
-    weighted_in = norm_in_grad * norm1_gain
-    tokens_grad = (
-        residual_grad
-        + own_scale * weighted_in
-        - own_source * own_scale**3 * jnp.mean(weighted_in * own_source, axis=2, keepdims=True)
-    )
-    tokens_grad = in_sequence(double_rows(tokens_grad.astype(bf16), tensor_steps, 1)).astype(f32)
-
-    first_gain = reduce_small(first_gain_part)
+
     return (
         layer_out,
         tokens_grad,
-        first_gain[0],
+        small[experts + 1],
         grad_query,
         grad_key,
         grad_value,

time: 617 us -> 593 us (0.961)
  waiting for transfers between devices: 149 us -> 136 us
  starting transfers between devices: 96.4 us -> 90.2 us
    all_to_all x3, waiting for transfers between devices: 19.9 us -> 37.3 us  [far_exchange(): lax.all_to_all(blocks, 'expert', split_axis=0, concat_axis=0, axis_index_...]
    all_to_all x1, waiting for transfers between devices: 16.7 us -> 1.46 us  [pairs_from_heads(): lax.all_to_all(blocks, 'expert', split_axis=0, concat_axis=0, tiled=True)]
    all_to_all x2, waiting for transfers between devices: 16.5 us -> 3.91 us  [near_exchange(): lax.all_to_all(jnp.stack(parts), 'expert', split_axis=0, concat_axis=0, a...]
    ppermute x52 -> x50, starting transfers between devices: 52.4 us -> 43.6 us  [swap(): lax.ppermute(operand, axis_name, [(i, i ^ bit) for i in range(count)])]
    all_gather x1, waiting for transfers between devices: 6.44 us -> 0.01 us  [near_gather(): lax.all_gather(operand, 'expert', axis_index_groups=near_groups, axis=0,...]
    ppermute x52 -> x50, waiting for transfers between devices: 52.5 us -> 55.6 us  [swap(): lax.ppermute(operand, axis_name, [(i, i ^ bit) for i in range(count)])]
    unnamed x128 -> x134, local copies, waits for them, and re-layouts: 23.6 us -> 22.4 us
  transfers between devices with their start and end apart: 65 -> 62, of which waited for: 25 -> 21; matrix products, arithmetic and copies ran while one was open for 19% -> 19% of each run, Pallas kernels for 24% -> 31%
where the time goes in v3:
time: 593 us; the launch traced here: 584 us
  Pallas kernels  182 us (31%)
  waiting for transfers between devices  136 us (23%)
  starting transfers between devices  90.2 us (15%)
  other arithmetic  57 us (10%)
  local copies, waits for them, and re-layouts  56.6 us (10%)
  matrix products  22.4 us (4%)
  blocking collectives  20.4 us (3%)
  between operations  19.7 us (3%)
    pallas_call x2, Pallas kernels, expert_call(): pl.pallas_call(functools.partial(expert_kernel, plan, copy_count, width),...  66.5 us
    ppermute x50, waiting for transfers between devices, swap(): lax.ppermute(operand, axis_name, [(i, i ^ bit) for i in range(count)])  55.6 us
    pallas_call x3, Pallas kernels, expert_grads(): pl.pallas_call(product_kernel, grid=(owned,), out_shape=jax.ShapeDtypeStr...  45.4 us
    ppermute x50, starting transfers between devices, swap(): lax.ppermute(operand, axis_name, [(i, i ^ bit) for i in range(count)])  43.6 us
    all_to_all x3, waiting for transfers between devices, far_exchange(): lax.all_to_all(blocks, 'expert', split_axis=0, concat_axis=0, axis_index_...  37.3 us
    all_to_all x2, waiting for transfers between devices, pairs_to_heads(): lax.all_to_all(blocks, 'expert', split_axis=0, concat_axis=0, tiled=True)  32.8 us
    pallas_call x2, Pallas kernels, upstream_products(): pl.pallas_call(functools.partial(upstream_kernel, place, blocks, width),...  24.1 us
    unnamed x134, local copies, waits for them, and re-layouts  22.4 us
  transfers between devices with their start and end apart: 62, of which 21 were waited for; matrix products, arithmetic and copies ran while one was open for 19% of the time, Pallas kernels for 31%

profile of v3, /device:TPU:0, one launch (start us, length us, event | category | flops | bytes accessed | tf_op | source)
XLA Modules:
  0.0 584.2 jit_solution(2693975529933608211)
XLA Ops:
  14.1 5.8 shard_map.263
  30.3 5.7 all-to-all-start
  36.1 32.8 %all-to-all-done = bf16[8,128,384]{2,1,0:T(8,128)(2,1)} async-done(((bf16[8,128,384]{2,1,0:T(8,128)(2,1)}), bf16[8,128,384]{2,1,0:T(8,128)(2,1)}, u32[]{:S(2)}, u32[]{:S(2)}) %all-to-all-start) | async-done | bytes 786464 | tf_op jit(solution)/shard_map/all_to_all | solution.py:810
  74.6 20.4 %all_to_all.55 = bf16[8,128,128]{2,1,0:T(8,128)(2,1)S(1)} all-to-all(bf16[8,128,128]{2,1,0:T(8,128)(2,1)S(1)} %bitcast.190), channel_id=1, replica_groups=mesh['expert'=8,'tensor'=4] {'expert'}, dimensions={0} | all-to-all | bytes 524288 | tf_op jit(solution)/shard_map/all_to_all | solution.py:820
  99.0 7.5 %collective-permute-done.4 = bf16[2,32,2048]{2,1,0:T(8,128)(2,1)S(1)} collective-permute-done((bf16[2,32,2048]{2,1,0:T(8,128)(2,1)S(1)}, bf16[2,32,2048]{2,1,0:T(8,128)(2,1)S(1)}, u32[]{:S(2)}, u32[]{:S(2)}) %collective-permute-start.4) | collective-permute-done | bytes 262176 | tf_op jit(solution)/shard_map/ppermute | solution.py:51
  112.6 12.0 %shard_map.265 = (f32[1024,1024]{1,0:T(8,128)}, bf16[1024,128]{1,0:T(8,128)(2,1)}, bf16[2048,2048]{1,0:T(8,128)(2,1)}) custom-call(s32[32]{0:T(128)} %stack.164.table_ref, bf16[4,256,2048]{2,1,0:T(8,128)(2,1)} %down_ref.7, bf16[2048,2176]{1,0:T(8,128)(2,1)} %all-gather.3.cloned.1.call-done.gathered_ref, bf16[64,2048]{1,0:T(8,128)(2,1)} %copy-done.32), custom_call_target="tpu_custom_call" | custom-call | flops 4294967296 | bytes 16777216 | tf_op jit(solution)/shard_map/pallas_call | solution.py:149
  124.6 12.7 %all-to-all-done.2.refs_0_ = bf16[4,64,2048]{2,1,0:T(8,128)(2,1)S(1)} async-done(((bf16[4,64,2048]{2,1,0:T(8,128)(2,1)}), bf16[4,64,2048]{2,1,0:T(8,128)(2,1)S(1)}, u32[]{:S(2)}, u32[]{:S(2)}) %all-to-all-start.2) | async-done | bytes 1048608 | tf_op jit(solution)/shard_map/all_to_all | solution.py:853
  140.6 12.0 %shard_map.267 = (f32[1024,1024]{1,0:T(8,128)}, bf16[1024,128]{1,0:T(8,128)(2,1)}, bf16[2048,2048]{1,0:T(8,128)(2,1)}) custom-call(s32[32]{0:T(128)} %stack.164.table_ref, bf16[4,256,2048]{2,1,0:T(8,128)(2,1)} %down_ref.7, bf16[2048,2176]{1,0:T(8,128)(2,1)} %all-gather.3.cloned.1.call-done.gathered_ref, ...), custom_call_target="tpu_custom_call", output_to_operand_aliasing={{2}: (3, {})} | custom-call | flops 4294967296 | bytes 16777216 | tf_op jit(solution)/shard_map/pallas_call | solution.py:149
  152.7 10.1 %collective-permute-done.7.refs_0_ = bf16[256,2048]{1,0:T(8,128)(2,1)} collective-permute-done((bf16[256,2048]{1,0:T(8,128)(2,1)}, bf16[256,2048]{1,0:T(8,128)(2,1)}, u32[]{:S(2)}, u32[]{:S(2)}) %collective-permute-start.7) | collective-permute-done | bytes 1048608 | tf_op jit(solution)/shard_map/ppermute | solution.py:51
  170.1 9.2 %collective-permute-done.8.refs_2_ = bf16[128,2048]{1,0:T(8,128)(2,1)} collective-permute-done((bf16[128,2048]{1,0:T(8,128)(2,1)}, bf16[128,2048]{1,0:T(8,128)(2,1)}, u32[]{:S(2)}, u32[]{:S(2)}) %collective-permute-start.8) | collective-permute-done | bytes 524320 | tf_op jit(solution)/shard_map/ppermute | solution.py:51
  181.9 33.3 %shard_map.270 = (bf16[512,2176]{1,0:T(8,128)(2,1)}, bf16[512,2176]{1,0:T(8,128)(2,1)}, bf16[2048,2048]{1,0:T(8,128)(2,1)}, bf16[2048,1024]{1,0:T(8,128)(2,1)}, ...) custom-call(s32[1]{0:T(128)} %bitcast.13.base_ref, bf16[1024,128]{1,0:T(8,128)(2,1)} %get-tuple-element.65.mask_ref, ...), custom_call_target="tpu_custom_call" | custom-call | flops 17179869184 | bytes 25165824 | tf_op jit(solution)/shard_map/pallas_call | solution.py:331
  221.8 33.1 %shard_map.271 = (bf16[512,2176]{1,0:T(8,128)(2,1)}, bf16[512,2176]{1,0:T(8,128)(2,1)}, bf16[2048,2048]{1,0:T(8,128)(2,1)}, bf16[2048,1024]{1,0:T(8,128)(2,1)}, ...) custom-call(s32[1]{0:T(128)} %bitcast.13.base_ref, ...), custom_call_target="tpu_custom_call", output_to_operand_aliasing={{2}: (12, {}), {3}: (13, {}), {4}: (14, {}), {5}: (15, {})} | custom-call | flops 17179869184 | bytes 25165824 | tf_op jit(solution)/shard_map/pallas_call | solution.py:331
  270.5 9.7 %shard_map.275 = (bf16[512,2048]{1,0:T(8,128)(2,1)}, bf16[512,2048]{1,0:T(8,128)(2,1)}) custom-call(bf16[2048,1024]{1,0:T(8,128)(2,1)} %get-tuple-element.70.gated_ref.left_ref, bf16[4,256,2048]{2,1,0:T(8,128)(2,1)} %down_ref.7, bf16[128,2176]{1,0:T(8,128)(2,1)} %get-tuple-element.178.refs_0_, bf16[512,2176]{1,0:T(8,128)(2,1)} %copy-done.17), custom_call_target="tpu_custom_call" | custom-call | flops 4294967296 | bytes 8388608 | tf_op jit(solution)/shard_map/pallas_call | solution.py:377
  284.9 9.8 %shard_map.277 = (bf16[512,2048]{1,0:T(8,128)(2,1)}, bf16[512,2048]{1,0:T(8,128)(2,1)}) custom-call(bf16[2048,1024]{1,0:T(8,128)(2,1)} %get-tuple-element.70.gated_ref.left_ref, bf16[4,256,2048]{2,1,0:T(8,128)(2,1)} %down_ref.7, bf16[256,2176]{1,0:T(8,128)(2,1)} %pad_maximum_fusion.refs_0_), custom_call_target="tpu_custom_call" | custom-call | flops 4294967296 | bytes 8388608 | tf_op jit(solution)/shard_map/pallas_call | solution.py:377
  301.8 14.6 %shard_map.278.refs_2_ = f32[4,256,2048]{2,1,0:T(8,128)} custom-call(bf16[2048,1024]{1,0:T(8,128)(2,1)} %get-tuple-element.70.gated_ref.left_ref, bf16[2048,2048]{1,0:T(8,128)(2,1)} %get-tuple-element.80.right_ref, bf16[256,2176]{1,0:T(8,128)(2,1)} %pad_maximum_fusion.refs_0_), custom_call_target="tpu_custom_call" | custom-call | flops 8589934592 | bytes 25165824 | tf_op jit(solution)/shard_map/pallas_call | solution.py:414
  317.4 8.2 %collective-permute-done.22.refs_0_ = bf16[256,2176]{1,0:T(8,128)(2,1)} collective-permute-done((bf16[256,2176]{1,0:T(8,128)(2,1)}, bf16[256,2176]{1,0:T(8,128)(2,1)}, u32[]{:S(2)}, u32[]{:S(2)}) %collective-permute-start.22) | collective-permute-done | bytes 1114144 | tf_op jit(solution)/shard_map/ppermute | solution.py:51
  342.5 16.9 %all-to-all-done.4.refs_0_ = bf16[4,64,2176]{2,1,0:T(8,128)(2,1)S(1)} async-done(((bf16[4,64,2176]{2,1,0:T(8,128)(2,1)}), bf16[4,64,2176]{2,1,0:T(8,128)(2,1)S(1)}, u32[]{:S(2)}, u32[]{:S(2)}) %all-to-all-start.4) | async-done | bytes 1114144 | tf_op jit(solution)/shard_map/all_to_all | solution.py:853
  383.1 15.4 %shard_map.286.refs_1_ = f32[4,2048,256]{2,1,0:T(8,128)} custom-call(bf16[2048,2048]{1,0:T(8,128)(2,1)} %get-tuple-element.82.left_ref, bf16[2048,1024]{1,0:T(8,128)(2,1)} %get-tuple-element.83.right_ref, bf16[8,128,128]{2,1,0:T(8,128)(2,1)} %bitcast.188), custom_call_target="tpu_custom_call" | custom-call | flops 8589934592 | bytes 25165824 | tf_op jit(solution)/shard_map/pallas_call | solution.py:414
  428.7 15.4 %shard_map.293.refs_1_ = f32[4,2048,256]{2,1,0:T(8,128)} custom-call(bf16[2048,2048]{1,0:T(8,128)(2,1)} %get-tuple-element.82.left_ref, bf16[2048,1024]{1,0:T(8,128)(2,1)} %get-tuple-element.84.right_ref, bf16[1,1024,384]{2,1,0:T(8,128)(2,1)} %shard_map.292.refs_0_), custom_call_target="tpu_custom_call" | custom-call | flops 8589934592 | bytes 25165824 | tf_op jit(solution)/shard_map/pallas_call | solution.py:414
  456.8 4.6 shard_map.296
  468.1 7.8 %all-to-all-done.8.refs_1_.refs_0_ = bf16[4,64,2048]{2,1,0:T(8,128)(2,1)S(1)} async-done(((bf16[4,64,2048]{2,1,0:T(8,128)(2,1)}), bf16[4,64,2048]{2,1,0:T(8,128)(2,1)S(1)}, u32[]{:S(2)}, u32[]{:S(2)}) %all-to-all-start.8) | async-done | bytes 1048608 | tf_op jit(solution)/shard_map/all_to_all | solution.py:853
  503.4 6.4 %shard_map.306 = (bf16[256,2048]{1,0:T(8,128)(2,1)}, f32[1,2048]{1,0:T(1,128)}) custom-call(bf16[256,512]{1,0:T(8,128)(2,1)} %shard_map.305.q_ref, bf16[256,512]{1,0:T(8,128)(2,1)} %get-tuple-element.92.k_ref, bf16[256,512]{1,0:T(8,128)(2,1)} %get-tuple-element.91.v_ref, bf16[256,2048]{1,0:T(8,128)(2,1)} %bitcast.168, f32[256,1]{1,0:T(8,128)} %copy.135.scale_ref, ...), custom_call_target="tpu_custom_call" | custom-call | tf_op jit(solution)/shard_map/pallas_call | solution.py:645
  529.2 4.9 collective-permute-done.43
  539.8 11.2 %all-to-all-start.10 = ((bf16[8,48,256]{2,1,0:T(8,128)(2,1)}), bf16[8,48,256]{2,1,0:T(8,128)(2,1)}, u32[]{:S(2)}, u32[]{:S(2)}) async-start(bf16[8,48,256]{2,1,0:T(8,128)(2,1)} %bitcast.149), calls=%async_computation.10 | async-start | bytes 393216 | tf_op jit(solution)/shard_map/all_to_all | solution.py:1250
  (418 shorter events, 244.9 us)
Async XLA Ops:
  8.0 104.5 %all-gather.3.cloned.1.call-start = ((), (), s32[]{:S(2)}) async-start(), calls=%async_computation.11 | async-start | bytes 9191424 | tf_op jit(solution)/shard_map/all_gather | solution.py:1000
  30.3 38.6 %all-to-all-start = ((bf16[8,128,384]{2,1,0:T(8,128)(2,1)}), bf16[8,128,384]{2,1,0:T(8,128)(2,1)}, u32[]{:S(2)}, u32[]{:S(2)}) async-start(bf16[8,128,384]{2,1,0:T(8,128)(2,1)} %get-tuple-element.60), calls=%async_computation | async-start | bytes 1572864 | tf_op jit(solution)/shard_map/all_to_all | solution.py:810
  108.1 29.2 %all-to-all-start.2 = ((bf16[4,64,2048]{2,1,0:T(8,128)(2,1)}), bf16[4,64,2048]{2,1,0:T(8,128)(2,1)S(1)}, u32[]{:S(2)}, u32[]{:S(2)}) async-start(bf16[4,64,2048]{2,1,0:T(8,128)(2,1)} %broadcast_in_dim.28), calls=%async_computation.2 | async-start | bytes 2097152 | tf_op jit(solution)/shard_map/all_to_all | solution.py:853
  139.8 25.7 %collective-permute-start.5 = (bf16[256,2048]{1,0:T(8,128)(2,1)}, bf16[256,2048]{1,0:T(8,128)(2,1)S(1)}, u32[]{:S(2)}, u32[]{:S(2)}) collective-permute-start(bf16[256,2048]{1,0:T(8,128)(2,1)} %bitcast.160), channel_id=1, source_target_pairs={{0,2},{1,3},{2,0},{3,1},{4,6},{5,7},{6,4},{7,5},{8,10},{9,11},{10,... | collective-permute-start | bytes 3145736 | tf_op jit(solution)/shard_map/ppermute | solution.py:51
  140.6 41.2 %collective-permute-start.12 = (bf16[256,2048]{1,0:T(8,128)(2,1)}, bf16[256,2048]{1,0:T(8,128)(2,1)}, u32[]{:S(2)}, u32[]{:S(2)}) collective-permute-start(bf16[256,2048]{1,0:T(8,128)(2,1)} %bitcast.161), channel_id=1, source_target_pairs={{0,1},{1,0},{2,3},{3,2},{4,5},{5,4},{6,7},{7,6},{8,9},{9,8},{10,11... | collective-permute-start | bytes 3145736 | tf_op jit(solution)/shard_map/ppermute | solution.py:51
  170.1 51.7 %collective-permute-start.9 = (bf16[256,2048]{1,0:T(8,128)(2,1)}, bf16[256,2048]{1,0:T(8,128)(2,1)}, u32[]{:S(2)}, u32[]{:S(2)}) collective-permute-start(bf16[256,2048]{1,0:T(8,128)(2,1)} %shard_map.268.refs_0_), channel_id=1, source_target_pairs={{0,1},{1,0},{2,3},{3,2},{4,5},{5,4},{6,7},{7,6},{8,9},{9,8},{10,11... | collective-permute-start | bytes 3145736 | tf_op jit(solution)/shard_map/ppermute | solution.py:51
  179.3 42.5 %collective-permute-start.11 = (bf16[128,2048]{1,0:T(8,128)(2,1)}, bf16[128,2048]{1,0:T(8,128)(2,1)}, u32[]{:S(2)}, u32[]{:S(2)}) collective-permute-start(bf16[128,2048]{1,0:T(8,128)(2,1)} %collective-permute-done.8.refs_2_), channel_id=1, source_target_pairs={{0,1},{1,0},{2,3},{3,2},{4,5},{5,4},{6,7},{7,6},{8,9},{9,8},{10,11... | collective-permute-start | bytes 1572872 | tf_op jit(solution)/shard_map/ppermute | solution.py:51
  181.8 40.0 %collective-permute-start.10 = (bf16[128,2048]{1,0:T(8,128)(2,1)}, bf16[128,2048]{1,0:T(8,128)(2,1)}, u32[]{:S(2)}, u32[]{:S(2)}) collective-permute-start(bf16[128,2048]{1,0:T(8,128)(2,1)} %collective-permute-done.6.refs_1_), channel_id=1, source_target_pairs={{0,1},{1,0},{2,3},{3,2},{4,5},{5,4},{6,7},{7,6},{8,9},{9,8},{10,11... | collective-permute-start | bytes 1572872 | tf_op jit(solution)/shard_map/ppermute | solution.py:51
  217.8 37.1 %all-to-all-start.3 = ((bf16[4,256,512]{2,1,0:T(8,128)(2,1)}), bf16[4,256,512]{2,1,0:T(8,128)(2,1)S(1)}, u32[]{:S(2)}, u32[]{:S(2)}) async-start(bf16[4,256,512]{2,1,0:T(8,128)(2,1)} %pad_maximum_fusion.3), calls=%async_computation.3 | async-start | bytes 2097152 | tf_op jit(solution)/shard_map/all_to_all | solution.py:965
  221.3 139.0 %all-gather.5.cloned.1.call-start = ((), (), s32[]{:S(2)}) async-start(), calls=%async_computation.12 | async-start | bytes 1310720 | tf_op jit(solution)/shard_map/all_gather | solution.py:976
  268.6 26.0 %collective-permute-start.21 = (bf16[128,2176]{1,0:T(8,128)(2,1)}, bf16[128,2176]{1,0:T(8,128)(2,1)}, u32[]{:S(2)}, u32[]{:S(2)}) collective-permute-start(bf16[128,2176]{1,0:T(8,128)(2,1)} %get-tuple-element.178.refs_0_), channel_id=1, source_target_pairs={{0,4},{4,0},{8,12},{12,8},{16,20},{20,16},{24,28},{28,24},{1,5},{5... | collective-permute-start | bytes 1671176 | tf_op jit(solution)/shard_map/ppermute | solution.py:51
  283.6 32.8 %collective-permute-start.20 = (bf16[256,2176]{1,0:T(8,128)(2,1)}, bf16[256,2176]{1,0:T(8,128)(2,1)S(1)}, u32[]{:S(2)}, u32[]{:S(2)}) collective-permute-start(bf16[256,2176]{1,0:T(8,128)(2,1)} %pad_maximum_fusion.refs_0_), channel_id=1, source_target_pairs={{0,4},{4,0},{8,12},{12,8},{16,20},{20,16},{24,28},{28,24},{1,5},{5... | collective-permute-start | bytes 3342344 | tf_op jit(solution)/shard_map/ppermute | solution.py:51
  296.0 36.1 %collective-permute-start.18 = (bf16[512,2048]{1,0:T(8,128)(2,1)}, bf16[512,2048]{1,0:T(8,128)(2,1)}, u32[]{:S(2)}, u32[]{:S(2)}) collective-permute-start(bf16[512,2048]{1,0:T(8,128)(2,1)} %get-tuple-element.79), channel_id=1, source_target_pairs={{0,1},{1,0},{2,3},{3,2},{4,5},{5,4},{6,7},{7,6},{8,9},{9,8},{10,11... | collective-permute-start | bytes 6291464 | tf_op jit(solution)/shard_map/ppermute | solution.py:51
  298.3 27.3 %collective-permute-start.22 = (bf16[256,2176]{1,0:T(8,128)(2,1)}, bf16[256,2176]{1,0:T(8,128)(2,1)}, u32[]{:S(2)}, u32[]{:S(2)}) collective-permute-start(bf16[256,2176]{1,0:T(8,128)(2,1)} %pad_maximum_fusion.1), channel_id=1, source_target_pairs={{0,2},{1,3},{2,0},{3,1},{4,6},{5,7},{6,4},{7,5},{8,10},{9,11},{10,... | collective-permute-start | bytes 3342344 | tf_op jit(solution)/shard_map/ppermute | solution.py:51
  301.5 36.0 %collective-permute-start.16 = (bf16[512,2048]{1,0:T(8,128)(2,1)}, bf16[512,2048]{1,0:T(8,128)(2,1)}, u32[]{:S(2)}, u32[]{:S(2)}) collective-permute-start(bf16[512,2048]{1,0:T(8,128)(2,1)} %get-tuple-element.77), channel_id=1, source_target_pairs={{0,1},{1,0},{2,3},{3,2},{4,5},{5,4},{6,7},{7,6},{8,9},{9,8},{10,11... | collective-permute-start | bytes 6291464 | tf_op jit(solution)/shard_map/ppermute | solution.py:51
  328.6 30.8 %all-to-all-start.4 = ((bf16[4,64,2176]{2,1,0:T(8,128)(2,1)}), bf16[4,64,2176]{2,1,0:T(8,128)(2,1)S(1)}, u32[]{:S(2)}, u32[]{:S(2)}) async-start(bf16[4,64,2176]{2,1,0:T(8,128)(2,1)} %bitcast.171), calls=%async_computation.4 | async-start | bytes 2228224 | tf_op jit(solution)/shard_map/all_to_all | solution.py:853
  336.3 28.8 %collective-permute-start.19 = (bf16[128,2048]{1,0:T(8,128)(2,1)}, bf16[128,2048]{1,0:T(8,128)(2,1)}, u32[]{:S(2)}, u32[]{:S(2)}) collective-permute-start(bf16[128,2048]{1,0:T(8,128)(2,1)} %get-tuple-element.179), channel_id=1, source_target_pairs={{0,2},{1,3},{2,0},{3,1},{4,6},{5,7},{6,4},{7,5},{8,10},{9,11},{10,... | collective-permute-start | bytes 1572872 | tf_op jit(solution)/shard_map/ppermute | solution.py:51
  341.8 26.6 %collective-permute-start.26 = (bf16[128,2048]{1,0:T(8,128)(2,1)}, bf16[128,2048]{1,0:T(8,128)(2,1)}, u32[]{:S(2)}, u32[]{:S(2)}) collective-permute-start(bf16[128,2048]{1,0:T(8,128)(2,1)} %get-tuple-element.181), channel_id=1, source_target_pairs={{0,4},{4,0},{8,12},{12,8},{16,20},{20,16},{24,28},{28,24},{1,5},{5... | collective-permute-start | bytes 1572872 | tf_op jit(solution)/shard_map/ppermute | solution.py:51
  367.6 30.9 %collective-permute-start.23 = (bf16[256,2048]{1,0:T(8,128)(2,1)}, bf16[256,2048]{1,0:T(8,128)(2,1)}, u32[]{:S(2)}, u32[]{:S(2)}) collective-permute-start(bf16[256,2048]{1,0:T(8,128)(2,1)} %pad_maximum_fusion.4), channel_id=1, source_target_pairs={{0,4},{4,0},{8,12},{12,8},{16,20},{20,16},{24,28},{28,24},{1,5},{5... | collective-permute-start | bytes 3145736 | tf_op jit(solution)/shard_map/ppermute | solution.py:51
  374.1 25.8 %collective-permute-start.27 = (bf16[256,2048]{1,0:T(8,128)(2,1)}, bf16[256,2048]{1,0:T(8,128)(2,1)}, u32[]{:S(2)}, u32[]{:S(2)}) collective-permute-start(bf16[256,2048]{1,0:T(8,128)(2,1)} %pad_maximum_fusion.6), channel_id=1, source_target_pairs={{0,2},{1,3},{2,0},{3,1},{4,6},{5,7},{6,4},{7,5},{8,10},{9,11},{10,... | collective-permute-start | bytes 3145736 | tf_op jit(solution)/shard_map/ppermute | solution.py:51
  446.5 29.4 %all-to-all-start.8 = ((bf16[4,64,2048]{2,1,0:T(8,128)(2,1)}), bf16[4,64,2048]{2,1,0:T(8,128)(2,1)S(1)}, u32[]{:S(2)}, u32[]{:S(2)}) async-start(bf16[4,64,2048]{2,1,0:T(8,128)(2,1)} %bitcast.166), calls=%async_computation.8 | async-start | bytes 2097152 | tf_op jit(solution)/shard_map/all_to_all | solution.py:853
  497.7 25.2 %collective-permute-start.44 = (bf16[256,512]{1,0:T(8,128)(2,1)}, bf16[256,512]{1,0:T(8,128)(2,1)}, u32[]{:S(2)}, u32[]{:S(2)}) collective-permute-start(bf16[256,512]{1,0:T(8,128)(2,1)} %shard_map.312), channel_id=1, source_target_pairs={{0,4},{4,0},{8,12},{12,8},{16,20},{20,16},{24,28},{28,24},{1,5},{5... | collective-permute-start | bytes 786440 | tf_op jit(solution)/shard_map/ppermute | solution.py:51
  529.2 36.1 %collective-permute-start.47 = (bf16[256,512]{1,0:T(8,128)(2,1)}, bf16[256,512]{1,0:T(8,128)(2,1)}, u32[]{:S(2)}, u32[]{:S(2)}) collective-permute-start(bf16[256,512]{1,0:T(8,128)(2,1)} %slice.199), channel_id=1, source_target_pairs={{0,16},{4,20},{8,24},{12,28},{16,0},{20,4},{24,8},{28,12},{1,17},{... | collective-permute-start | bytes 786440 | tf_op jit(solution)/shard_map/ppermute | solution.py:51
  537.2 32.3 %collective-permute-start.36 = (bf16[2,32,2048]{2,1,0:T(8,128)(2,1)}, bf16[2,32,2048]{2,1,0:T(8,128)(2,1)S(1)}, u32[]{:S(2)}, u32[]{:S(2)}) collective-permute-start(bf16[2,32,2048]{2,1,0:T(8,128)(2,1)} %fusion.29.refs_1_), channel_id=1, source_target_pairs={{0,2},{1,3},{2,0},{3,1},{4,6},{5,7},{6,4},{7,5},{8,10},{9,11},{10,... | collective-permute-start | bytes 786440 | tf_op jit(solution)/shard_map/ppermute | solution.py:51
  (104 other events, 950.8 us)
Sparse Core Ops, SparseCore 0:
  11.7 95.4 all-gather.2
Sparse Core Ops, SparseCore 1:
  301.6 26.9 all-gather.4

commit v4 on v3

--- a/solution.py
+++ b/solution.py
@@ -986,7 +986,10 @@
         return [swap(operand, "expert", place) for place in low_places]
 
     def halve_product(product):
-        return halve_rows(product, [("expert", bit) for bit in high_bits[::-1]], 0, f32)
+        for bit in high_bits[:0:-1]:
+            product = halve_rows(product, [("expert", bit)], 0)
+        kept_half, sent = jnp.split(product, 2, axis=0)
+        return kept_half, swap(sent, "expert", high_bits[0])
 
     grad_rows = lax.dynamic_slice_in_dim(out_grad, tensor_at * own_rows, own_rows, axis=1)
     route_rows = lax.dynamic_slice_in_dim(routes, tensor_at * own_rows, own_rows, axis=1)
@@ -1204,11 +1207,7 @@
     query_product = near_product(query_grad_low, query_arrived)
     key_arrived = after_all(key_arrived, query_product)
     key_product = near_product(key_grad_low, key_arrived)
-    grad_value, grad_query = (halve_product(item) for item in (value_product, query_product))
-    grad_key = halve_product(key_product)
-    output_product = t_mm(residual_gathered, after(attended_gathered, query_grad_low))
-    grad_output = halve_product(output_product.astype(bf16)).T
-
+    halves_made = [halve_product(item) for item in (value_product, query_product, key_product)]
     scale_in = rms_scale(tokens_here.astype(f32))
     norm_in_part, first_gain_part = project_back(
         after(query_grad_low, value_product),
@@ -1220,12 +1219,11 @@
         w_key,
         w_value,
     )
-    norm_in_grad = halve_rows(
-        norm_in_part.reshape(micro_count, rows_here, width),
-        tensor_steps[::-1],
-        1,
-        f32,
-    )
+    halves = jnp.split(norm_in_part.reshape(micro_count, rows_here, width), 2, axis=1)
+    norm_in_half = add(halves[0], swap(halves[1], *tensor_steps[-1])).astype(bf16)
+    norm_in_grad = halve_rows(norm_in_half, tensor_steps[:-1][::-1], 1, f32)
+    output_product = t_mm(residual_gathered, after(attended_gathered, query_grad_low))
+    halves_made.append(halve_product(output_product.astype(bf16)))
     own_scale = scale_in[:, :own_rows]
     weighted_in = norm_in_grad * norm1_gain
     tokens_grad = (
@@ -1273,6 +1271,10 @@
     own_heads = own_heads[0, : 2 * heads_here * head_block].reshape(2, heads_here, head_block)
 
 
+    grad_value, grad_query, grad_key, grad_output = (
+        add(own_half, after(other_half, layer_out)) for own_half, other_half in halves_made
+    )
+    grad_output = grad_output.T
     return (
         layer_out,
         tokens_grad,

time: 593 us -> 600 us (1.012)
  waiting for transfers between devices: 136 us -> 148 us
  starting transfers between devices: 90.2 us -> 81.8 us
    ppermute x50, waiting for transfers between devices: 55.6 us -> 73.8 us  [swap(): lax.ppermute(operand, axis_name, [(i, i ^ bit) for i in range(count)])]
    all_to_all x1, starting transfers between devices: 11.2 us -> 4.65 us  [reduce_small(): lax.all_to_all(rows, 'expert', split_axis=0, concat_axis=0, tiled=True)]
    unnamed x134 -> x132, local copies, waits for them, and re-layouts: 22.4 us -> 23.2 us
  transfers between devices with their start and end apart: 62 -> 62, of which waited for: 21 -> 24; matrix products, arithmetic and copies ran while one was open for 19% -> 18% of each run, Pallas kernels for 31% -> 30%
where the time goes in v4:
time: 600 us; the launch traced here: 591 us
  Pallas kernels  182 us (30%)
  waiting for transfers between devices  148 us (25%)
  starting transfers between devices  81.8 us (14%)
  other arithmetic  59.5 us (10%)
  local copies, waits for them, and re-layouts  57.9 us (10%)
  matrix products  22.7 us (4%)
  blocking collectives  20.4 us (3%)
  between operations  19.6 us (3%)
    ppermute x50, waiting for transfers between devices, swap(): lax.ppermute(operand, axis_name, [(i, i ^ bit) for i in range(count)])  73.8 us
    pallas_call x2, Pallas kernels, expert_call(): pl.pallas_call(functools.partial(expert_kernel, plan, copy_count, width),...  66.5 us
    pallas_call x3, Pallas kernels, expert_grads(): pl.pallas_call(product_kernel, grid=(owned,), out_shape=jax.ShapeDtypeStr...  45.4 us
    ppermute x50, starting transfers between devices, swap(): lax.ppermute(operand, axis_name, [(i, i ^ bit) for i in range(count)])  41.8 us
    all_to_all x3, waiting for transfers between devices, far_exchange(): lax.all_to_all(blocks, 'expert', split_axis=0, concat_axis=0, axis_index_...  35.6 us
    all_to_all x2, waiting for transfers between devices, pairs_to_heads(): lax.all_to_all(blocks, 'expert', split_axis=0, concat_axis=0, tiled=True)  32.8 us
    pallas_call x2, Pallas kernels, upstream_products(): pl.pallas_call(functools.partial(upstream_kernel, place, blocks, width),...  24.1 us
    unnamed x132, local copies, waits for them, and re-layouts  23.2 us
  transfers between devices with their start and end apart: 62, of which 24 were waited for; matrix products, arithmetic and copies ran while one was open for 18% of the time, Pallas kernels for 30%

profile of v4, /device:TPU:0, one launch (start us, length us, event | category | flops | bytes accessed | tf_op | source)
XLA Modules:
  0.0 591.5 jit_solution(5644224570323340334)
XLA Ops:
  14.1 5.8 shard_map.263
  30.3 5.7 all-to-all-start
  36.1 32.8 %all-to-all-done = bf16[8,128,384]{2,1,0:T(8,128)(2,1)} async-done(((bf16[8,128,384]{2,1,0:T(8,128)(2,1)}), bf16[8,128,384]{2,1,0:T(8,128)(2,1)}, u32[]{:S(2)}, u32[]{:S(2)}) %all-to-all-start) | async-done | bytes 786464 | tf_op jit(solution)/shard_map/all_to_all | solution.py:810
  74.6 20.4 %all_to_all.55 = bf16[8,128,128]{2,1,0:T(8,128)(2,1)S(1)} all-to-all(bf16[8,128,128]{2,1,0:T(8,128)(2,1)S(1)} %bitcast.195), channel_id=1, replica_groups=mesh['expert'=8,'tensor'=4] {'expert'}, dimensions={0} | all-to-all | bytes 524288 | tf_op jit(solution)/shard_map/all_to_all | solution.py:820
  99.0 7.6 %collective-permute-done.4 = bf16[2,32,2048]{2,1,0:T(8,128)(2,1)S(1)} collective-permute-done((bf16[2,32,2048]{2,1,0:T(8,128)(2,1)S(1)}, bf16[2,32,2048]{2,1,0:T(8,128)(2,1)S(1)}, u32[]{:S(2)}, u32[]{:S(2)}) %collective-permute-start.4) | collective-permute-done | bytes 262176 | tf_op jit(solution)/shard_map/ppermute | solution.py:51
  112.5 12.0 %shard_map.265 = (f32[1024,1024]{1,0:T(8,128)}, bf16[1024,128]{1,0:T(8,128)(2,1)}, bf16[2048,2048]{1,0:T(8,128)(2,1)}) custom-call(s32[32]{0:T(128)} %stack.164.table_ref, bf16[4,256,2048]{2,1,0:T(8,128)(2,1)} %down_ref.7, bf16[2048,2176]{1,0:T(8,128)(2,1)} %all-gather.3.cloned.1.call-done.gathered_ref, bf16[64,2048]{1,0:T(8,128)(2,1)} %copy-done.34), custom_call_target="tpu_custom_call" | custom-call | flops 4294967296 | bytes 16777216 | tf_op jit(solution)/shard_map/pallas_call | solution.py:149
  124.5 12.7 %all-to-all-done.2.refs_0_ = bf16[4,64,2048]{2,1,0:T(8,128)(2,1)S(1)} async-done(((bf16[4,64,2048]{2,1,0:T(8,128)(2,1)}), bf16[4,64,2048]{2,1,0:T(8,128)(2,1)S(1)}, u32[]{:S(2)}, u32[]{:S(2)}) %all-to-all-start.2) | async-done | bytes 1048608 | tf_op jit(solution)/shard_map/all_to_all | solution.py:853
  140.6 12.0 %shard_map.267 = (f32[1024,1024]{1,0:T(8,128)}, bf16[1024,128]{1,0:T(8,128)(2,1)}, bf16[2048,2048]{1,0:T(8,128)(2,1)}) custom-call(s32[32]{0:T(128)} %stack.164.table_ref, bf16[4,256,2048]{2,1,0:T(8,128)(2,1)} %down_ref.7, bf16[2048,2176]{1,0:T(8,128)(2,1)} %all-gather.3.cloned.1.call-done.gathered_ref, ...), custom_call_target="tpu_custom_call", output_to_operand_aliasing={{2}: (3, {})} | custom-call | flops 4294967296 | bytes 16777216 | tf_op jit(solution)/shard_map/pallas_call | solution.py:149
  152.6 10.1 %collective-permute-done.7.refs_0_ = bf16[256,2048]{1,0:T(8,128)(2,1)} collective-permute-done((bf16[256,2048]{1,0:T(8,128)(2,1)}, bf16[256,2048]{1,0:T(8,128)(2,1)}, u32[]{:S(2)}, u32[]{:S(2)}) %collective-permute-start.7) | collective-permute-done | bytes 1048608 | tf_op jit(solution)/shard_map/ppermute | solution.py:51
  170.1 9.2 %collective-permute-done.8.refs_2_ = bf16[128,2048]{1,0:T(8,128)(2,1)} collective-permute-done((bf16[128,2048]{1,0:T(8,128)(2,1)}, bf16[128,2048]{1,0:T(8,128)(2,1)}, u32[]{:S(2)}, u32[]{:S(2)}) %collective-permute-start.8) | collective-permute-done | bytes 524320 | tf_op jit(solution)/shard_map/ppermute | solution.py:51
  181.9 33.3 %shard_map.270 = (bf16[512,2176]{1,0:T(8,128)(2,1)}, bf16[512,2176]{1,0:T(8,128)(2,1)}, bf16[2048,2048]{1,0:T(8,128)(2,1)}, bf16[2048,1024]{1,0:T(8,128)(2,1)}, ...) custom-call(s32[1]{0:T(128)} %bitcast.13.base_ref, bf16[1024,128]{1,0:T(8,128)(2,1)} %get-tuple-element.65.mask_ref, ...), custom_call_target="tpu_custom_call" | custom-call | flops 17179869184 | bytes 25165824 | tf_op jit(solution)/shard_map/pallas_call | solution.py:331
  221.9 33.1 %shard_map.271 = (bf16[512,2176]{1,0:T(8,128)(2,1)}, bf16[512,2176]{1,0:T(8,128)(2,1)}, bf16[2048,2048]{1,0:T(8,128)(2,1)}, bf16[2048,1024]{1,0:T(8,128)(2,1)}, ...) custom-call(s32[1]{0:T(128)} %bitcast.13.base_ref, ...), custom_call_target="tpu_custom_call", output_to_operand_aliasing={{2}: (12, {}), {3}: (13, {}), {4}: (14, {}), {5}: (15, {})} | custom-call | flops 17179869184 | bytes 25165824 | tf_op jit(solution)/shard_map/pallas_call | solution.py:331
  270.6 9.7 %shard_map.275 = (bf16[512,2048]{1,0:T(8,128)(2,1)}, bf16[512,2048]{1,0:T(8,128)(2,1)}) custom-call(bf16[2048,1024]{1,0:T(8,128)(2,1)} %get-tuple-element.70.gated_ref.left_ref, bf16[4,256,2048]{2,1,0:T(8,128)(2,1)} %down_ref.7, bf16[128,2176]{1,0:T(8,128)(2,1)} %get-tuple-element.164.refs_0_, bf16[512,2176]{1,0:T(8,128)(2,1)} %copy-done.16), custom_call_target="tpu_custom_call" | custom-call | flops 4294967296 | bytes 8388608 | tf_op jit(solution)/shard_map/pallas_call | solution.py:377
  284.9 9.8 %shard_map.277 = (bf16[512,2048]{1,0:T(8,128)(2,1)}, bf16[512,2048]{1,0:T(8,128)(2,1)}) custom-call(bf16[2048,1024]{1,0:T(8,128)(2,1)} %get-tuple-element.70.gated_ref.left_ref, bf16[4,256,2048]{2,1,0:T(8,128)(2,1)} %down_ref.7, bf16[256,2176]{1,0:T(8,128)(2,1)} %pad_maximum_fusion.refs_0_), custom_call_target="tpu_custom_call" | custom-call | flops 4294967296 | bytes 8388608 | tf_op jit(solution)/shard_map/pallas_call | solution.py:377
  301.8 14.6 %shard_map.278.refs_2_ = f32[4,256,2048]{2,1,0:T(8,128)} custom-call(bf16[2048,1024]{1,0:T(8,128)(2,1)} %get-tuple-element.70.gated_ref.left_ref, bf16[2048,2048]{1,0:T(8,128)(2,1)} %get-tuple-element.80.right_ref, bf16[256,2176]{1,0:T(8,128)(2,1)} %pad_maximum_fusion.refs_0_), custom_call_target="tpu_custom_call" | custom-call | flops 8589934592 | bytes 25165824 | tf_op jit(solution)/shard_map/pallas_call | solution.py:414
  317.4 8.2 %collective-permute-done.22.refs_0_ = bf16[256,2176]{1,0:T(8,128)(2,1)} collective-permute-done((bf16[256,2176]{1,0:T(8,128)(2,1)}, bf16[256,2176]{1,0:T(8,128)(2,1)}, u32[]{:S(2)}, u32[]{:S(2)}) %collective-permute-start.22) | collective-permute-done | bytes 1114144 | tf_op jit(solution)/shard_map/ppermute | solution.py:51
  342.5 16.9 %all-to-all-done.4.refs_0_ = bf16[4,64,2176]{2,1,0:T(8,128)(2,1)S(1)} async-done(((bf16[4,64,2176]{2,1,0:T(8,128)(2,1)}), bf16[4,64,2176]{2,1,0:T(8,128)(2,1)S(1)}, u32[]{:S(2)}, u32[]{:S(2)}) %all-to-all-start.4) | async-done | bytes 1114144 | tf_op jit(solution)/shard_map/all_to_all | solution.py:853
  383.1 15.4 %shard_map.286.refs_1_ = f32[4,2048,256]{2,1,0:T(8,128)} custom-call(bf16[2048,2048]{1,0:T(8,128)(2,1)} %get-tuple-element.82.left_ref, bf16[2048,1024]{1,0:T(8,128)(2,1)} %get-tuple-element.83.right_ref, bf16[8,128,128]{2,1,0:T(8,128)(2,1)} %bitcast.193), custom_call_target="tpu_custom_call" | custom-call | flops 8589934592 | bytes 25165824 | tf_op jit(solution)/shard_map/pallas_call | solution.py:414
  428.8 15.4 %shard_map.293.refs_1_ = f32[4,2048,256]{2,1,0:T(8,128)} custom-call(bf16[2048,2048]{1,0:T(8,128)(2,1)} %get-tuple-element.82.left_ref, bf16[2048,1024]{1,0:T(8,128)(2,1)} %get-tuple-element.84.right_ref, bf16[1,1024,384]{2,1,0:T(8,128)(2,1)} %shard_map.292.refs_0_), custom_call_target="tpu_custom_call" | custom-call | flops 8589934592 | bytes 25165824 | tf_op jit(solution)/shard_map/pallas_call | solution.py:414
  469.9 6.0 %all-to-all-done.8.refs_1_.refs_0_ = bf16[4,64,2048]{2,1,0:T(8,128)(2,1)S(1)} async-done(((bf16[4,64,2048]{2,1,0:T(8,128)(2,1)}), bf16[4,64,2048]{2,1,0:T(8,128)(2,1)S(1)}, u32[]{:S(2)}, u32[]{:S(2)}) %all-to-all-start.8) | async-done | bytes 1048608 | tf_op jit(solution)/shard_map/all_to_all | solution.py:853
  498.0 6.4 %shard_map.306 = (bf16[256,2048]{1,0:T(8,128)(2,1)}, f32[1,2048]{1,0:T(1,128)}) custom-call(bf16[256,512]{1,0:T(8,128)(2,1)} %shard_map.305.q_ref, bf16[256,512]{1,0:T(8,128)(2,1)} %get-tuple-element.92.k_ref, bf16[256,512]{1,0:T(8,128)(2,1)} %get-tuple-element.91.v_ref, bf16[256,2048]{1,0:T(8,128)(2,1)} %bitcast.167, f32[256,1]{1,0:T(8,128)} %copy.125.scale_ref, ...), custom_call_target="tpu_custom_call" | custom-call | tf_op jit(solution)/shard_map/pallas_call | solution.py:645
  543.8 4.7 all-to-all-start.10
  551.7 5.9 collective-permute-done.48.refs_0_
  559.5 9.2 %collective-permute-done.47.refs_0_ = bf16[256,512]{1,0:T(8,128)(2,1)} collective-permute-done((bf16[256,512]{1,0:T(8,128)(2,1)}, bf16[256,512]{1,0:T(8,128)(2,1)}, u32[]{:S(2)}, u32[]{:S(2)}) %collective-permute-start.47) | collective-permute-done | bytes 262176 | tf_op jit(solution)/shard_map/ppermute | solution.py:51
  (420 shorter events, 254.9 us)
Async XLA Ops:
  8.0 104.5 %all-gather.3.cloned.1.call-start = ((), (), s32[]{:S(2)}) async-start(), calls=%async_computation.11 | async-start | bytes 9191424 | tf_op jit(solution)/shard_map/all_gather | solution.py:1003
  30.3 38.6 %all-to-all-start = ((bf16[8,128,384]{2,1,0:T(8,128)(2,1)}), bf16[8,128,384]{2,1,0:T(8,128)(2,1)}, u32[]{:S(2)}, u32[]{:S(2)}) async-start(bf16[8,128,384]{2,1,0:T(8,128)(2,1)} %get-tuple-element.60), calls=%async_computation | async-start | bytes 1572864 | tf_op jit(solution)/shard_map/all_to_all | solution.py:810
  108.1 29.2 %all-to-all-start.2 = ((bf16[4,64,2048]{2,1,0:T(8,128)(2,1)}), bf16[4,64,2048]{2,1,0:T(8,128)(2,1)S(1)}, u32[]{:S(2)}, u32[]{:S(2)}) async-start(bf16[4,64,2048]{2,1,0:T(8,128)(2,1)} %broadcast_in_dim.28), calls=%async_computation.2 | async-start | bytes 2097152 | tf_op jit(solution)/shard_map/all_to_all | solution.py:853
  140.6 41.3 %collective-permute-start.12 = (bf16[256,2048]{1,0:T(8,128)(2,1)}, bf16[256,2048]{1,0:T(8,128)(2,1)}, u32[]{:S(2)}, u32[]{:S(2)}) collective-permute-start(bf16[256,2048]{1,0:T(8,128)(2,1)} %bitcast.160), channel_id=1, source_target_pairs={{0,1},{1,0},{2,3},{3,2},{4,5},{5,4},{6,7},{7,6},{8,9},{9,8},{10,11... | collective-permute-start | bytes 3145736 | tf_op jit(solution)/shard_map/ppermute | solution.py:51
  170.1 51.8 %collective-permute-start.9 = (bf16[256,2048]{1,0:T(8,128)(2,1)}, bf16[256,2048]{1,0:T(8,128)(2,1)}, u32[]{:S(2)}, u32[]{:S(2)}) collective-permute-start(bf16[256,2048]{1,0:T(8,128)(2,1)} %shard_map.268.refs_0_), channel_id=1, source_target_pairs={{0,1},{1,0},{2,3},{3,2},{4,5},{5,4},{6,7},{7,6},{8,9},{9,8},{10,11... | collective-permute-start | bytes 3145736 | tf_op jit(solution)/shard_map/ppermute | solution.py:51
  179.3 42.5 %collective-permute-start.11 = (bf16[128,2048]{1,0:T(8,128)(2,1)}, bf16[128,2048]{1,0:T(8,128)(2,1)}, u32[]{:S(2)}, u32[]{:S(2)}) collective-permute-start(bf16[128,2048]{1,0:T(8,128)(2,1)} %collective-permute-done.8.refs_2_), channel_id=1, source_target_pairs={{0,1},{1,0},{2,3},{3,2},{4,5},{5,4},{6,7},{7,6},{8,9},{9,8},{10,11... | collective-permute-start | bytes 1572872 | tf_op jit(solution)/shard_map/ppermute | solution.py:51
  181.9 40.0 %collective-permute-start.10 = (bf16[128,2048]{1,0:T(8,128)(2,1)}, bf16[128,2048]{1,0:T(8,128)(2,1)}, u32[]{:S(2)}, u32[]{:S(2)}) collective-permute-start(bf16[128,2048]{1,0:T(8,128)(2,1)} %collective-permute-done.6.refs_1_), channel_id=1, source_target_pairs={{0,1},{1,0},{2,3},{3,2},{4,5},{5,4},{6,7},{7,6},{8,9},{9,8},{10,11... | collective-permute-start | bytes 1572872 | tf_op jit(solution)/shard_map/ppermute | solution.py:51
  217.8 37.2 %all-to-all-start.3 = ((bf16[4,256,512]{2,1,0:T(8,128)(2,1)}), bf16[4,256,512]{2,1,0:T(8,128)(2,1)S(1)}, u32[]{:S(2)}, u32[]{:S(2)}) async-start(bf16[4,256,512]{2,1,0:T(8,128)(2,1)} %pad_maximum_fusion.3), calls=%async_computation.3 | async-start | bytes 2097152 | tf_op jit(solution)/shard_map/all_to_all | solution.py:965
  221.4 139.0 %all-gather.5.cloned.1.call-start = ((), (), s32[]{:S(2)}) async-start(), calls=%async_computation.12 | async-start | bytes 1310720 | tf_op jit(solution)/shard_map/all_gather | solution.py:976
  283.6 32.8 %collective-permute-start.20 = (bf16[256,2176]{1,0:T(8,128)(2,1)}, bf16[256,2176]{1,0:T(8,128)(2,1)S(1)}, u32[]{:S(2)}, u32[]{:S(2)}) collective-permute-start(bf16[256,2176]{1,0:T(8,128)(2,1)} %pad_maximum_fusion.refs_0_), channel_id=1, source_target_pairs={{0,4},{4,0},{8,12},{12,8},{16,20},{20,16},{24,28},{28,24},{1,5},{5... | collective-permute-start | bytes 3342344 | tf_op jit(solution)/shard_map/ppermute | solution.py:51
  296.1 36.1 %collective-permute-start.18 = (bf16[512,2048]{1,0:T(8,128)(2,1)}, bf16[512,2048]{1,0:T(8,128)(2,1)}, u32[]{:S(2)}, u32[]{:S(2)}) collective-permute-start(bf16[512,2048]{1,0:T(8,128)(2,1)} %get-tuple-element.79), channel_id=1, source_target_pairs={{0,1},{1,0},{2,3},{3,2},{4,5},{5,4},{6,7},{7,6},{8,9},{9,8},{10,11... | collective-permute-start | bytes 6291464 | tf_op jit(solution)/shard_map/ppermute | solution.py:51
  298.3 27.3 %collective-permute-start.22 = (bf16[256,2176]{1,0:T(8,128)(2,1)}, bf16[256,2176]{1,0:T(8,128)(2,1)}, u32[]{:S(2)}, u32[]{:S(2)}) collective-permute-start(bf16[256,2176]{1,0:T(8,128)(2,1)} %pad_maximum_fusion.1), channel_id=1, source_target_pairs={{0,2},{1,3},{2,0},{3,1},{4,6},{5,7},{6,4},{7,5},{8,10},{9,11},{10,... | collective-permute-start | bytes 3342344 | tf_op jit(solution)/shard_map/ppermute | solution.py:51
  301.5 36.0 %collective-permute-start.16 = (bf16[512,2048]{1,0:T(8,128)(2,1)}, bf16[512,2048]{1,0:T(8,128)(2,1)}, u32[]{:S(2)}, u32[]{:S(2)}) collective-permute-start(bf16[512,2048]{1,0:T(8,128)(2,1)} %get-tuple-element.77), channel_id=1, source_target_pairs={{0,1},{1,0},{2,3},{3,2},{4,5},{5,4},{6,7},{7,6},{8,9},{9,8},{10,11... | collective-permute-start | bytes 6291464 | tf_op jit(solution)/shard_map/ppermute | solution.py:51
  328.6 30.8 %all-to-all-start.4 = ((bf16[4,64,2176]{2,1,0:T(8,128)(2,1)}), bf16[4,64,2176]{2,1,0:T(8,128)(2,1)S(1)}, u32[]{:S(2)}, u32[]{:S(2)}) async-start(bf16[4,64,2176]{2,1,0:T(8,128)(2,1)} %bitcast.175), calls=%async_computation.4 | async-start | bytes 2228224 | tf_op jit(solution)/shard_map/all_to_all | solution.py:853
  336.4 28.8 %collective-permute-start.19 = (bf16[128,2048]{1,0:T(8,128)(2,1)}, bf16[128,2048]{1,0:T(8,128)(2,1)}, u32[]{:S(2)}, u32[]{:S(2)}) collective-permute-start(bf16[128,2048]{1,0:T(8,128)(2,1)} %get-tuple-element.165), channel_id=1, source_target_pairs={{0,2},{1,3},{2,0},{3,1},{4,6},{5,7},{6,4},{7,5},{8,10},{9,11},{10,... | collective-permute-start | bytes 1572872 | tf_op jit(solution)/shard_map/ppermute | solution.py:51
  367.6 30.8 %collective-permute-start.23 = (bf16[256,2048]{1,0:T(8,128)(2,1)}, bf16[256,2048]{1,0:T(8,128)(2,1)}, u32[]{:S(2)}, u32[]{:S(2)}) collective-permute-start(bf16[256,2048]{1,0:T(8,128)(2,1)} %pad_maximum_fusion.4), channel_id=1, source_target_pairs={{0,4},{4,0},{8,12},{12,8},{16,20},{20,16},{24,28},{28,24},{1,5},{5... | collective-permute-start | bytes 3145736 | tf_op jit(solution)/shard_map/ppermute | solution.py:51
  446.5 29.4 %all-to-all-start.8 = ((bf16[4,64,2048]{2,1,0:T(8,128)(2,1)}), bf16[4,64,2048]{2,1,0:T(8,128)(2,1)S(1)}, u32[]{:S(2)}, u32[]{:S(2)}) async-start(bf16[4,64,2048]{2,1,0:T(8,128)(2,1)} %bitcast.165), calls=%async_computation.8 | async-start | bytes 2097152 | tf_op jit(solution)/shard_map/all_to_all | solution.py:853
  456.6 29.8 %collective-permute-start.32 = (bf16[256,512]{1,0:T(8,128)(2,1)}, bf16[256,512]{1,0:T(8,128)(2,1)}, u32[]{:S(2)}, u32[]{:S(2)}) collective-permute-start(bf16[256,512]{1,0:T(8,128)(2,1)} %get-tuple-element.91.v_ref), channel_id=1, source_target_pairs={{0,8},{4,12},{8,0},{12,4},{16,24},{20,28},{24,16},{28,20},{1,9},{5... | collective-permute-start | bytes 786440 | tf_op jit(solution)/shard_map/ppermute | solution.py:51
  458.6 27.8 %collective-permute-start.33 = (bf16[256,512]{1,0:T(8,128)(2,1)}, bf16[256,512]{1,0:T(8,128)(2,1)}, u32[]{:S(2)}, u32[]{:S(2)}) collective-permute-start(bf16[256,512]{1,0:T(8,128)(2,1)} %get-tuple-element.91.v_ref), channel_id=1, source_target_pairs={{0,12},{4,8},{8,4},{12,0},{16,28},{20,24},{24,20},{28,16},{1,13},{... | collective-permute-start | bytes 786440 | tf_op jit(solution)/shard_map/ppermute | solution.py:51
  517.3 32.5 %collective-permute-start.49 = (bf16[256,512]{1,0:T(8,128)(2,1)}, bf16[256,512]{1,0:T(8,128)(2,1)}, u32[]{:S(2)}, u32[]{:S(2)}) collective-permute-start(bf16[256,512]{1,0:T(8,128)(2,1)} %split.59), channel_id=1, source_target_pairs={{0,16},{4,20},{8,24},{12,28},{16,0},{20,4},{24,8},{28,12},{1,17},{... | collective-permute-start | bytes 786440 | tf_op jit(solution)/shard_map/ppermute | solution.py:51
  518.9 38.8 %collective-permute-start.48 = (bf16[256,512]{1,0:T(8,128)(2,1)}, bf16[256,512]{1,0:T(8,128)(2,1)}, u32[]{:S(2)}, u32[]{:S(2)}) collective-permute-start(bf16[256,512]{1,0:T(8,128)(2,1)} %split.57), channel_id=1, source_target_pairs={{0,16},{4,20},{8,24},{12,28},{16,0},{20,4},{24,8},{28,12},{1,17},{... | collective-permute-start | bytes 786440 | tf_op jit(solution)/shard_map/ppermute | solution.py:51
  521.8 48.9 %collective-permute-start.43 = (bf16[256,512]{1,0:T(8,128)(2,1)}, bf16[256,512]{1,0:T(8,128)(2,1)}, u32[]{:S(2)}, u32[]{:S(2)}) collective-permute-start(bf16[256,512]{1,0:T(8,128)(2,1)} %split.53), channel_id=1, source_target_pairs={{0,16},{4,20},{8,24},{12,28},{16,0},{20,4},{24,8},{28,12},{1,17},{... | collective-permute-start | bytes 786440 | tf_op jit(solution)/shard_map/ppermute | solution.py:51
  538.4 30.3 %collective-permute-start.47 = (bf16[256,512]{1,0:T(8,128)(2,1)}, bf16[256,512]{1,0:T(8,128)(2,1)}, u32[]{:S(2)}, u32[]{:S(2)}) collective-permute-start(bf16[256,512]{1,0:T(8,128)(2,1)} %split.55), channel_id=1, source_target_pairs={{0,16},{4,20},{8,24},{12,28},{16,0},{20,4},{24,8},{28,12},{1,17},{... | collective-permute-start | bytes 786440 | tf_op jit(solution)/shard_map/ppermute | solution.py:51
  540.1 36.7 %collective-permute-start.36 = (bf16[2,32,2048]{2,1,0:T(8,128)(2,1)S(1)}, bf16[2,32,2048]{2,1,0:T(8,128)(2,1)}, u32[]{:S(2)}, u32[]{:S(2)}) collective-permute-start(bf16[2,32,2048]{2,1,0:T(8,128)(2,1)S(1)} %copy-done.23), channel_id=1, source_target_pairs={{0,2},{1,3},{2,0},{3,1},{4,6},{5,7},{6,4},{7,5},{8,10},{9,11},{10,... | collective-permute-start | bytes 786440 | tf_op jit(solution)/shard_map/ppermute | solution.py:51
  (103 other events, 937.3 us)
Sparse Core Ops, SparseCore 0:
  11.7 95.4 all-gather.2
Sparse Core Ops, SparseCore 1:
  301.6 27.0 all-gather.4
